TPU v7x, 256 devices: a whole 4x4x8 slice. The times are simulated.
256 devices in a mesh: section: 2 (over core), dp: 4 (over y), latent: 32 (over z, x).
Axes of the slice: x: 4, y: 4, z: 8, core: 2. Of those that a mesh axis runs over, the one named last changes fastest.
Arguments:
- tokens: bfloat16 [512, 5120], P(None, 'dp'), may hold values from -8 to 8
- cotangent: bfloat16 [512, 5120], P(None, 'dp'), may hold values from -6 to 6
- enc_weight: bfloat16 [2, 5120, 32768], P('section', 'dp', 'latent'), may hold values from -0.078125 to 0.078125
- enc_bias: float32 [2, 32768], P('section', 'latent'), may hold values from -3 to 3
- dec_weight: bfloat16 [2, 32768, 5120], P('section', 'latent', 'dp'), may hold values from -0.078125 to 0.078125
- dec_bias: float32 [2, 5120], P('section', 'dp'), may hold values from -3 to 3
- ln_gain: float32 [2, 5120], P('section', 'dp'), may hold values from 0.1 to 1.9
- ln_bias: float32 [2, 5120], P('section', 'dp'), may hold values from -3 to 3
- in_weight: bfloat16 [2, 5120, 12288], P('section', 'dp', 'latent'), may hold values from -0.078125 to 0.078125
- in_bias: float32 [2, 12288], P('section', 'latent'), may hold values from -3 to 3
- out_weight: bfloat16 [2, 12288, 5120], P('section', 'latent', 'dp'), may hold values from -0.0546875 to 0.0546875
- out_bias: float32 [2, 5120], P('section', 'dp'), may hold values from -3 to 3
Outputs:
- latent_effect: bfloat16 [2, 512, 32768], P('section', 'dp', 'latent')
- error_effect: float32 [2, 512], P('section', 'dp')
All inputs are finite; a program needn't handle non-finite values.
Results may differ from a plain program's by a relative error of at most 0.02.
Values may be sent and summed in bfloat16 or wider, within the bound.
No kernel may reach another device: no remote copies, remote signals or barrier semaphores. Data moves between devices by JAX's collectives and lax.ppermute only.
A program may use at most 128 MiB of HBM per device.

v0:
```python
import jax
import jax.numpy as jnp
from jax import lax
from jax.sharding import PartitionSpec as P

D = 5120


EPSILON = 1e-05
SQRT_HALF = 0.7071067811865476
INV_SQRT_TAU = 0.3989422804014327
CONTRACT_LAST = (((1,), (1,)), ((), ()))


def from_behind(x, axis, by):
    count = lax.axis_size(axis)
    pairs = [(i, i + by) for i in range(count) if 0 <= i + by < count]
    return lax.ppermute(x, axis, pairs)


def gelu_slope(values):
    cumulative = 0.5 * (1.0 + lax.erf(values * SQRT_HALF))
    return cumulative + values * jnp.exp(-0.5 * values * values) * INV_SQRT_TAU


def on_device(
    tokens,
    cotangent,
    enc_weight,
    enc_bias,
    dec_weight,
    dec_bias,
    ln_gain,
    ln_bias,
    in_weight,
    in_bias,
    out_weight,
    out_bias,
):
    dp_count = lax.axis_size("dp")
    latent_count = lax.axis_size("latent")
    micro_count = 2
    all_rows = tokens.shape[0]
    width_part = tokens.shape[1]
    batch_rows = all_rows // micro_count
    block_rows = batch_rows // dp_count
    share_rows = batch_rows // latent_count
    first_section = lax.axis_index("section") == 0
    dp_place = lax.axis_index("dp")
    latent_place = lax.axis_index("latent")
    enc_w = enc_weight[0]
    enc_b = enc_bias[0]
    dec_w = dec_weight[0]
    dec_b = dec_bias[0]
    norm_gain = ln_gain[0]
    norm_shift = ln_bias[0]
    in_w = in_weight[0]
    in_b = in_bias[0]
    out_w = out_weight[0]
    out_b = out_bias[0]

    def pick_block(values, block_index):
        columns = values.shape[-1]
        return values.reshape(dp_count, micro_count, block_rows, columns)[:, block_index].reshape(
            batch_rows, columns
        )

    def own_rows(values):
        return lax.dynamic_slice_in_dim(values, latent_place * share_rows, share_rows, 0)

    def select_section(early_state, late_state):
        return jnp.where(first_section, early_state, late_state)

    zeros_in = jnp.zeros((batch_rows, width_part), jnp.bfloat16)
    arrived = zeros_in
    saved_list = []
    for step_index in range(micro_count + 1):
        own_input = pick_block(tokens, step_index) if step_index < micro_count else zeros_in
        section_input = jnp.where(first_section, own_input, arrived)
        resid_f = section_input.astype(jnp.float32)
        pre_part = jnp.dot(section_input, enc_w, preferred_element_type=jnp.float32)
        pre_sum, row_total, row_square = lax.psum(
            (pre_part, jnp.sum(resid_f, axis=1), jnp.sum(resid_f * resid_f, axis=1)), "dp"
        )
        mean_row = row_total / D
        forward_inv_std = lax.rsqrt(row_square / D - mean_row * mean_row + EPSILON)
        forward_normed = (resid_f - mean_row[:, None]) * forward_inv_std[:, None]
        ln_out = (forward_normed * norm_gain + norm_shift).astype(jnp.bfloat16)
        forward_hidden = (
            lax.psum(jnp.dot(ln_out, in_w, preferred_element_type=jnp.float32), "dp") + in_b
        )
        forward_latent_codes = jnp.maximum(pre_sum + enc_b, 0.0).astype(jnp.bfloat16)
        act_out = jax.nn.gelu(forward_hidden, approximate=False).astype(jnp.bfloat16)
        mlp_share = lax.psum_scatter(
            jnp.dot(act_out, out_w, preferred_element_type=jnp.float32),
            "latent",
            scatter_dimension=0,
            tiled=True,
        )
        resid_share = own_rows(resid_f)
        new_share = (resid_share + mlp_share + out_b).astype(jnp.bfloat16)
        recon_share = (
            lax.psum_scatter(
                jnp.dot(forward_latent_codes, dec_w, preferred_element_type=jnp.float32).astype(
                    jnp.bfloat16
                ),
                "latent",
                scatter_dimension=0,
                tiled=True,
            ).astype(jnp.float32)
            + dec_b
        )
        forward_error_base = resid_share - recon_share
        whole_rows = lax.all_gather(new_share, "latent", axis=0, tiled=True)
        forward_arrived = from_behind(whole_rows, "section", 1)
        arrived = forward_arrived
        saved_state = (
            forward_normed,
            forward_inv_std,
            forward_latent_codes,
            forward_hidden,
            forward_error_base,
        )
        saved_list.append(saved_state)
    returned = zeros_in
    effects = []
    errors = []
    for step_index in range(micro_count + 1):
        early_state = saved_list[max(step_index - 1, 0)]
        late_state = saved_list[min(step_index + 1, micro_count)]
        saved_state = jax.tree.map(select_section, early_state, late_state)
        last_grad = pick_block(cotangent, step_index) if step_index < micro_count else zeros_in
        grad_out = jnp.where(first_section, returned, last_grad)
        normed, inv_std, latent_codes, hidden, error_base = saved_state
        grad_act = lax.psum(
            lax.dot_general(grad_out, out_w, CONTRACT_LAST, preferred_element_type=jnp.float32),
            "dp",
        )
        grad_hidden = (grad_act * gelu_slope(hidden)).astype(jnp.bfloat16)
        grad_ln = lax.psum_scatter(
            lax.dot_general(grad_hidden, in_w, CONTRACT_LAST, preferred_element_type=jnp.float32),
            "latent",
            scatter_dimension=0,
            tiled=True,
        )
        normed_share = own_rows(normed)
        grad_norm = grad_ln * norm_gain
        norm_total, norm_cross = lax.psum(
            (jnp.sum(grad_norm, axis=1), jnp.sum(grad_norm * normed_share, axis=1)), "dp"
        )
        grad_resid = (
            grad_norm - (norm_total / D)[:, None] - normed_share * (norm_cross / D)[:, None]
        ) * own_rows(inv_std[:, None])
        grad_share = (own_rows(grad_out).astype(jnp.float32) + grad_resid).astype(jnp.bfloat16)
        grad_full = lax.all_gather(grad_share, "latent", axis=0, tiled=True)
        backward_returned = from_behind(grad_full, "section", -1)
        grad_part = lax.dot_general(
            grad_full, dec_w, CONTRACT_LAST, preferred_element_type=jnp.float32
        )
        error_piece = jnp.sum(error_base * grad_share.astype(jnp.float32), axis=1)
        error_terms = lax.all_gather(error_piece, "latent", axis=0, tiled=True)
        grad_mine = lax.psum_scatter(grad_part, "dp", scatter_dimension=0, tiled=True)
        error_mine = lax.psum_scatter(error_terms, "dp", scatter_dimension=0, tiled=True)
        codes_mine = lax.dynamic_slice_in_dim(
            latent_codes, dp_place * block_rows, block_rows, 0
        ).astype(jnp.float32)
        effect = (codes_mine * grad_mine).astype(jnp.bfloat16)
        returned, effect, error_mine = (backward_returned, effect, error_mine)
        effects.append(effect)
        errors.append(error_mine)
    effect_rows = [
        jnp.where(first_section, effects[batch + 1], effects[batch]) for batch in range(micro_count)
    ]
    error_rows = [
        jnp.where(first_section, errors[batch + 1], errors[batch]) for batch in range(micro_count)
    ]
    return (jnp.concatenate(effect_rows, axis=0)[None], jnp.concatenate(error_rows, axis=0)[None])


def solution(mesh):
    in_specs = (
        P(None, "dp"),
        P(None, "dp"),
        P("section", "dp", "latent"),
        P("section", "latent"),
        P("section", "latent", "dp"),
        P("section", "dp"),
        P("section", "dp"),
        P("section", "dp"),
        P("section", "dp", "latent"),
        P("section", "latent"),
        P("section", "latent", "dp"),
        P("section", "dp"),
    )
    out_specs = (P("section", "dp", "latent"), P("section", "dp"))
    return jax.shard_map(
        on_device, mesh=mesh, in_specs=in_specs, out_specs=out_specs, check_vma=False
    )
```

profile of v0, /device:TPU:8, one launch (start us, length us, event | category | flops | bytes accessed | tf_op | source)
XLA Modules:
  0.0 2301.9 jit_solution(13273923838467559590)
XLA Ops:
  8.8 1.4 convert_reduce_fusion
  10.4 9.9 all-reduce.15
  23.0 47.8 %all-reduce.24.cloned.1.call-done = f32[256,384]{1,0:T(8,128)} async-done(((f32[256,384]{1,0:T(8,128)}), f32[256,384]{1,0:T(8,128)}) %all-reduce.24.cloned.1.call-update) | async-done | bytes 393232 | tf_op jit(solution)/shard_map/psum | solution.py:90
  70.8 3.7 fusion.40
  74.6 2.0 slice.17
  77.8 215.3 %reduce-scatter.12.cloned.1.call-done = f32[8,1280]{1,0:T(8,128)} async-done(((f32[256,1280]{1,0:T(8,128)}), f32[8,1280]{1,0:T(8,128)}) %reduce-scatter.12.cloned.1.call-update) | async-done | bytes 40976 | tf_op jit(solution)/shard_map/reduce_scatter | solution.py:94
  293.9 48.2 %all_gather.24 = bf16[256,1280]{1,0:T(8,128)(2,1)S(1)} all-gather(bf16[8,1280]{1,0:T(8,128)(2,1)S(1)} %add_convert_fusion.8), channel_id=1, replica_groups=mesh['section'=2,'dp'=4,'latent'=32] {'latent'}, dimensions={0}, use_global_device_ids=true | all-gather | bytes 675840 | tf_op jit(solution)/shard_map/all_gather | solution.py:114
  342.1 1.3 collective-permute-start
  348.4 8.6 all-reduce.14
  357.0 2.7 fusion.50
  359.8 47.2 %all-reduce.30.cloned.1.call-done = (f32[256,384]{1,0:T(8,128)}, f32[256,384]{1,0:T(8,128)}) async-done(((f32[256,384]{1,0:T(8,128)}, f32[256,384]{1,0:T(8,128)}), (f32[256,384]{1,0:T(8,128)}, f32[256,384]{1,0:T(8,128)})) %all-reduce.30.cloned.1.call-update) | async-done | bytes 786448 | tf_op jit(solution)/shard_map/psum | solution.py:135
  407.0 3.7 fusion.38
  410.7 3.3 fusion.48
  414.1 214.9 %reduce-scatter.14.cloned.1.call-done = f32[8,1280]{1,0:T(8,128)} async-done(((f32[256,1280]{1,0:T(8,128)}), f32[8,1280]{1,0:T(8,128)}) %reduce-scatter.14.cloned.1.call-update) | async-done | bytes 40976 | tf_op jit(solution)/shard_map/reduce_scatter | solution.py:94
  629.8 52.8 %all_gather.25 = bf16[256,1280]{1,0:T(8,128)(2,1)} all-gather(bf16[8,1280]{1,0:T(8,128)(2,1)S(1)} %add_convert_fusion.7), channel_id=1, replica_groups=mesh['section'=2,'dp'=4,'latent'=32] {'latent'}, dimensions={0}, use_global_device_ids=true | all-gather | bytes 675840 | tf_op jit(solution)/shard_map/all_gather | solution.py:114
  682.6 2.1 collective-permute-start.1
  684.7 1.4 subtract_multiply_fusion.1
  686.2 1.4 subtract_multiply_fusion.2
  687.6 159.8 %reduce-scatter.16.cloned.1.call-done = f32[8,1280]{1,0:T(8,128)} async-done(((f32[256,1280]{1,0:T(8,128)}), f32[8,1280]{1,0:T(8,128)}) %reduce-scatter.16.cloned.1.call-update) | async-done | bytes 40976 | tf_op jit(solution)/shard_map/reduce_scatter | solution.py:140
  848.7 8.6 all-reduce.13
  858.4 48.2 %all_gather.26 = bf16[256,1280]{1,0:T(8,128)(2,1)S(1)} all-gather(bf16[8,1280]{1,0:T(8,128)(2,1)S(1)} %add_convert_fusion.6), channel_id=1, replica_groups=mesh['section'=2,'dp'=4,'latent'=32] {'latent'}, dimensions={0}, use_global_device_ids=true | all-gather | bytes 675840 | tf_op jit(solution)/shard_map/all_gather | solution.py:155
  909.0 1.4 fusion.46
  913.0 49.3 %all-reduce.28.cloned.1.call-done = (f32[256,384]{1,0:T(8,128)}, f32[256,384]{1,0:T(8,128)}) async-done(((f32[256,384]{1,0:T(8,128)}, f32[256,384]{1,0:T(8,128)}), (f32[256,384]{1,0:T(8,128)}, f32[256,384]{1,0:T(8,128)})) %all-reduce.28.cloned.1.call-update) | async-done | bytes 786448 | tf_op jit(solution)/shard_map/psum | solution.py:135
  962.3 3.2 fusion.44
  965.8 3.7 fusion.16
  970.8 213.6 %reduce-scatter.18.cloned.1.call-done = f32[8,1280]{1,0:T(8,128)} async-done(((f32[256,1280]{1,0:T(8,128)}), f32[8,1280]{1,0:T(8,128)}) %reduce-scatter.18.cloned.1.call-update) | async-done | bytes 40976 | tf_op jit(solution)/shard_map/reduce_scatter | solution.py:140
  1185.4 8.6 all-reduce.12
  1194.9 48.5 %all_gather.27 = bf16[256,1280]{1,0:T(8,128)(2,1)S(1)} all-gather(bf16[8,1280]{1,0:T(8,128)(2,1)S(1)} %add_convert_fusion.5), channel_id=1, replica_groups=mesh['section'=2,'dp'=4,'latent'=32] {'latent'}, dimensions={0}, use_global_device_ids=true | all-gather | bytes 675840 | tf_op jit(solution)/shard_map/all_gather | solution.py:155
  1243.4 1.6 collective-permute-start.3
  1245.0 3.6 fusion.12
  1248.5 1.9 fusion.14
  1252.9 86.7 %all-reduce.26.cloned.1.call-done = (f32[256,1024]{1,0:T(8,128)}, f32[256,1024]{1,0:T(8,128)}, f32[256,384]{1,0:T(8,128)}, f32[256,1024]{1,0:T(8,128)}) async-done(((f32[256,1024]{1,0:T(8,128)}, f32[256,1024]{1,0:T(8,128)}, f32[256,384]{1,0:T(8,128)}, f32[256,1024]{1,0:T(8,128)}), (f32[256,1024]{1,0:T(8,128)}, f32[256,1024]{1,0:T(8,128)}, f32[256,384]{1,0:T(8,128)}, ...) | async-done | bytes 3538960 | tf_op jit(solution)/shard_map/psum | solution.py:82
  1339.7 3.3 fusion.42
  1343.6 3.3 maximum_convert_fusion.1
  1347.7 1.7 fusion.18
  1349.5 2.7 fusion.24
  1352.3 2.7 fusion.21
  1355.1 3.0 fusion.8
  1358.2 3.0 fusion.10
  1362.5 198.8 %reduce-scatter.24.cloned.1.call-done = f32[8,1280]{1,0:T(8,128)} async-done(((f32[256,1280]{1,0:T(8,128)}), f32[8,1280]{1,0:T(8,128)}) %reduce-scatter.24.cloned.1.call-update) | async-done | bytes 40976 | tf_op jit(solution)/shard_map/reduce_scatter | solution.py:140
  1562.3 8.6 all-reduce.11
  1570.9 187.3 %reduce-scatter.28.cloned.1.call-done = bf16[8,1280]{1,0:T(8,128)(2,1)} async-done(((bf16[256,1280]{1,0:T(8,128)(2,1)}), bf16[8,1280]{1,0:T(8,128)(2,1)}) %reduce-scatter.28.cloned.1.call-update) | async-done | bytes 20496 | tf_op jit(solution)/shard_map/reduce_scatter | solution.py:103
  1758.2 197.1 %reduce-scatter.32.cloned.1.call-done = bf16[8,1280]{1,0:T(8,128)(2,1)} async-done(((bf16[256,1280]{1,0:T(8,128)(2,1)}), bf16[8,1280]{1,0:T(8,128)(2,1)}) %reduce-scatter.32.cloned.1.call-update) | async-done | bytes 20496 | tf_op jit(solution)/shard_map/reduce_scatter | solution.py:103
  1955.3 196.9 %reduce-scatter.30.cloned.1.call-done = bf16[8,1280]{1,0:T(8,128)(2,1)} async-done(((bf16[256,1280]{1,0:T(8,128)(2,1)}), bf16[8,1280]{1,0:T(8,128)(2,1)}) %reduce-scatter.30.cloned.1.call-update) | async-done | bytes 20496 | tf_op jit(solution)/shard_map/reduce_scatter | solution.py:103
  2153.4 48.2 %all_gather.28 = bf16[256,1280]{1,0:T(8,128)(2,1)S(1)} all-gather(bf16[8,1280]{1,0:T(8,128)(2,1)S(1)} %get-tuple-element.43), channel_id=1, replica_groups=mesh['section'=2,'dp'=4,'latent'=32] {'latent'}, dimensions={0}, use_global_device_ids=true | all-gather | bytes 675840 | tf_op jit(solution)/shard_map/all_gather | solution.py:155
  2201.6 1.9 fusion.6
  2208.0 9.7 all-reduce.10
  2217.9 75.1 %all-reduce.9 = (f32[64]{0:T(128)S(1)}, f32[64]{0:T(128)S(1)}, f32[64]{0:T(128)S(1)}) all-reduce(f32[64]{0:T(128)S(1)} %dynamic-slice.20, f32[64]{0:T(128)S(1)} %dynamic-slice.16, f32[64]{0:T(128)S(1)} %dynamic-slice.18), channel_id=1, replica_groups=mesh['section'=2,'dp'=4,'latent'=32] {'latent'}, use_global_device_ids=true, to_apply=%add.2 | all-reduce | flops 192 | bytes 1536
  (144 shorter events, 36.9 us)
Async XLA Ops:
  7.2 1340.5 %copy-start = (bf16[1,1024,1280]{2,1,0:T(8,128)(2,1)S(1)}, bf16[1,1024,1280]{2,1,0:T(8,128)(2,1)}, u32[]{:S(2)}) copy-start(bf16[1,1024,1280]{2,1,0:T(8,128)(2,1)} %param.16) | copy-start | bytes 7864324
  7.2 63.6 %all-reduce.24.cloned.1.call-start = ((), (), s32[]{:S(2)}) async-start(), calls=%async_computation.11 | async-start | bytes 786432 | tf_op jit(solution)/shard_map/psum | solution.py:90
  20.4 1.2 copy-start.1
  20.8 2.2 copy-start.19
  22.9 270.1 %reduce-scatter.12.cloned.1.call-start = ((), (), s32[]{:S(2)}) async-start(), calls=%async_computation.12 | async-start | bytes 1351680 | tf_op jit(solution)/shard_map/reduce_scatter | solution.py:94
  74.5 2.1 copy-start.16
  74.5 332.4 %all-reduce.30.cloned.1.call-start = ((), (), s32[]{:S(2)}) async-start(), calls=%async_computation.25 | async-start | bytes 1572864 | tf_op jit(solution)/shard_map/psum | solution.py:135
  293.0 51.6 %copy-start.3 = (bf16[1,384,1280]{2,1,0:T(8,128)(2,1)S(1)}, bf16[1,384,1280]{2,1,0:T(8,128)(2,1)}, u32[]{:S(2)}) copy-start(bf16[1,384,1280]{2,1,0:T(8,128)(2,1)} %param.22) | copy-start | bytes 2949124
  342.1 3.8 collective-permute-start
  344.6 1.3 copy-start.9
  344.6 1.3 copy-start.11
  347.2 0.9 copy-start.6
  359.7 269.2 %reduce-scatter.14.cloned.1.call-start = ((), (), s32[]{:S(2)}) async-start(), calls=%async_computation.13 | async-start | bytes 1351680 | tf_op jit(solution)/shard_map/reduce_scatter | solution.py:94
  410.7 436.7 %reduce-scatter.16.cloned.1.call-start = ((), (), s32[]{:S(2)}) async-start(), calls=%async_computation.14 | async-start | bytes 1351680 | tf_op jit(solution)/shard_map/reduce_scatter | solution.py:140
  414.0 548.2 %all-reduce.28.cloned.1.call-start = ((), (), s32[]{:S(2)}) async-start(), calls=%async_computation.24 | async-start | bytes 1572864 | tf_op jit(solution)/shard_map/psum | solution.py:135
  629.8 56.4 %copy-start.7 = (bf16[256,1280]{1,0:T(8,128)(2,1)S(1)}, bf16[256,1280]{1,0:T(8,128)(2,1)}, u32[]{:S(2)}) copy-start(bf16[256,1280]{1,0:T(8,128)(2,1)} %copy-done.6) | copy-start | bytes 1966084
  682.6 165.8 %collective-permute-start.1 = (bf16[256,1280]{1,0:T(8,128)(2,1)}, bf16[256,1280]{1,0:T(8,128)(2,1)}, u32[]{:S(2)}, u32[]{:S(2)}) collective-permute-start(bf16[256,1280]{1,0:T(8,128)(2,1)} %all_gather.25), channel_id=1, source_target_pairs={{0,128},{1,129},{2,130},{3,131},{4,132},{5,133},{6,134},{7,135},{8... | collective-permute-start | bytes 1966088 | tf_op jit(solution)/shard_map/ppermute | solution.py:18
  857.3 51.7 %copy-start.2 = (bf16[1,1280,384]{2,1,0:T(8,128)(2,1)S(1)}, bf16[1,1280,384]{2,1,0:T(8,128)(2,1)}, u32[]{:S(2)}) copy-start(bf16[1,1280,384]{2,1,0:T(8,128)(2,1)} %param.20) | copy-start | bytes 2949124
  906.6 3.8 copy-start.14
  906.6 4.0 collective-permute-start.2
  910.4 1.2 copy-start.4
  910.7 0.8 copy-start.10
  912.9 271.5 %reduce-scatter.18.cloned.1.call-start = ((), (), s32[]{:S(2)}) async-start(), calls=%async_computation.15 | async-start | bytes 1351680 | tf_op jit(solution)/shard_map/reduce_scatter | solution.py:140
  965.5 374.1 %all-reduce.26.cloned.1.call-start = ((), (), s32[]{:S(2)}) async-start(), calls=%async_computation.23 | async-start | bytes 7077888 | tf_op jit(solution)/shard_map/psum | solution.py:82
  969.5 275.4 %copy-start.8 = (bf16[256,1280]{1,0:T(8,128)(2,1)S(1)}, bf16[256,1280]{1,0:T(8,128)(2,1)}, u32[]{:S(2)}) copy-start(bf16[256,1280]{1,0:T(8,128)(2,1)} %copy-done.6) | copy-start | bytes 1966084
  1243.4 5.1 copy-start.15
  1243.4 5.1 copy-start.20
  1243.4 7.0 collective-permute-start.3
  1250.4 1.2 copy-start.5
  1252.9 308.4 %reduce-scatter.24.cloned.1.call-start = ((), (), s32[]{:S(2)}) async-start(), calls=%async_computation.18 | async-start | bytes 1351680 | tf_op jit(solution)/shard_map/reduce_scatter | solution.py:140
  1343.0 0.7 copy-start.18
  1343.0 415.2 %reduce-scatter.28.cloned.1.call-start = ((), (), s32[]{:S(2)}) async-start(), calls=%async_computation.20 | async-start | bytes 675840 | tf_op jit(solution)/shard_map/reduce_scatter | solution.py:103
  1346.9 0.8 copy-start.13
  1349.4 605.9 %reduce-scatter.32.cloned.1.call-start = ((), (), s32[]{:S(2)}) async-start(), calls=%async_computation.22 | async-start | bytes 675840 | tf_op jit(solution)/shard_map/reduce_scatter | solution.py:103
  1352.2 800.0 %reduce-scatter.30.cloned.1.call-start = ((), (), s32[]{:S(2)}) async-start(), calls=%async_computation.21 | async-start | bytes 675840 | tf_op jit(solution)/shard_map/reduce_scatter | solution.py:103
  1355.0 851.0 %reduce-scatter.22.cloned.1.call-start = ((), (), s32[]{:S(2)}) async-start(), calls=%async_computation.17 | async-start | bytes 1310720 | tf_op jit(solution)/shard_map/reduce_scatter | solution.py:162
  1358.1 3.1 copy-start.17
  1358.1 847.9 %reduce-scatter.20.cloned.1.call-start = ((), (), s32[]{:S(2)}) async-start(), calls=%async_computation.16 | async-start | bytes 1310720 | tf_op jit(solution)/shard_map/reduce_scatter | solution.py:162
  1361.2 932.4 %reduce-scatter.26.cloned.1.call-start = ((), (), s32[]{:S(2)}) async-start(), calls=%async_computation.19 | async-start | bytes 1310720 | tf_op jit(solution)/shard_map/reduce_scatter | solution.py:162
  2201.6 1.9 copy-start.22
  2201.6 3.2 copy-start.21
  2201.6 4.5 copy-start.12
Sparse Core Ops, SparseCore 0:
  23.0 47.7 all-reduce.23
  75.1 217.8 reduce-scatter.11
  359.9 47.0 all-reduce.29
  411.1 217.7 reduce-scatter.13
  633.1 214.2 reduce-scatter.15
  913.1 49.1 all-reduce.27
  966.6 217.7 reduce-scatter.17
  1253.0 86.6 all-reduce.25
  1344.0 217.2 reduce-scatter.23
  1565.3 192.8 reduce-scatter.27
  1762.3 192.9 reduce-scatter.31
  1959.3 192.8 reduce-scatter.29
  2154.9 22.3 reduce-scatter.21
  2179.8 25.6 reduce-scatter.19
  2208.0 26.0 reduce-scatter.25
where the time goes:
time: 2300 us
  waiting for transfers between devices  1820 us (79%)
  blocking collectives  375 us (16%)
  matrix products  50.5 us (2%)
  other arithmetic  27.6 us (1%)
    reduce_scatter x3, waiting for transfers between devices, on_device(): lax.psum_scatter(jnp.dot(forward_latent_codes, dec_w, preferred_element_t...  581 us
    reduce_scatter x3, waiting for transfers between devices, on_device(): lax.psum_scatter(lax.dot_general(grad_hidden, in_w, CONTRACT_LAST, prefer...  572 us
    reduce_scatter x2, waiting for transfers between devices, on_device(): lax.psum_scatter(jnp.dot(act_out, out_w, preferred_element_type=jnp.float...  430 us
    all_gather x3, blocking collectives, on_device(): grad_full = lax.all_gather(grad_share, 'latent', axis=0, tiled=True)  145 us
    all_gather x2, blocking collectives, on_device(): whole_rows = lax.all_gather(new_share, 'latent', axis=0, tiled=True)  101 us
    psum x2, waiting for transfers between devices, on_device(): lax.psum(lax.dot_general(grad_out, out_w, CONTRACT_LAST, preferred_elemen...  96.5 us
    psum x1, waiting for transfers between devices, on_device(): lax.psum((pre_part, jnp.sum(resid_f, axis=1), jnp.sum(resid_f * resid_f,...  86.7 us
    unnamed x2, blocking collectives  84.8 us
  transfers between devices with their start and end apart: 19, of which 13 were waited for; matrix products, arithmetic and copies ran while one was open for 2% of the time, Pallas kernels for 0%

commit v1 on v0

v1 whole, which is shorter than its diff:
```python
import jax
import jax.numpy as jnp
from jax import lax
from jax.sharding import PartitionSpec as P

D = 5120
EPSILON = 1e-05
SQRT_HALF = 0.7071067811865476
INV_SQRT_TAU = 0.3989422804014327
CONTRACT_LAST = (((1,), (1,)), ((), ()))
F32 = jnp.float32
BF16 = jnp.bfloat16


def gelu_slope(values):
    cumulative = 0.5 * (1.0 + lax.erf(values * SQRT_HALF))
    return cumulative + values * jnp.exp(-0.5 * values * values) * INV_SQRT_TAU


def split3(values):
    high = values.astype(BF16)
    rest = values - high.astype(F32)
    middle = rest.astype(BF16)
    low = (rest - middle.astype(F32)).astype(BF16)
    return [high, middle, low]


def dot(left, right):
    return jnp.dot(left, right, preferred_element_type=F32)


def dot_t(left, right):
    return lax.dot_general(left, right, CONTRACT_LAST, preferred_element_type=F32)


def spread(values, axis):
    count = lax.axis_size(axis)
    copies = jnp.broadcast_to(values[None], (count,) + values.shape)
    return lax.all_to_all(copies, axis, 0, 0)


def exchange(values, axis):
    count = lax.axis_size(axis)
    rows = values.shape[0] // count
    return lax.all_to_all(values.reshape(count, rows, values.shape[1]), axis, 0, 0)


def turn(values, axis, by):
    count = lax.axis_size(axis)
    return lax.ppermute(values, axis, [(i, (i + by) % count) for i in range(count)])


def gather_ring(values, axis):
    return [values] + [turn(values, axis, by) for by in range(1, lax.axis_size(axis))]


def total_ring(values, axis):
    return sum(part.astype(F32) for part in gather_ring(values, axis))


def scatter_ring(values, axis):
    count, place = lax.axis_size(axis), lax.axis_index(axis)
    rows = values.shape[0] // count

    def block(by):
        return lax.dynamic_slice_in_dim(values, (place + by) % count * rows, rows, 0)

    parts = [turn(block(by), axis, by) for by in range(1, count)]
    return block(0).astype(F32) + sum(part.astype(F32) for part in parts)


def pack_rows(values, width, rows):
    terms = jnp.stack(split3(values.reshape(-1, width))).reshape(-1, width)
    return jnp.pad(terms, ((0, rows - terms.shape[0]), (0, 0)))


def unpack_rows(terms, count):
    terms = terms[..., : 3 * count, :].astype(F32)
    return terms[..., :count, :] + terms[..., count : 2 * count, :] + terms[..., 2 * count :, :]


def on_device(
    tokens,
    cotangent,
    enc_weight,
    enc_bias,
    dec_weight,
    dec_bias,
    ln_gain,
    ln_bias,
    in_weight,
    in_bias,
    out_weight,
    out_bias,
):
    dp_count = lax.axis_size("dp")
    latent_count = lax.axis_size("latent")
    all_rows, width = tokens.shape
    half = all_rows // 2
    share = half // latent_count
    block = all_rows // dp_count
    hid = in_weight.shape[2]
    core = lax.axis_index("section")
    first = core == 0
    dp_place = lax.axis_index("dp")
    latent_place = lax.axis_index("latent")
    swap = [(0, 1), (1, 0)]

    def other(values):
        return lax.ppermute(values, "section", swap)

    def pick(mine_if_first, mine_if_second):
        return jnp.where(first, mine_if_first, mine_if_second)

    def own_rows(values):
        return lax.dynamic_slice_in_dim(values, latent_place * share, share, 0)

    in_w = in_weight[0]
    out_w = out_weight[0]
    gained = (in_w.astype(F32) * ln_gain[0][:, None]).astype(BF16)
    column_sum = jnp.sum(gained.astype(F32), axis=0)
    shift_in = jnp.sum(in_w.astype(F32) * ln_bias[0][:, None], axis=0)
    pad_bias = jnp.pad(out_bias[0], (0, -width % hid))
    vector_count = 3 + pad_bias.shape[0] // hid
    vectors = jnp.concatenate([column_sum, shift_in, in_bias[0], pad_bias])

    def row_parts(resid):
        resid_f = resid.astype(F32)
        local_mean = jnp.mean(resid_f, axis=1)
        centred = resid_f - local_mean[:, None]
        return local_mean, jnp.sum(centred * centred, axis=1)

    def stat_columns(local_mean, square):
        stats = jnp.stack(split3(local_mean) + split3(square), axis=1)
        return jnp.pad(stats, ((0, 0), (0, 128 - stats.shape[1])))

    def row_stats(parts):
        means, squares = [], []
        for stats in parts:
            stats = stats[:, :6].astype(F32)
            means.append(stats[:, 0] + stats[:, 1] + stats[:, 2])
            squares.append(stats[:, 3] + stats[:, 4] + stats[:, 5])
        mean = sum(means) / dp_count
        aparts = [local_mean - mean for local_mean in means]
        variance = sum(squares) / D + sum(apart * apart for apart in aparts) / dp_count
        return mean, lax.rsqrt(variance + EPSILON), aparts

    def pre_hidden(parts, aparts, inv, sums):
        total = sum(part.astype(F32) for part in parts)
        total = total + sum(apart[:, None] * s[None] for apart, s in zip(aparts, sums))
        return total * inv[:, None]

    tokens_half = lax.dynamic_slice_in_dim(tokens, core * half, half, 0)
    cot_half = lax.dynamic_slice_in_dim(cotangent, core * half, half, 0)
    mean_all, square_all = row_parts(tokens)
    forward_all = (dot(tokens, gained) - mean_all[:, None] * column_sum[None]).astype(BF16)
    grad_all = dot_t(cotangent, out_w).astype(BF16)
    packed = pack_rows(vectors, hid, 32)
    there = other(jnp.concatenate([pick(forward_all[half:], grad_all[:half]), packed], axis=0))
    part_0 = pick(forward_all[:half], there[:half])
    grad_act_part = pick(there[:half], grad_all[half:])
    vectors_there = unpack_rows(there[half:], vector_count)
    vectors = vectors.reshape(-1, hid)
    vectors_0 = pick(vectors, vectors_there)
    vectors_1 = pick(vectors_there, vectors)

    gained_there = other(gained)
    out_there = other(out_w)
    gained_0, gained_1 = pick(gained, gained_there), pick(gained_there, gained)
    out_w0 = pick(out_w, out_there)

    def gathered(part, stats, layer_vectors):
        rows = pack_rows(layer_vectors[:2].reshape(-1), hid, 16)
        payload = jnp.concatenate([part, rows], axis=0)
        stats = jnp.pad(stats, ((0, 16), (0, 0)))
        got = gather_ring(jnp.concatenate([payload, stats], axis=1), "dp")
        mean, inv, aparts = row_stats([g[:half, hid:] for g in got])
        dp_vectors = [unpack_rows(g[half:, :hid], 2) for g in got]
        sums = [v[0] for v in dp_vectors]
        pre = pre_hidden([g[:half, :hid] for g in got], aparts, inv, sums)
        shift = sum(v[1] for v in dp_vectors) + layer_vectors[2]
        return pre, pre + shift[None], mean, inv, sum(sums)

    def half_of(values):
        return lax.dynamic_slice_in_dim(values, core * half, half, 0)

    stats_0 = stat_columns(half_of(mean_all), half_of(square_all))
    pre_0, hidden_0, mean_0, inv_0, sums_0 = gathered(part_0, stats_0, vectors_0)
    act_0 = jax.nn.gelu(hidden_0, approximate=False).astype(BF16)
    mlp = exchange(dot(act_0, out_w0).astype(BF16), "latent")
    tokens_rows = own_rows(tokens_half).astype(F32)
    bias_row = vectors_0[3:].reshape(-1)[:width]
    resid_rows = (tokens_rows + jnp.sum(mlp.astype(F32), axis=0) + bias_row[None]).astype(BF16)
    resid_half = spread(resid_rows, "latent").reshape(half, width)

    local_mean, square = row_parts(resid_half)
    part_1 = dot(resid_half, gained_1) - local_mean[:, None] * vectors_1[0][None]
    pre_1, hidden_1, mean_1, inv_1, sums_1 = gathered(
        part_1.astype(BF16), stat_columns(local_mean, square), vectors_1
    )
    grad_act_1 = total_ring(grad_act_part, "dp")

    def backward(grad_act, hidden, pre, weight, sums, resid, mean, inv, grad_rows):
        grad_hidden = (grad_act * gelu_slope(hidden)).astype(BF16)
        grad_f = grad_hidden.astype(F32)
        total = jnp.sum(grad_f * sums[None], axis=1)
        cross = jnp.sum(grad_f * pre, axis=1)
        extra = jnp.stack(split3(total) + split3(cross), axis=1)
        extra = jnp.pad(extra, ((0, 0), (0, 128 - extra.shape[1])))
        partial = dot_t(grad_hidden, weight).astype(BF16)
        summed = exchange(jnp.concatenate([partial, extra], axis=1), "latent")
        summed = jnp.sum(summed.astype(F32), axis=0)
        grad_norm, extra = summed[:, :width], summed[:, width : width + 6] / D
        mean_grad = (extra[:, 0] + extra[:, 1] + extra[:, 2])[:, None]
        mean_cross = (extra[:, 3] + extra[:, 4] + extra[:, 5])[:, None]
        inv_rows = own_rows(inv)[:, None]
        normed = (resid - own_rows(mean)[:, None]) * inv_rows
        grad_resid = inv_rows * (grad_norm - mean_grad - normed * mean_cross)
        new_rows = (grad_rows + grad_resid).astype(BF16)
        return new_rows, spread(new_rows, "latent").reshape(half, width)

    cot_rows = own_rows(cot_half).astype(F32)
    grad_rows_1, grad_half_1 = backward(
        grad_act_1, hidden_1, pre_1, gained_1, sums_1, resid_rows.astype(F32), mean_1, inv_1, cot_rows
    )
    grad_act_0 = total_ring(dot_t(grad_half_1, out_w0).astype(BF16), "dp")
    _, grad_half_0 = backward(
        grad_act_0, hidden_0, pre_0, gained_0, sums_0, tokens_rows, mean_0, inv_0,
        grad_rows_1.astype(F32),
    )

    resid_all = pick(tokens, jnp.concatenate([other(resid_half), resid_half], axis=0))
    pre_codes = scatter_ring(dot(resid_all, enc_weight[0]).astype(BF16), "dp")
    codes = jnp.maximum(pre_codes + enc_bias[0][None], 0.0).astype(BF16)

    grad_there = other(pick(grad_half_1, grad_half_0))
    grad_all = pick(
        jnp.concatenate([grad_half_0, grad_there], axis=0),
        jnp.concatenate([grad_there, grad_half_1], axis=0),
    )
    effect = codes.astype(F32) * scatter_ring(dot_t(grad_all, dec_weight[0]).astype(BF16), "dp")
    error = (resid_all.astype(F32) - dec_bias[0][None]) * grad_all.astype(F32)
    error = (jnp.sum(error, axis=1) / latent_count).reshape(dp_count, 1, block)
    error = lax.all_to_all(error, "dp", 0, 0)
    error = jnp.sum(error, axis=0) - jnp.sum(effect, axis=1)[None]
    error = jnp.sum(spread(error, "latent"), axis=(0, 1))
    return effect.astype(BF16)[None], error[None]


def solution(mesh):
    in_specs = (
        P(None, "dp"),
        P(None, "dp"),
        P("section", "dp", "latent"),
        P("section", "latent"),
        P("section", "latent", "dp"),
        P("section", "dp"),
        P("section", "dp"),
        P("section", "dp"),
        P("section", "dp", "latent"),
        P("section", "latent"),
        P("section", "latent", "dp"),
        P("section", "dp"),
    )
    out_specs = (P("section", "dp", "latent"), P("section", "dp"))
    return jax.shard_map(
        on_device, mesh=mesh, in_specs=in_specs, out_specs=out_specs, check_vma=False
    )
```

time: 2300 us -> 321 us (0.14)
  waiting for transfers between devices: 1820 us -> 144 us
  blocking collectives: 375 us -> 38.5 us
  starting transfers between devices: 7.1 us -> 67 us
  matrix products: 50.5 us -> 17.6 us
    reduce_scatter x11 -> x0, waiting for transfers between devices: 1580 us -> none  [the longest x3 581 us: on_device(): lax.psum_scatter(jnp.dot(forward_latent_codes, dec_w, preferred_element_t...]
    all_gather x5 -> x0, blocking collectives: 246 us -> none  [the longest x3 145 us: on_device(): grad_full = lax.all_gather(grad_share, 'latent', axis=0, tiled=True)]
    psum x4 -> x0, waiting for transfers between devices: 231 us -> none  [the longest x2 96.5 us: on_device(): lax.psum(lax.dot_general(grad_out, out_w, CONTRACT_LAST, preferred_elemen...]
    all_to_all x0 -> x6, waiting for transfers between devices: none -> 103 us  [the longest x3 60.6 us: exchange(): lax.all_to_all(values.reshape(count, rows, values.shape[1]), axis, 0, 0)]
    unnamed x2 -> x0, blocking collectives: 84.8 us -> none
    psum x5 -> x0, blocking collectives: 44.3 us -> none  [the longest x3 25.8 us: on_device(): lax.psum((jnp.sum(grad_norm, axis=1), jnp.sum(grad_norm * normed_share, a...]
    ppermute x4 -> x23, waiting for transfers between devices: 0.15 us -> 41.3 us  [the longest x18 41.3 us: turn(): lax.ppermute(values, axis, [(i, (i + by) % count) for i in range(count)])]
    all_to_all x0 -> x6, starting transfers between devices: none -> 39.6 us  [the longest x3 24.6 us: exchange(): lax.all_to_all(values.reshape(count, rows, values.shape[1]), axis, 0, 0)]
  transfers between devices with their start and end apart: 19 -> 29, of which waited for: 13 -> 15; matrix products, arithmetic and copies ran while one was open for 2% -> 8% of each run, Pallas kernels for 0% -> 0%
where the time goes in v1:
time: 321 us; the launch traced here: 319 us
  waiting for transfers between devices  144 us (45%)
  starting transfers between devices  67 us (21%)
  blocking collectives  38.5 us (12%)
  other arithmetic  37.1 us (12%)
  matrix products  17.6 us (5%)
  local copies, waits for them, and re-layouts  13.5 us (4%)
    all_to_all x3, waiting for transfers between devices, exchange(): lax.all_to_all(values.reshape(count, rows, values.shape[1]), axis, 0, 0)  60.6 us
    ppermute x18, waiting for transfers between devices, turn(): lax.ppermute(values, axis, [(i, (i + by) % count) for i in range(count)])  41.3 us
    all_to_all x2, blocking collectives, spread(): return lax.all_to_all(copies, axis, 0, 0)  38.5 us
    all_to_all x2, waiting for transfers between devices, spread(): return lax.all_to_all(copies, axis, 0, 0)  34.4 us
    ppermute x18, starting transfers between devices, turn(): lax.ppermute(values, axis, [(i, (i + by) % count) for i in range(count)])  26.8 us
    all_to_all x3, starting transfers between devices, exchange(): lax.all_to_all(values.reshape(count, rows, values.shape[1]), axis, 0, 0)  24.6 us
    all_to_all x2, starting transfers between devices, spread(): return lax.all_to_all(copies, axis, 0, 0)  10.5 us
    dot_general x4, matrix products, dot(): return jnp.dot(left, right, preferred_element_type=F32)  9.83 us
  transfers between devices with their start and end apart: 29, of which 15 were waited for; matrix products, arithmetic and copies ran while one was open for 8% of the time, Pallas kernels for 0%

profile of v1, /device:TPU:8, one launch (start us, length us, event | category | flops | bytes accessed | tf_op | source)
XLA Modules:
  0.0 319.5 jit_solution(3340758879919050674)
XLA Ops:
  2.2 1.6 convert_reduce_fusion
  5.2 2.6 convert_reduce_fusion.1
  8.1 2.5 fusion.20
  12.3 1.8 fusion.1
  17.7 1.9 slice_select_fusion
  19.6 2.3 collective-permute-start.3
  23.0 1.9 collective-permute-start.1
  25.0 6.3 %collective-permute-done.3 = bf16[272,512]{0,1:T(8,128)(2,1)S(1)} collective-permute-done((bf16[272,512]{0,1:T(8,128)(2,1)S(1)}, bf16[272,512]{0,1:T(8,128)(2,1)S(1)}, u32[]{:S(2)}, u32[]{:S(2)}) %collective-permute-start.3) | collective-permute-done | bytes 278560 | tf_op jit(solution)/shard_map/ppermute | solution.py:50
  31.5 9.2 %collective-permute-done.2 = bf16[272,512]{0,1:T(8,128)(2,1)S(1)} collective-permute-done((bf16[272,512]{0,1:T(8,128)(2,1)S(1)}, bf16[272,512]{0,1:T(8,128)(2,1)S(1)}, u32[]{:S(2)}, u32[]{:S(2)}) %collective-permute-start.2) | collective-permute-done | bytes 278560 | tf_op jit(solution)/shard_map/ppermute | solution.py:50
  45.1 2.3 fusion.6
  47.4 11.4 %all-to-all-start = ((bf16[32,8,1280]{2,1,0:T(8,128)(2,1)}), bf16[32,8,1280]{2,1,0:T(8,128)(2,1)}, u32[]{:S(2)}, u32[]{:S(2)}) async-start(bf16[32,8,1280]{2,1,0:T(8,128)(2,1)} %fusion.6), calls=%async_computation | async-start | bytes 1310720 | tf_op jit(solution)/shard_map/all_to_all | solution.py:45
  59.1 19.6 %all-to-all-done = bf16[32,8,1280]{2,1,0:T(8,128)(2,1)} async-done(((bf16[32,8,1280]{2,1,0:T(8,128)(2,1)}), bf16[32,8,1280]{2,1,0:T(8,128)(2,1)}, u32[]{:S(2)}, u32[]{:S(2)}) %all-to-all-start) | async-done | bytes 655392 | tf_op jit(solution)/shard_map/all_to_all | solution.py:45
  81.5 5.0 %all-to-all-start.1 = ((bf16[32,8,1280]{2,1,0:T(8,128)(2,1)}), bf16[32,8,1280]{2,1,0:T(8,128)(2,1)S(1)}, u32[]{:S(2)}, u32[]{:S(2)}) async-start(bf16[32,8,1280]{2,1,0:T(8,128)(2,1)} %broadcast_in_dim.12), calls=%async_computation.1 | async-start | bytes 1310720 | tf_op jit(solution)/shard_map/all_to_all | solution.py:39
  90.8 15.1 %all-to-all-done.1 = bf16[32,8,1280]{2,1,0:T(8,128)(2,1)S(1)} async-done(((bf16[32,8,1280]{2,1,0:T(8,128)(2,1)}), bf16[32,8,1280]{2,1,0:T(8,128)(2,1)S(1)}, u32[]{:S(2)}, u32[]{:S(2)}) %all-to-all-start.1) | async-done | bytes 655392 | tf_op jit(solution)/shard_map/all_to_all | solution.py:39
  106.8 1.9 fusion.21
  108.7 3.5 %collective-permute-start.12 = (bf16[272,512]{0,1:T(8,128)(2,1)S(1)}, bf16[272,512]{0,1:T(8,128)(2,1)S(1)}, u32[]{:S(2)}, u32[]{:S(2)}) collective-permute-start(bf16[272,512]{0,1:T(8,128)(2,1)S(1)} %fusion.58), channel_id=1, source_target_pairs={{0,96},{32,0},{64,32},{96,64},{1,97},{33,1},{65,33},{97,65},{2,98}... | collective-permute-start | bytes 835592 | tf_op jit(solution)/shard_map/ppermute | solution.py:50
  112.3 2.1 collective-permute-start.14
  115.1 2.4 collective-permute-start.11
  117.5 4.3 %collective-permute-done.12 = bf16[272,512]{0,1:T(8,128)(2,1)S(1)} collective-permute-done((bf16[272,512]{0,1:T(8,128)(2,1)S(1)}, bf16[272,512]{0,1:T(8,128)(2,1)S(1)}, u32[]{:S(2)}, u32[]{:S(2)}) %collective-permute-start.12) | collective-permute-done | bytes 278560 | tf_op jit(solution)/shard_map/ppermute | solution.py:50
  123.0 12.0 %collective-permute-done.11 = bf16[272,512]{0,1:T(8,128)(2,1)S(1)} collective-permute-done((bf16[272,512]{0,1:T(8,128)(2,1)S(1)}, bf16[272,512]{0,1:T(8,128)(2,1)S(1)}, u32[]{:S(2)}, u32[]{:S(2)}) %collective-permute-start.11) | collective-permute-done | bytes 278560 | tf_op jit(solution)/shard_map/ppermute | solution.py:50
  135.2 1.6 collective-permute-done.10
  139.2 1.8 convolution_convert_fusion.1
  141.9 7.0 %all-to-all-start.2 = ((bf16[32,8,1408]{2,1,0:T(8,128)(2,1)}), bf16[32,8,1408]{2,1,0:T(8,128)(2,1)}, u32[]{:S(2)}, u32[]{:S(2)}) async-start(bf16[32,8,1408]{2,1,0:T(8,128)(2,1)} %fusion.30), calls=%async_computation.2 | async-start | bytes 1441792 | tf_op jit(solution)/shard_map/all_to_all | solution.py:45
  149.1 20.4 %all-to-all-done.2 = bf16[32,8,1408]{2,1,0:T(8,128)(2,1)} async-done(((bf16[32,8,1408]{2,1,0:T(8,128)(2,1)}), bf16[32,8,1408]{2,1,0:T(8,128)(2,1)}, u32[]{:S(2)}, u32[]{:S(2)}) %all-to-all-start.2) | async-done | bytes 720928 | tf_op jit(solution)/shard_map/all_to_all | solution.py:45
  169.5 1.4 convert_reduce_fusion.4
  172.6 24.2 %all_to_all.40 = bf16[32,8,1280]{2,1,0:T(8,128)(2,1)S(1)} all-to-all(bf16[32,8,1280]{2,1,0:T(8,128)(2,1)S(1)} %broadcast_in_dim.13), channel_id=1, replica_groups=mesh['section'=2,'dp'=4,'latent'=32] {'latent'}, dimensions={0} | all-to-all | bytes 1310720 | tf_op jit(solution)/shard_map/all_to_all | solution.py:39
  197.7 2.5 collective-permute-start.16
  200.2 1.4 collective-permute-start.17
  202.3 3.3 %collective-permute-done.16 = bf16[256,384]{0,1:T(8,128)(2,1)S(1)} collective-permute-done((bf16[256,384]{0,1:T(8,128)(2,1)S(1)}, bf16[256,384]{0,1:T(8,128)(2,1)S(1)}, u32[]{:S(2)}, u32[]{:S(2)}) %collective-permute-start.16) | collective-permute-done | bytes 196640 | tf_op jit(solution)/shard_map/ppermute | solution.py:50
  205.6 1.9 collective-permute-done.17
  207.5 1.9 collective-permute-done.18
  210.0 1.8 convolution_convert_fusion
  212.8 6.2 %all-to-all-start.4 = ((bf16[32,8,1408]{2,1,0:T(8,128)(2,1)}), bf16[32,8,1408]{2,1,0:T(8,128)(2,1)}, u32[]{:S(2)}, u32[]{:S(2)}) async-start(bf16[32,8,1408]{2,1,0:T(8,128)(2,1)} %fusion.32), calls=%async_computation.4 | async-start | bytes 1441792 | tf_op jit(solution)/shard_map/all_to_all | solution.py:45
  219.2 20.7 %all-to-all-done.4 = bf16[32,8,1408]{2,1,0:T(8,128)(2,1)} async-done(((bf16[32,8,1408]{2,1,0:T(8,128)(2,1)}), bf16[32,8,1408]{2,1,0:T(8,128)(2,1)}, u32[]{:S(2)}, u32[]{:S(2)}) %all-to-all-start.4) | async-done | bytes 720928 | tf_op jit(solution)/shard_map/all_to_all | solution.py:45
  239.8 1.2 convert_reduce_fusion.3
  243.0 5.4 %all-to-all-start.5 = ((bf16[32,8,1280]{2,1,0:T(8,128)(2,1)}), bf16[32,8,1280]{2,1,0:T(8,128)(2,1)}, u32[]{:S(2)}, u32[]{:S(2)}) async-start(bf16[32,8,1280]{2,1,0:T(8,128)(2,1)} %broadcast_in_dim.14), calls=%async_computation.5 | async-start | bytes 1310720 | tf_op jit(solution)/shard_map/all_to_all | solution.py:39
  248.6 19.2 %all-to-all-done.5 = bf16[32,8,1280]{2,1,0:T(8,128)(2,1)} async-done(((bf16[32,8,1280]{2,1,0:T(8,128)(2,1)}), bf16[32,8,1280]{2,1,0:T(8,128)(2,1)}, u32[]{:S(2)}, u32[]{:S(2)}) %all-to-all-start.5) | async-done | bytes 655392 | tf_op jit(solution)/shard_map/all_to_all | solution.py:39
  267.8 2.2 broadcast_select_fusion.2
  270.1 3.2 fusion.9
  275.1 1.6 collective-permute-start.7
  276.7 2.6 collective-permute-start.8
  279.3 3.1 fusion.12
  283.3 2.5 collective-permute-start.21
  286.7 2.5 multiply_reduce_fusion
  289.8 4.5 %all-to-all-start.6 = ((f32[4,1,128]{2,1,0:T(1,128)}), f32[4,1,128]{2,1,0:T(1,128)S(1)}, u32[]{:S(2)}, u32[]{:S(2)}) async-start(f32[4,1,128]{2,1,0:T(1,128)} %bitcast.44), calls=%async_computation.6 | async-start | bytes 4096 | tf_op jit(solution)/shard_map/all_to_all | solution.py:244
  294.3 7.8 %all-to-all-done.6 = f32[4,1,128]{2,1,0:T(1,128)S(1)} async-done(((f32[4,1,128]{2,1,0:T(1,128)}), f32[4,1,128]{2,1,0:T(1,128)S(1)}, u32[]{:S(2)}, u32[]{:S(2)}) %all-to-all-start.6) | async-done | bytes 2080 | tf_op jit(solution)/shard_map/all_to_all | solution.py:244
  302.2 2.5 fusion.174
  304.7 14.3 %all_to_all.41 = f32[32,1,128]{2,1,0:T(1,128)S(1)} all-to-all(f32[32,1,128]{2,1,0:T(1,128)S(1)} %broadcast_in_dim.16), channel_id=1, replica_groups=mesh['section'=2,'dp'=4,'latent'=32] {'latent'}, dimensions={0} | all-to-all | bytes 32768 | tf_op jit(solution)/shard_map/all_to_all | solution.py:39
  (239 shorter events, 39.6 us)
Async XLA Ops:
  0.6 269.4 %copy-start = (bf16[1,1280,1024]{2,1,0:T(8,128)(2,1)S(1)}, bf16[1,1280,1024]{2,1,0:T(8,128)(2,1)}, u32[]{:S(2)}) copy-start(bf16[1,1280,1024]{2,1,0:T(8,128)(2,1)} %param.14) | copy-start | bytes 7864324
  12.3 2.3 collective-permute-start
  19.6 11.7 %collective-permute-start.3 = (bf16[272,512]{0,1:T(8,128)(2,1)S(1)}, bf16[272,512]{0,1:T(8,128)(2,1)S(1)}, u32[]{:S(2)}, u32[]{:S(2)}) collective-permute-start(bf16[272,512]{0,1:T(8,128)(2,1)S(1)} %fusion.56), channel_id=1, source_target_pairs={{0,96},{32,0},{64,32},{96,64},{1,97},{33,1},{65,33},{97,65},{2,98}... | collective-permute-start | bytes 835592 | tf_op jit(solution)/shard_map/ppermute | solution.py:50
  21.9 22.2 %collective-permute-start.4 = (bf16[384,1280]{1,0:T(8,128)(2,1)S(1)}, bf16[384,1280]{1,0:T(8,128)(2,1)S(1)}, u32[]{:S(2)}, u32[]{:S(2)}) collective-permute-start(bf16[384,1280]{1,0:T(8,128)(2,1)S(1)} %bitcast.136), channel_id=1, source_target_pairs={{0,128},{128,0},{1,129},{129,1},{2,130},{130,2},{3,131},{131,3},{4... | collective-permute-start | bytes 2949128 | tf_op jit(solution)/shard_map/ppermute | solution.py:110
  22.1 18.5 %collective-permute-start.2 = (bf16[272,512]{0,1:T(8,128)(2,1)S(1)}, bf16[272,512]{0,1:T(8,128)(2,1)S(1)}, u32[]{:S(2)}, u32[]{:S(2)}) collective-permute-start(bf16[272,512]{0,1:T(8,128)(2,1)S(1)} %fusion.56), channel_id=1, source_target_pairs={{0,64},{32,96},{64,0},{96,32},{1,65},{33,97},{65,1},{97,33},{2,66}... | collective-permute-start | bytes 835592 | tf_op jit(solution)/shard_map/ppermute | solution.py:50
  23.0 18.8 %collective-permute-start.1 = (bf16[272,512]{0,1:T(8,128)(2,1)S(1)}, bf16[272,512]{0,1:T(8,128)(2,1)S(1)}, u32[]{:S(2)}, u32[]{:S(2)}) collective-permute-start(bf16[272,512]{0,1:T(8,128)(2,1)S(1)} %fusion.56), channel_id=1, source_target_pairs={{0,32},{32,64},{64,96},{96,0},{1,33},{33,65},{65,97},{97,1},{2,34}... | collective-permute-start | bytes 835592 | tf_op jit(solution)/shard_map/ppermute | solution.py:50
  47.4 31.2 %all-to-all-start = ((bf16[32,8,1280]{2,1,0:T(8,128)(2,1)}), bf16[32,8,1280]{2,1,0:T(8,128)(2,1)}, u32[]{:S(2)}, u32[]{:S(2)}) async-start(bf16[32,8,1280]{2,1,0:T(8,128)(2,1)} %fusion.6), calls=%async_computation | async-start | bytes 1310720 | tf_op jit(solution)/shard_map/all_to_all | solution.py:45
  81.5 24.4 %all-to-all-start.1 = ((bf16[32,8,1280]{2,1,0:T(8,128)(2,1)}), bf16[32,8,1280]{2,1,0:T(8,128)(2,1)S(1)}, u32[]{:S(2)}, u32[]{:S(2)}) async-start(bf16[32,8,1280]{2,1,0:T(8,128)(2,1)} %broadcast_in_dim.12), calls=%async_computation.1 | async-start | bytes 1310720 | tf_op jit(solution)/shard_map/all_to_all | solution.py:39
  86.6 20.2 %collective-permute-start.9 = (bf16[1280,384]{1,0:T(8,128)(2,1)}, bf16[1280,384]{1,0:T(8,128)(2,1)}, u32[]{:S(2)}, u32[]{:S(2)}) collective-permute-start(bf16[1280,384]{1,0:T(8,128)(2,1)} %get-tuple-element.53), channel_id=1, source_target_pairs={{0,128},{128,0},{1,129},{129,1},{2,130},{130,2},{3,131},{131,3},{4... | collective-permute-start | bytes 2949128 | tf_op jit(solution)/shard_map/ppermute | solution.py:110
  108.7 13.1 %collective-permute-start.12 = (bf16[272,512]{0,1:T(8,128)(2,1)S(1)}, bf16[272,512]{0,1:T(8,128)(2,1)S(1)}, u32[]{:S(2)}, u32[]{:S(2)}) collective-permute-start(bf16[272,512]{0,1:T(8,128)(2,1)S(1)} %fusion.58), channel_id=1, source_target_pairs={{0,96},{32,0},{64,32},{96,64},{1,97},{33,1},{65,33},{97,65},{2,98}... | collective-permute-start | bytes 835592 | tf_op jit(solution)/shard_map/ppermute | solution.py:50
  112.2 26.1 %collective-permute-start.13 = (bf16[256,384]{0,1:T(8,128)(2,1)S(1)}, bf16[256,384]{0,1:T(8,128)(2,1)S(1)}, u32[]{:S(2)}, u32[]{:S(2)}) collective-permute-start(bf16[256,384]{0,1:T(8,128)(2,1)S(1)} %copy-done.9), channel_id=1, source_target_pairs={{0,32},{32,64},{64,96},{96,0},{1,33},{33,65},{65,97},{97,1},{2,34}... | collective-permute-start | bytes 589832 | tf_op jit(solution)/shard_map/ppermute | solution.py:50
  112.3 26.0 %collective-permute-start.14 = (bf16[256,384]{0,1:T(8,128)(2,1)S(1)}, bf16[256,384]{0,1:T(8,128)(2,1)S(1)}, u32[]{:S(2)}, u32[]{:S(2)}) collective-permute-start(bf16[256,384]{0,1:T(8,128)(2,1)S(1)} %copy-done.9), channel_id=1, source_target_pairs={{0,64},{32,96},{64,0},{96,32},{1,65},{33,97},{65,1},{97,33},{2,66}... | collective-permute-start | bytes 589832 | tf_op jit(solution)/shard_map/ppermute | solution.py:50
  114.4 23.9 %collective-permute-start.15 = (bf16[256,384]{0,1:T(8,128)(2,1)S(1)}, bf16[256,384]{0,1:T(8,128)(2,1)S(1)}, u32[]{:S(2)}, u32[]{:S(2)}) collective-permute-start(bf16[256,384]{0,1:T(8,128)(2,1)S(1)} %copy-done.9), channel_id=1, source_target_pairs={{0,96},{32,0},{64,32},{96,64},{1,97},{33,1},{65,33},{97,65},{2,98}... | collective-permute-start | bytes 589832 | tf_op jit(solution)/shard_map/ppermute | solution.py:50
  115.1 19.9 %collective-permute-start.11 = (bf16[272,512]{0,1:T(8,128)(2,1)S(1)}, bf16[272,512]{0,1:T(8,128)(2,1)S(1)}, u32[]{:S(2)}, u32[]{:S(2)}) collective-permute-start(bf16[272,512]{0,1:T(8,128)(2,1)S(1)} %fusion.58), channel_id=1, source_target_pairs={{0,64},{32,96},{64,0},{96,32},{1,65},{33,97},{65,1},{97,33},{2,66}... | collective-permute-start | bytes 835592 | tf_op jit(solution)/shard_map/ppermute | solution.py:50
  121.8 15.0 %collective-permute-start.10 = (bf16[272,512]{0,1:T(8,128)(2,1)S(1)}, bf16[272,512]{0,1:T(8,128)(2,1)S(1)}, u32[]{:S(2)}, u32[]{:S(2)}) collective-permute-start(bf16[272,512]{0,1:T(8,128)(2,1)S(1)} %fusion.58), channel_id=1, source_target_pairs={{0,32},{32,64},{64,96},{96,0},{1,33},{33,65},{65,97},{97,1},{2,34}... | collective-permute-start | bytes 835592 | tf_op jit(solution)/shard_map/ppermute | solution.py:50
  140.9 8.0 %copy-start.19 = (f32[256,1]{0,1:T(1,128)S(1)}, f32[256,1]{0,1:T(1,128)}, u32[]{:S(2)}) copy-start(f32[256,1]{0,1:T(1,128)} %copy-done.18) | copy-start | bytes 3076
  140.9 8.0 %copy-start.21 = (f32[256,1]{0,1:T(1,128)S(1)}, f32[256,1]{0,1:T(1,128)}, u32[]{:S(2)}) copy-start(f32[256,1]{0,1:T(1,128)} %copy-done.20) | copy-start | bytes 3076
  141.0 8.0 %copy-start.23 = (f32[256,1]{0,1:T(1,128)S(1)}, f32[256,1]{0,1:T(1,128)}, u32[]{:S(2)}) copy-start(f32[256,1]{0,1:T(1,128)} %copy-done.22) | copy-start | bytes 3076
  141.0 8.0 %copy-start.25 = (f32[256,1]{0,1:T(1,128)S(1)}, f32[256,1]{0,1:T(1,128)}, u32[]{:S(2)}) copy-start(f32[256,1]{0,1:T(1,128)} %copy-done.24) | copy-start | bytes 3076
  141.0 8.0 %copy-start.32 = (f32[256,1]{0,1:T(1,128)S(1)}, f32[256,1]{0,1:T(1,128)}, u32[]{:S(2)}) copy-start(f32[256,1]{0,1:T(1,128)} %get-tuple-element.31) | copy-start | bytes 3076
  141.9 29.2 %copy-start.15 = (bf16[8,1280]{1,0:T(8,128)(2,1)S(1)}, bf16[8,1280]{1,0:T(8,128)(2,1)}, u32[]{:S(2)}) copy-start(bf16[8,1280]{1,0:T(8,128)(2,1)} %copy-done.14) | copy-start | bytes 61444
  141.9 27.6 %all-to-all-start.2 = ((bf16[32,8,1408]{2,1,0:T(8,128)(2,1)}), bf16[32,8,1408]{2,1,0:T(8,128)(2,1)}, u32[]{:S(2)}, u32[]{:S(2)}) async-start(bf16[32,8,1408]{2,1,0:T(8,128)(2,1)} %fusion.30), calls=%async_computation.2 | async-start | bytes 1441792 | tf_op jit(solution)/shard_map/all_to_all | solution.py:45
  169.5 27.3 %copy-start.37 = (bf16[1,384,1280]{2,1,0:T(8,128)(2,1)S(1)}, bf16[1,384,1280]{2,1,0:T(8,128)(2,1)}, u32[]{:S(2)}) copy-start(bf16[1,384,1280]{2,1,0:T(8,128)(2,1)} %param.22) | copy-start | bytes 2949124
  169.5 27.3 %copy-start.39 = (bf16[384,1280]{1,0:T(8,128)(2,1)S(1)}, bf16[384,1280]{1,0:T(8,128)(2,1)}, u32[]{:S(2)}) copy-start(bf16[384,1280]{1,0:T(8,128)(2,1)} %copy-done.38) | copy-start | bytes 2949124
  196.8 12.6 %copy-start.5 = (f32[256,384]{0,1:T(8,128)S(1)}, f32[256,384]{0,1:T(8,128)}, u32[]{:S(2)}) copy-start(f32[256,384]{0,1:T(8,128)} %copy-done.4) | copy-start | bytes 1179652
  196.8 12.6 %copy-start.26 = (f32[384]{0:T(512)S(1)}, f32[384]{0:T(512)}, u32[]{:S(2)}) copy-start(f32[384]{0:T(512)} %get-tuple-element.2) | copy-start | bytes 4612
  196.8 12.6 %copy-start.28 = (f32[384]{0:T(512)S(1)}, f32[384]{0:T(512)}, u32[]{:S(2)}) copy-start(f32[384]{0:T(512)} %copy-done.27) | copy-start | bytes 4612
  197.7 7.9 %collective-permute-start.16 = (bf16[256,384]{0,1:T(8,128)(2,1)S(1)}, bf16[256,384]{0,1:T(8,128)(2,1)S(1)}, u32[]{:S(2)}, u32[]{:S(2)}) collective-permute-start(bf16[256,384]{0,1:T(8,128)(2,1)S(1)} %convolution_convert_fusion.4), channel_id=1, source_target_pairs={{0,32},{32,64},{64,96},{96,0},{1,33},{33,65},{65,97},{97,1},{2,34}... | collective-permute-start | bytes 589832 | tf_op jit(solution)/shard_map/ppermute | solution.py:50
  200.2 7.3 %collective-permute-start.17 = (bf16[256,384]{0,1:T(8,128)(2,1)S(1)}, bf16[256,384]{0,1:T(8,128)(2,1)S(1)}, u32[]{:S(2)}, u32[]{:S(2)}) collective-permute-start(bf16[256,384]{0,1:T(8,128)(2,1)S(1)} %convolution_convert_fusion.4), channel_id=1, source_target_pairs={{0,64},{32,96},{64,0},{96,32},{1,65},{33,97},{65,1},{97,33},{2,66}... | collective-permute-start | bytes 589832 | tf_op jit(solution)/shard_map/ppermute | solution.py:50
  201.6 7.8 %collective-permute-start.18 = (bf16[256,384]{0,1:T(8,128)(2,1)S(1)}, bf16[256,384]{0,1:T(8,128)(2,1)S(1)}, u32[]{:S(2)}, u32[]{:S(2)}) collective-permute-start(bf16[256,384]{0,1:T(8,128)(2,1)S(1)} %convolution_convert_fusion.4), channel_id=1, source_target_pairs={{0,96},{32,0},{64,32},{96,64},{1,97},{33,1},{65,33},{97,65},{2,98}... | collective-permute-start | bytes 589832 | tf_op jit(solution)/shard_map/ppermute | solution.py:50
  211.8 7.2 %copy-start.17 = (f32[256,1]{0,1:T(1,128)S(1)}, f32[256,1]{0,1:T(1,128)}, u32[]{:S(2)}) copy-start(f32[256,1]{0,1:T(1,128)} %copy-done.16) | copy-start | bytes 3076
  211.8 7.2 %copy-start.31 = (f32[256,1]{0,1:T(1,128)S(1)}, f32[256,1]{0,1:T(1,128)}, u32[]{:S(2)}) copy-start(f32[256,1]{0,1:T(1,128)} %get-tuple-element.42) | copy-start | bytes 3076
  212.8 28.5 %copy-start.13 = (bf16[8,1280]{1,0:T(8,128)(2,1)S(1)}, bf16[8,1280]{1,0:T(8,128)(2,1)}, u32[]{:S(2)}) copy-start(bf16[8,1280]{1,0:T(8,128)(2,1)} %copy-done.12) | copy-start | bytes 61444
  212.8 27.1 %all-to-all-start.4 = ((bf16[32,8,1408]{2,1,0:T(8,128)(2,1)}), bf16[32,8,1408]{2,1,0:T(8,128)(2,1)}, u32[]{:S(2)}, u32[]{:S(2)}) async-start(bf16[32,8,1408]{2,1,0:T(8,128)(2,1)} %fusion.32), calls=%async_computation.4 | async-start | bytes 1441792 | tf_op jit(solution)/shard_map/all_to_all | solution.py:45
  243.0 27.0 %copy-start.29 = (f32[1,1280]{1,0:T(1,128)S(1)}, f32[1,1280]{1,0:T(1,128)}, u32[]{:S(2)}) copy-start(f32[1,1280]{1,0:T(1,128)} %param.17) | copy-start | bytes 15364
  243.0 24.8 %all-to-all-start.5 = ((bf16[32,8,1280]{2,1,0:T(8,128)(2,1)}), bf16[32,8,1280]{2,1,0:T(8,128)(2,1)}, u32[]{:S(2)}, u32[]{:S(2)}) async-start(bf16[32,8,1280]{2,1,0:T(8,128)(2,1)} %broadcast_in_dim.14), calls=%async_computation.5 | async-start | bytes 1310720 | tf_op jit(solution)/shard_map/all_to_all | solution.py:39
  248.5 21.6 %collective-permute-start.5 = (bf16[256,1280]{1,0:T(8,128)(2,1)S(1)}, bf16[256,1280]{1,0:T(8,128)(2,1)}, u32[]{:S(2)}, u32[]{:S(2)}) collective-permute-start(bf16[256,1280]{1,0:T(8,128)(2,1)S(1)} %bitcast.97), channel_id=1, source_target_pairs={{0,128},{128,0},{1,129},{129,1},{2,130},{130,2},{3,131},{131,3},{4... | collective-permute-start | bytes 1966088 | tf_op jit(solution)/shard_map/ppermute | solution.py:110
  270.0 9.3 %collective-permute-start.19 = (bf16[256,1280]{1,0:T(8,128)(2,1)}, bf16[256,1280]{1,0:T(8,128)(2,1)}, u32[]{:S(2)}, u32[]{:S(2)}) collective-permute-start(bf16[256,1280]{1,0:T(8,128)(2,1)} %broadcast_select_fusion.2), channel_id=1, source_target_pairs={{0,128},{128,0},{1,129},{129,1},{2,130},{130,2},{3,131},{131,3},{4... | collective-permute-start | bytes 1966088 | tf_op jit(solution)/shard_map/ppermute | solution.py:110
  270.1 9.3 %copy-start.34 = (bf16[1,1024,1280]{2,1,0:T(8,128)(2,1)S(1)}, bf16[1,1024,1280]{2,1,0:T(8,128)(2,1)}, u32[]{:S(2)}) copy-start(bf16[1,1024,1280]{2,1,0:T(8,128)(2,1)} %param.16) | copy-start | bytes 7864324
  275.1 10.8 %collective-permute-start.6 = (bf16[128,1024]{1,0:T(8,128)(2,1)S(1)}, bf16[128,1024]{1,0:T(8,128)(2,1)S(1)}, u32[]{:S(2)}, u32[]{:S(2)}) collective-permute-start(bf16[128,1024]{1,0:T(8,128)(2,1)S(1)} %get-tuple-element.54), channel_id=1, source_target_pairs={{0,32},{32,64},{64,96},{96,0},{1,33},{33,65},{65,97},{97,1},{2,34}... | collective-permute-start | bytes 786440 | tf_op jit(solution)/shard_map/ppermute | solution.py:50
  275.1 27.0 %collective-permute-start.7 = (bf16[128,1024]{1,0:T(8,128)(2,1)}, bf16[128,1024]{1,0:T(8,128)(2,1)}, u32[]{:S(2)}, u32[]{:S(2)}) collective-permute-start(bf16[128,1024]{1,0:T(8,128)(2,1)} %get-tuple-element.56), channel_id=1, source_target_pairs={{0,64},{32,96},{64,0},{96,32},{1,65},{33,97},{65,1},{97,33},{2,66}... | collective-permute-start | bytes 786440 | tf_op jit(solution)/shard_map/ppermute | solution.py:50
  276.7 25.4 %collective-permute-start.8 = (bf16[128,1024]{1,0:T(8,128)(2,1)}, bf16[128,1024]{1,0:T(8,128)(2,1)}, u32[]{:S(2)}, u32[]{:S(2)}) collective-permute-start(bf16[128,1024]{1,0:T(8,128)(2,1)} %get-tuple-element.55), channel_id=1, source_target_pairs={{0,96},{32,0},{64,32},{96,64},{1,97},{33,1},{65,33},{97,65},{2,98}... | collective-permute-start | bytes 786440 | tf_op jit(solution)/shard_map/ppermute | solution.py:50
  282.4 6.8 %copy-start.7 = (bf16[512,1024]{1,0:T(8,128)(2,1)}, bf16[512,1024]{1,0:T(8,128)(2,1)S(1)}, u32[]{:S(2)}) copy-start(bf16[512,1024]{1,0:T(8,128)(2,1)S(1)} %fusion.12) | copy-start | bytes 3145732
  283.3 18.8 %collective-permute-start.20 = (bf16[128,1024]{1,0:T(8,128)(2,1)}, bf16[128,1024]{1,0:T(8,128)(2,1)}, u32[]{:S(2)}, u32[]{:S(2)}) collective-permute-start(bf16[128,1024]{1,0:T(8,128)(2,1)} %get-tuple-element.57), channel_id=1, source_target_pairs={{0,32},{32,64},{64,96},{96,0},{1,33},{33,65},{65,97},{97,1},{2,34}... | collective-permute-start | bytes 786440 | tf_op jit(solution)/shard_map/ppermute | solution.py:50
  283.3 18.8 %collective-permute-start.21 = (bf16[128,1024]{1,0:T(8,128)(2,1)}, bf16[128,1024]{1,0:T(8,128)(2,1)}, u32[]{:S(2)}, u32[]{:S(2)}) collective-permute-start(bf16[128,1024]{1,0:T(8,128)(2,1)} %get-tuple-element.59), channel_id=1, source_target_pairs={{0,64},{32,96},{64,0},{96,32},{1,65},{33,97},{65,1},{97,33},{2,66}... | collective-permute-start | bytes 786440 | tf_op jit(solution)/shard_map/ppermute | solution.py:50
  285.9 16.3 %copy-start.30 = (f32[1,1024]{1,0:T(1,128)S(1)}, f32[1,1024]{1,0:T(1,128)}, u32[]{:S(2)}) copy-start(f32[1,1024]{1,0:T(1,128)} %param.15) | copy-start | bytes 12292
  285.9 16.3 %collective-permute-start.22 = (bf16[128,1024]{1,0:T(8,128)(2,1)}, bf16[128,1024]{1,0:T(8,128)(2,1)}, u32[]{:S(2)}, u32[]{:S(2)}) collective-permute-start(bf16[128,1024]{1,0:T(8,128)(2,1)} %get-tuple-element.58), channel_id=1, source_target_pairs={{0,96},{32,0},{64,32},{96,64},{1,97},{33,1},{65,33},{97,65},{2,98}... | collective-permute-start | bytes 786440 | tf_op jit(solution)/shard_map/ppermute | solution.py:50
  289.8 12.3 %all-to-all-start.6 = ((f32[4,1,128]{2,1,0:T(1,128)}), f32[4,1,128]{2,1,0:T(1,128)S(1)}, u32[]{:S(2)}, u32[]{:S(2)}) async-start(f32[4,1,128]{2,1,0:T(1,128)} %bitcast.44), calls=%async_computation.6 | async-start | bytes 4096 | tf_op jit(solution)/shard_map/all_to_all | solution.py:244
  (21 other events, 51.4 us)

commit v2 on v1

--- a/solution.py
+++ b/solution.py
@@ -1,6 +1,8 @@
 import jax
 import jax.numpy as jnp
 from jax import lax
+from jax.experimental import pallas as pl
+from jax.experimental.pallas import tpu as pltpu
 from jax.sharding import PartitionSpec as P
 
 D = 5120
@@ -69,14 +71,82 @@
     return block(0).astype(F32) + sum(part.astype(F32) for part in parts)
 
 
-def pack_rows(values, width, rows):
-    terms = jnp.stack(split3(values.reshape(-1, width))).reshape(-1, width)
-    return jnp.pad(terms, ((0, rows - terms.shape[0]), (0, 0)))
-
-
-def unpack_rows(terms, count):
-    terms = terms[..., : 3 * count, :].astype(F32)
-    return terms[..., :count, :] + terms[..., count : 2 * count, :] + terms[..., 2 * count :, :]
+def start_kernel(
+    core_ref,
+    tokens_ref,
+    cot_ref,
+    in_w_ref,
+    out_w_ref,
+    gain_ref,
+    bias_ref,
+    in_bias_ref,
+    out_bias_ref,
+    gained_ref,
+    mine_ref,
+    send_ref,
+):
+    width, hid = in_w_ref.shape
+    half = tokens_ref.shape[0] // 2
+    gain = jnp.broadcast_to(gain_ref[...], (128, width)).T
+    for at in range(0, hid, 128):
+        columns = slice(at, at + 128)
+        gained_ref[:, columns] = (in_w_ref[:, columns].astype(F32) * gain).astype(BF16)
+    gained = gained_ref[...]
+    column_sum = dot(jnp.ones((16, width), BF16), gained)[:1]
+    terms = split3(bias_ref[...])
+    terms = jnp.concatenate([t.astype(F32) for t in terms] + [jnp.zeros((13, width), F32)], axis=0)
+    shift = jnp.sum(dot(terms.astype(BF16), in_w_ref[...]), axis=0, keepdims=True)
+    rows = [column_sum, shift, in_bias_ref[...]]
+    out_bias = out_bias_ref[...]
+    for at in range(0, width, hid):
+        piece = out_bias[:, at : at + hid]
+        if piece.shape[1] < hid:
+            piece = jnp.concatenate([piece, jnp.zeros((1, hid - piece.shape[1]), F32)], axis=1)
+        rows.append(piece)
+    rows.append(jnp.zeros((8 - len(rows), hid), F32))
+    high = jnp.concatenate(rows, axis=0)
+    packed = []
+    for term in split3(high):
+        packed.append(term.astype(F32))
+    packed.append(jnp.zeros((8, hid), F32))
+    packed = jnp.concatenate(packed, axis=0).astype(BF16)
+    mine_ref[half : half + 32, :] = packed
+    send_ref[half : half + 32, :] = packed
+
+    @pl.when(core_ref[0] == 0)
+    def _():
+        for start, target in ((0, mine_ref), (half, send_ref)):
+            rows = tokens_ref[start : start + half, :]
+            mean = jnp.sum(rows.astype(F32), axis=1, keepdims=True) / width
+            target[:half, :] = (dot(rows, gained) - mean * column_sum).astype(BF16)
+
+    @pl.when(core_ref[0] != 0)
+    def _():
+        for start, target in ((half, mine_ref), (0, send_ref)):
+            rows = cot_ref[start : start + half, :]
+            target[:half, :] = dot_t(rows, out_w_ref[...]).astype(BF16)
+
+
+def start_products(core, tokens, cotangent, in_w, out_w, gain, bias, in_bias, out_bias):
+    width, hid = in_w.shape
+    half = tokens.shape[0] // 2
+    part = jax.ShapeDtypeStruct((half + 32, hid), BF16)
+    return pl.pallas_call(
+        start_kernel,
+        out_shape=(jax.ShapeDtypeStruct((width, hid), BF16), part, part),
+        in_specs=[pl.BlockSpec(memory_space=pltpu.SMEM)]
+        + [pl.BlockSpec(memory_space=pltpu.VMEM)] * 8,
+        out_specs=(pl.BlockSpec(memory_space=pltpu.VMEM),) * 3,
+        compiler_params=pltpu.CompilerParams(vmem_limit_bytes=40 * 1024 * 1024),
+        cost_estimate=pl.CostEstimate(
+            flops=4 * half * width * hid, bytes_accessed=7_000_000, transcendentals=0
+        ),
+    )(core.reshape(1), tokens, cotangent, in_w, out_w, gain, bias, in_bias, out_bias)
+
+
+def unpack_vectors(part, half):
+    terms = part[..., half : half + 24, :].astype(F32)
+    return terms[..., :8, :] + terms[..., 8:16, :] + terms[..., 16:24, :]
 
 
 def on_device(
@@ -117,12 +187,6 @@
 
     in_w = in_weight[0]
     out_w = out_weight[0]
-    gained = (in_w.astype(F32) * ln_gain[0][:, None]).astype(BF16)
-    column_sum = jnp.sum(gained.astype(F32), axis=0)
-    shift_in = jnp.sum(in_w.astype(F32) * ln_bias[0][:, None], axis=0)
-    pad_bias = jnp.pad(out_bias[0], (0, -width % hid))
-    vector_count = 3 + pad_bias.shape[0] // hid
-    vectors = jnp.concatenate([column_sum, shift_in, in_bias[0], pad_bias])
 
     def row_parts(resid):
         resid_f = resid.astype(F32)
@@ -130,75 +194,66 @@
         centred = resid_f - local_mean[:, None]
         return local_mean, jnp.sum(centred * centred, axis=1)
 
-    def stat_columns(local_mean, square):
-        stats = jnp.stack(split3(local_mean) + split3(square), axis=1)
-        return jnp.pad(stats, ((0, 0), (0, 128 - stats.shape[1])))
+    def with_stats(part, local_mean, square):
+        stats = jnp.stack(split3(local_mean) + split3(square))
+        stats = stats.reshape(-1, hid)
+        return part + jnp.pad(stats, ((half + 24, 8 - stats.shape[0]), (0, 0)))
 
     def row_stats(parts):
         means, squares = [], []
-        for stats in parts:
-            stats = stats[:, :6].astype(F32)
-            means.append(stats[:, 0] + stats[:, 1] + stats[:, 2])
-            squares.append(stats[:, 3] + stats[:, 4] + stats[:, 5])
+        for part in parts:
+            count = 6 * half // hid
+            stats = part[half + 24 : half + 24 + count].reshape(6, half).astype(F32)
+            means.append(stats[0] + stats[1] + stats[2])
+            squares.append(stats[3] + stats[4] + stats[5])
         mean = sum(means) / dp_count
         aparts = [local_mean - mean for local_mean in means]
         variance = sum(squares) / D + sum(apart * apart for apart in aparts) / dp_count
         return mean, lax.rsqrt(variance + EPSILON), aparts
 
-    def pre_hidden(parts, aparts, inv, sums):
-        total = sum(part.astype(F32) for part in parts)
-        total = total + sum(apart[:, None] * s[None] for apart, s in zip(aparts, sums))
-        return total * inv[:, None]
-
+    gained, mine, send = start_products(
+        core, tokens, cotangent, in_w, out_w, ln_gain, ln_bias, in_bias, out_bias
+    )
+    there = other(send)
     tokens_half = lax.dynamic_slice_in_dim(tokens, core * half, half, 0)
     cot_half = lax.dynamic_slice_in_dim(cotangent, core * half, half, 0)
-    mean_all, square_all = row_parts(tokens)
-    forward_all = (dot(tokens, gained) - mean_all[:, None] * column_sum[None]).astype(BF16)
-    grad_all = dot_t(cotangent, out_w).astype(BF16)
-    packed = pack_rows(vectors, hid, 32)
-    there = other(jnp.concatenate([pick(forward_all[half:], grad_all[:half]), packed], axis=0))
-    part_0 = pick(forward_all[:half], there[:half])
-    grad_act_part = pick(there[:half], grad_all[half:])
-    vectors_there = unpack_rows(there[half:], vector_count)
-    vectors = vectors.reshape(-1, hid)
-    vectors_0 = pick(vectors, vectors_there)
-    vectors_1 = pick(vectors_there, vectors)
-
+    part_0 = with_stats(pick(mine, there), *row_parts(tokens_half))
+    part_grad = pick(there, mine)
+    vectors_0 = unpack_vectors(part_0, half)
+    vectors_1 = unpack_vectors(part_grad, half)
     gained_there = other(gained)
-    out_there = other(out_w)
     gained_0, gained_1 = pick(gained, gained_there), pick(gained_there, gained)
-    out_w0 = pick(out_w, out_there)
-
-    def gathered(part, stats, layer_vectors):
-        rows = pack_rows(layer_vectors[:2].reshape(-1), hid, 16)
-        payload = jnp.concatenate([part, rows], axis=0)
-        stats = jnp.pad(stats, ((0, 16), (0, 0)))
-        got = gather_ring(jnp.concatenate([payload, stats], axis=1), "dp")
-        mean, inv, aparts = row_stats([g[:half, hid:] for g in got])
-        dp_vectors = [unpack_rows(g[half:, :hid], 2) for g in got]
-        sums = [v[0] for v in dp_vectors]
-        pre = pre_hidden([g[:half, :hid] for g in got], aparts, inv, sums)
-        shift = sum(v[1] for v in dp_vectors) + layer_vectors[2]
+    out_w0 = pick(out_w, other(out_w))
+
+    def gathered(part, in_b):
+        got = gather_ring(part, "dp")
+        mean, inv, aparts = row_stats(got)
+        vectors = [unpack_vectors(g, half) for g in got]
+        sums = [v[0] for v in vectors]
+        total = sum(g[:half].astype(F32) for g in got)
+        total = total + sum(apart[:, None] * s[None] for apart, s in zip(aparts, sums))
+        pre = total * inv[:, None]
+        shift = sum(v[1] for v in vectors) + in_b
         return pre, pre + shift[None], mean, inv, sum(sums)
 
-    def half_of(values):
-        return lax.dynamic_slice_in_dim(values, core * half, half, 0)
-
-    stats_0 = stat_columns(half_of(mean_all), half_of(square_all))
-    pre_0, hidden_0, mean_0, inv_0, sums_0 = gathered(part_0, stats_0, vectors_0)
+    pre_0, hidden_0, mean_0, inv_0, sums_0 = gathered(part_0, vectors_0[2])
     act_0 = jax.nn.gelu(hidden_0, approximate=False).astype(BF16)
     mlp = exchange(dot(act_0, out_w0).astype(BF16), "latent")
     tokens_rows = own_rows(tokens_half).astype(F32)
-    bias_row = vectors_0[3:].reshape(-1)[:width]
+    bias_row = vectors_0[3:7].reshape(-1)[:width]
     resid_rows = (tokens_rows + jnp.sum(mlp.astype(F32), axis=0) + bias_row[None]).astype(BF16)
+    grad_act_1 = total_ring(part_grad[:half], "dp")
+    resid_rows, grad_act_1 = lax.optimization_barrier((resid_rows, grad_act_1))
     resid_half = spread(resid_rows, "latent").reshape(half, width)
 
     local_mean, square = row_parts(resid_half)
     part_1 = dot(resid_half, gained_1) - local_mean[:, None] * vectors_1[0][None]
+    part_1 = jnp.concatenate([part_1.astype(BF16), part_grad[half:]], axis=0)
+    resid_there = other(resid_half)
     pre_1, hidden_1, mean_1, inv_1, sums_1 = gathered(
-        part_1.astype(BF16), stat_columns(local_mean, square), vectors_1
-    )
-    grad_act_1 = total_ring(grad_act_part, "dp")
+        with_stats(part_1, local_mean, square), vectors_1[2]
+    )
+    hidden_1, resid_there = lax.optimization_barrier((hidden_1, resid_there))
 
     def backward(grad_act, hidden, pre, weight, sums, resid, mean, inv, grad_rows):
         grad_hidden = (grad_act * gelu_slope(hidden)).astype(BF16)
@@ -223,27 +278,33 @@
     grad_rows_1, grad_half_1 = backward(
         grad_act_1, hidden_1, pre_1, gained_1, sums_1, resid_rows.astype(F32), mean_1, inv_1, cot_rows
     )
+    resid_all = pick(tokens, jnp.concatenate([resid_there, resid_half], axis=0))
+    pre_codes = scatter_ring(dot(resid_all, enc_weight[0]).astype(BF16), "dp")
+    grad_half_1, pre_codes = lax.optimization_barrier((grad_half_1, pre_codes))
     grad_act_0 = total_ring(dot_t(grad_half_1, out_w0).astype(BF16), "dp")
     _, grad_half_0 = backward(
         grad_act_0, hidden_0, pre_0, gained_0, sums_0, tokens_rows, mean_0, inv_0,
         grad_rows_1.astype(F32),
     )
 
-    resid_all = pick(tokens, jnp.concatenate([other(resid_half), resid_half], axis=0))
-    pre_codes = scatter_ring(dot(resid_all, enc_weight[0]).astype(BF16), "dp")
     codes = jnp.maximum(pre_codes + enc_bias[0][None], 0.0).astype(BF16)
-
-    grad_there = other(pick(grad_half_1, grad_half_0))
-    grad_all = pick(
-        jnp.concatenate([grad_half_0, grad_there], axis=0),
-        jnp.concatenate([grad_there, grad_half_1], axis=0),
-    )
-    effect = codes.astype(F32) * scatter_ring(dot_t(grad_all, dec_weight[0]).astype(BF16), "dp")
-    error = (resid_all.astype(F32) - dec_bias[0][None]) * grad_all.astype(F32)
-    error = (jnp.sum(error, axis=1) / latent_count).reshape(dp_count, 1, block)
-    error = lax.all_to_all(error, "dp", 0, 0)
-    error = jnp.sum(error, axis=0) - jnp.sum(effect, axis=1)[None]
-    error = jnp.sum(spread(error, "latent"), axis=(0, 1))
+    resid_own = lax.dynamic_slice_in_dim(resid_all, core * half, half, 0)
+    resid_rest = lax.dynamic_slice_in_dim(resid_all, (1 - core) * half, half, 0)
+
+    def attributed(grad, resid):
+        error = (resid.astype(F32) - dec_bias[0][None]) * grad.astype(F32)
+        error = jnp.stack(split3(jnp.sum(error, axis=1) / latent_count), axis=1)
+        error = jnp.pad(error, ((0, 0), (0, 128 - error.shape[1])))
+        return jnp.concatenate([dot_t(grad, dec_weight[0]).astype(BF16), error], axis=1)
+
+    rest = attributed(other(pick(grad_half_1, grad_half_0)), resid_rest)
+    own = attributed(pick(grad_half_0, grad_half_1), resid_own)
+    parts = pick(jnp.concatenate([own, rest], axis=0), jnp.concatenate([rest, own], axis=0))
+    summed = scatter_ring(parts, "dp")
+    latents = codes.shape[1]
+    effect = codes.astype(F32) * summed[:, :latents]
+    error = jnp.sum(summed[:, latents : latents + 3], axis=1) - jnp.sum(effect, axis=1)
+    error = jnp.sum(spread(error[None], "latent"), axis=(0, 1))
     return effect.astype(BF16)[None], error[None]
 
 

time: 321 us -> 290 us (0.903)
  waiting for transfers between devices: 144 us -> 110 us
  blocking collectives: 38.5 us -> 34.8 us
    all_to_all x3, waiting for transfers between devices: 60.6 us -> 41.9 us  [exchange(): lax.all_to_all(values.reshape(count, rows, values.shape[1]), axis, 0, 0)]
    all_to_all x2, waiting for transfers between devices: 34.4 us -> 18.5 us  [spread(): return lax.all_to_all(copies, axis, 0, 0)]
    unnamed x80 -> x60, local copies, waits for them, and re-layouts: 3.13 us -> 12.4 us
    ppermute x18, waiting for transfers between devices: 41.3 us -> 49.4 us  [turn(): lax.ppermute(values, axis, [(i, (i + by) % count) for i in range(count)])]
    all_to_all x1 -> x0, waiting for transfers between devices: 7.76 us -> none  [on_device(): error = lax.all_to_all(error, 'dp', 0, 0)]
    convert_element_type x17 -> x19, other arithmetic: 1.05 us -> 7.2 us  [the longest x9 3.7 us: unpack_vectors(): terms = part[..., half:half + 24, :].astype(F32)]
    reduce_sum x5 -> x4, other arithmetic: 8.2 us -> 3.12 us  [the longest x1 1.71 us: attributed(): error = jnp.stack(split3(jnp.sum(error, axis=1) / latent_count), axis=1)]
    add x8 -> x19, other arithmetic: 1.32 us -> 6.18 us  [the longest x2 2.28 us: scatter_ring(): return block(0).astype(F32) + sum((part.astype(F32) for part in parts))]
  transfers between devices with their start and end apart: 29 -> 28, of which waited for: 15 -> 19; matrix products, arithmetic and copies ran while one was open for 8% -> 11% of each run, Pallas kernels for 0% -> 1%
where the time goes in v2:
time: 290 us; the launch traced here: 287 us
  waiting for transfers between devices  110 us (38%)
  starting transfers between devices  66.8 us (23%)
  other arithmetic  37.4 us (13%)
  blocking collectives  34.8 us (12%)
  matrix products  18.5 us (6%)
  local copies, waits for them, and re-layouts  16.6 us (6%)
    ppermute x18, waiting for transfers between devices, turn(): lax.ppermute(values, axis, [(i, (i + by) % count) for i in range(count)])  49.4 us
    all_to_all x3, waiting for transfers between devices, exchange(): lax.all_to_all(values.reshape(count, rows, values.shape[1]), axis, 0, 0)  41.9 us
    all_to_all x2, blocking collectives, spread(): return lax.all_to_all(copies, axis, 0, 0)  34.8 us
    ppermute x18, starting transfers between devices, turn(): lax.ppermute(values, axis, [(i, (i + by) % count) for i in range(count)])  29.4 us
    all_to_all x3, starting transfers between devices, exchange(): lax.all_to_all(values.reshape(count, rows, values.shape[1]), axis, 0, 0)  26.4 us
    all_to_all x2, waiting for transfers between devices, spread(): return lax.all_to_all(copies, axis, 0, 0)  18.5 us
    unnamed x60, local copies, waits for them, and re-layouts  12.4 us
    dot_general x5, matrix products, dot_t(): lax.dot_general(left, right, CONTRACT_LAST, preferred_element_type=F32)  11.9 us
  transfers between devices with their start and end apart: 28, of which 19 were waited for; matrix products, arithmetic and copies ran while one was open for 11% of the time, Pallas kernels for 1%

profile of v2, /device:TPU:8, one launch (start us, length us, event | category | flops | bytes accessed | tf_op | source)
XLA Modules:
  0.0 286.8 jit_solution(14499559631091428640)
XLA Ops:
  8.7 1.5 shard_map.131
  16.0 2.2 collective-permute-start.3
  19.1 1.9 collective-permute-start.1
  21.0 3.0 %collective-permute-done.3 = bf16[288,384]{1,0:T(8,128)(2,1)S(1)} collective-permute-done((bf16[288,384]{1,0:T(8,128)(2,1)S(1)}, bf16[288,384]{1,0:T(8,128)(2,1)S(1)}, u32[]{:S(2)}, u32[]{:S(2)}) %collective-permute-start.3) | collective-permute-done | bytes 221216 | tf_op jit(solution)/shard_map/ppermute | solution.py:52
  24.0 5.4 %collective-permute-done.2 = bf16[288,384]{1,0:T(8,128)(2,1)} collective-permute-done((bf16[288,384]{1,0:T(8,128)(2,1)S(1)}, bf16[288,384]{1,0:T(8,128)(2,1)}, u32[]{:S(2)}, u32[]{:S(2)}) %collective-permute-start.2) | collective-permute-done | bytes 221216 | tf_op jit(solution)/shard_map/ppermute | solution.py:52
  35.7 3.3 %fusion.6 = bf16[32,8,1280]{2,1,0:T(8,128)(2,1)} fusion(bf16[384,1280]{1,0:T(8,128)(2,1)} %collective-permute-done.4, pred[]{:T(512)S(6)} %eq.12, f32[256,384]{1,0:T(8,128)S(1)} %add_multiply_fusion.1, f32[384]{0:T(512)S(1)} %get-tuple-element.27, bf16[1,384,1280]{2,1,0:T(8,128)(2,1)} %param.22), kind=kOutput, calls=%fused_computation.9 | convolution fusion | flops 258965504 | bytes 3016193 | tf_op jit(solution)/shard_map/dot_general | solution.py:31
  39.0 11.3 %all-to-all-start = ((bf16[32,8,1280]{2,1,0:T(8,128)(2,1)}), bf16[32,8,1280]{2,1,0:T(8,128)(2,1)S(1)}, u32[]{:S(2)}, u32[]{:S(2)}) async-start(bf16[32,8,1280]{2,1,0:T(8,128)(2,1)} %fusion.6), calls=%async_computation | async-start | bytes 1310720 | tf_op jit(solution)/shard_map/all_to_all | solution.py:47
  51.1 2.3 collective-permute-start.6
  53.4 2.0 collective-permute-start.5
  55.5 5.0 %collective-permute-done.6 = bf16[256,384]{1,0:T(8,128)(2,1)} collective-permute-done((bf16[256,384]{1,0:T(8,128)(2,1)}, bf16[256,384]{1,0:T(8,128)(2,1)}, u32[]{:S(2)}, u32[]{:S(2)}) %collective-permute-start.6) | collective-permute-done | bytes 196640 | tf_op jit(solution)/shard_map/ppermute | solution.py:52
  60.4 3.5 %collective-permute-done.5 = bf16[256,384]{1,0:T(8,128)(2,1)} collective-permute-done((bf16[256,384]{1,0:T(8,128)(2,1)}, bf16[256,384]{1,0:T(8,128)(2,1)}, u32[]{:S(2)}, u32[]{:S(2)}) %collective-permute-start.5) | collective-permute-done | bytes 196640 | tf_op jit(solution)/shard_map/ppermute | solution.py:52
  63.9 2.0 convert_add_fusion
  65.9 4.3 %all-to-all-done = bf16[32,8,1280]{2,1,0:T(8,128)(2,1)S(1)} async-done(((bf16[32,8,1280]{2,1,0:T(8,128)(2,1)}), bf16[32,8,1280]{2,1,0:T(8,128)(2,1)S(1)}, u32[]{:S(2)}, u32[]{:S(2)}) %all-to-all-start) | async-done | bytes 655392 | tf_op jit(solution)/shard_map/all_to_all | solution.py:47
  72.6 5.2 %all-to-all-start.1 = ((bf16[32,8,1280]{2,1,0:T(8,128)(2,1)}), bf16[32,8,1280]{2,1,0:T(8,128)(2,1)S(1)}, u32[]{:S(2)}, u32[]{:S(2)}) async-start(bf16[32,8,1280]{2,1,0:T(8,128)(2,1)} %broadcast_in_dim.12), calls=%async_computation.1 | async-start | bytes 1310720 | tf_op jit(solution)/shard_map/all_to_all | solution.py:41
  78.7 18.5 %all-to-all-done.1 = bf16[32,8,1280]{2,1,0:T(8,128)(2,1)S(1)} async-done(((bf16[32,8,1280]{2,1,0:T(8,128)(2,1)}), bf16[32,8,1280]{2,1,0:T(8,128)(2,1)S(1)}, u32[]{:S(2)}, u32[]{:S(2)}) %all-to-all-start.1) | async-done | bytes 655392 | tf_op jit(solution)/shard_map/all_to_all | solution.py:41
  98.1 1.7 fusion.22
  99.8 3.9 %collective-permute-start.11 = (bf16[288,384]{1,0:T(8,128)(2,1)S(1)}, bf16[288,384]{1,0:T(8,128)(2,1)}, u32[]{:S(2)}, u32[]{:S(2)}) collective-permute-start(bf16[288,384]{1,0:T(8,128)(2,1)S(1)} %maximum_add_fusion), channel_id=1, source_target_pairs={{0,96},{32,0},{64,32},{96,64},{1,97},{33,1},{65,33},{97,65},{2,98}... | collective-permute-start | bytes 663560 | tf_op jit(solution)/shard_map/ppermute | solution.py:52
  103.8 1.5 collective-permute-start.9
  105.9 2.4 collective-permute-done.11
  110.4 1.7 collective-permute-done.10
  119.2 1.8 convolution_convert_fusion.1
  121.9 5.8 %all-to-all-start.2 = ((bf16[32,8,1408]{2,1,0:T(8,128)(2,1)}), bf16[32,8,1408]{2,1,0:T(8,128)(2,1)}, u32[]{:S(2)}, u32[]{:S(2)}) async-start(bf16[32,8,1408]{2,1,0:T(8,128)(2,1)} %fusion.26), calls=%async_computation.2 | async-start | bytes 1441792 | tf_op jit(solution)/shard_map/all_to_all | solution.py:47
  127.9 20.2 %all-to-all-done.2 = bf16[32,8,1408]{2,1,0:T(8,128)(2,1)} async-done(((bf16[32,8,1408]{2,1,0:T(8,128)(2,1)}), bf16[32,8,1408]{2,1,0:T(8,128)(2,1)}, u32[]{:S(2)}, u32[]{:S(2)}) %all-to-all-start.2) | async-done | bytes 720928 | tf_op jit(solution)/shard_map/all_to_all | solution.py:47
  151.4 5.1 %all-to-all-start.3 = ((bf16[32,8,1280]{2,1,0:T(8,128)(2,1)}), bf16[32,8,1280]{2,1,0:T(8,128)(2,1)}, u32[]{:S(2)}, u32[]{:S(2)}) async-start(bf16[32,8,1280]{2,1,0:T(8,128)(2,1)} %broadcast_in_dim.13), calls=%async_computation.3 | async-start | bytes 1310720 | tf_op jit(solution)/shard_map/all_to_all | solution.py:41
  156.5 1.8 maximum_select_fusion
  158.3 1.6 fusion.7
  160.8 1.5 collective-permute-start.13
  163.8 2.4 collective-permute-start.14
  166.2 4.9 %collective-permute-done.13 = bf16[128,1024]{1,0:T(8,128)(2,1)} collective-permute-done((bf16[128,1024]{1,0:T(8,128)(2,1)S(1)}, bf16[128,1024]{1,0:T(8,128)(2,1)}, u32[]{:S(2)}, u32[]{:S(2)}) %collective-permute-start.13) | collective-permute-done | bytes 262176 | tf_op jit(solution)/shard_map/ppermute | solution.py:52
  171.1 4.9 %collective-permute-done.14 = bf16[128,1024]{1,0:T(8,128)(2,1)} collective-permute-done((bf16[128,1024]{1,0:T(8,128)(2,1)S(1)}, bf16[128,1024]{1,0:T(8,128)(2,1)}, u32[]{:S(2)}, u32[]{:S(2)}) %collective-permute-start.14) | collective-permute-done | bytes 262176 | tf_op jit(solution)/shard_map/ppermute | solution.py:52
  176.0 2.1 add_add_fusion.1
  178.1 2.0 convolution_convert_fusion.3
  181.4 1.9 collective-permute-start.17
  183.3 2.5 collective-permute-start.16
  187.1 2.1 collective-permute-done.17
  190.9 1.8 convolution_convert_fusion
  193.7 9.2 %all-to-all-start.4 = ((bf16[32,8,1408]{2,1,0:T(8,128)(2,1)}), bf16[32,8,1408]{2,1,0:T(8,128)(2,1)S(1)}, u32[]{:S(2)}, u32[]{:S(2)}) async-start(bf16[32,8,1408]{2,1,0:T(8,128)(2,1)} %fusion.28), calls=%async_computation.4 | async-start | bytes 1441792 | tf_op jit(solution)/shard_map/all_to_all | solution.py:47
  203.1 17.3 %all-to-all-done.4 = bf16[32,8,1408]{2,1,0:T(8,128)(2,1)S(1)} async-done(((bf16[32,8,1408]{2,1,0:T(8,128)(2,1)}), bf16[32,8,1408]{2,1,0:T(8,128)(2,1)S(1)}, u32[]{:S(2)}, u32[]{:S(2)}) %all-to-all-start.4) | async-done | bytes 720928 | tf_op jit(solution)/shard_map/all_to_all | solution.py:47
  221.6 20.8 %all_to_all.35 = bf16[32,8,1280]{2,1,0:T(8,128)(2,1)S(1)} all-to-all(bf16[32,8,1280]{2,1,0:T(8,128)(2,1)S(1)} %broadcast_in_dim.14), channel_id=1, replica_groups=mesh['section'=2,'dp'=4,'latent'=32] {'latent'}, dimensions={0} | all-to-all | bytes 1310720 | tf_op jit(solution)/shard_map/all_to_all | solution.py:41
  242.4 2.0 bitcast_select_fusion
  244.4 3.5 %fusion.16 = bf16[256,1024]{1,0:T(8,128)(2,1)} fusion(bf16[1,1024,1280]{2,1,0:T(8,128)(2,1)} %param.16, bf16[256,1280]{1,0:T(8,128)(2,1)} %bitcast.20, bf16[32,8,1280]{2,1,0:T(8,128)(2,1)S(1)} %all_to_all.35, pred[]{:T(512)S(6)} %eq.12), kind=kOutput, calls=%fused_computation.28 | convolution fusion | flops 671678464 | bytes 4456449 | tf_op jit(solution)/shard_map/dot_general | solution.py:35
  247.9 1.7 multiply_reduce_fusion.1
  250.1 2.9 fusion.19
  253.6 1.5 collective-permute-start.20
  255.7 1.5 collective-permute-start.21
  257.2 6.4 %collective-permute-done.20 = bf16[128,1152]{1,0:T(8,128)(2,1)S(1)} collective-permute-done((bf16[128,1152]{1,0:T(8,128)(2,1)S(1)}, bf16[128,1152]{1,0:T(8,128)(2,1)S(1)}, u32[]{:S(2)}, u32[]{:S(2)}) %collective-permute-start.20) | collective-permute-done | bytes 294944 | tf_op jit(solution)/shard_map/ppermute | solution.py:52
  264.7 6.5 %collective-permute-done.21 = bf16[128,1152]{1,0:T(8,128)(2,1)S(1)} collective-permute-done((bf16[128,1152]{1,0:T(8,128)(2,1)S(1)}, bf16[128,1152]{1,0:T(8,128)(2,1)S(1)}, u32[]{:S(2)}, u32[]{:S(2)}) %collective-permute-start.21) | collective-permute-done | bytes 294944 | tf_op jit(solution)/shard_map/ppermute | solution.py:52
  272.2 14.0 %all_to_all.36 = f32[32,1,128]{2,1,0:T(1,128)S(1)} all-to-all(f32[32,1,128]{2,1,0:T(1,128)S(1)} %broadcast_in_dim.16), channel_id=1, replica_groups=mesh['section'=2,'dp'=4,'latent'=32] {'latent'}, dimensions={0} | all-to-all | bytes 32768 | tf_op jit(solution)/shard_map/all_to_all | solution.py:41
  (210 shorter events, 53.0 us)
Async XLA Ops:
  0.6 157.6 %copy-start = (bf16[1,1280,1024]{2,1,0:T(8,128)(2,1)S(1)}, bf16[1,1280,1024]{2,1,0:T(8,128)(2,1)}, u32[]{:S(2)}) copy-start(bf16[1,1280,1024]{2,1,0:T(8,128)(2,1)} %param.14) | copy-start | bytes 7864324
  0.6 34.3 %collective-permute-start.4 = (bf16[384,1280]{1,0:T(8,128)(2,1)}, bf16[384,1280]{1,0:T(8,128)(2,1)}, u32[]{:S(2)}, u32[]{:S(2)}) collective-permute-start(bf16[384,1280]{1,0:T(8,128)(2,1)} %bitcast.71), channel_id=1, source_target_pairs={{0,128},{128,0},{1,129},{129,1},{2,130},{130,2},{3,131},{131,3},{4... | collective-permute-start | bytes 2949128 | tf_op jit(solution)/shard_map/ppermute | solution.py:180
  0.8 1.5 copy-start.1
  2.2 1.3 copy-start.3
  3.5 1.2 copy-start.4
  4.7 1.2 copy-start.5
  11.2 3.1 %collective-permute-start = (bf16[288,384]{1,0:T(8,128)(2,1)S(1)}, bf16[288,384]{1,0:T(8,128)(2,1)S(1)}, u32[]{:S(2)}, u32[]{:S(2)}) collective-permute-start(bf16[288,384]{1,0:T(8,128)(2,1)S(1)} %get-tuple-element.12), channel_id=1, source_target_pairs={{0,128},{128,0},{1,129},{129,1},{2,130},{130,2},{3,131},{131,3},{4... | collective-permute-start | bytes 663560 | tf_op jit(solution)/shard_map/ppermute | solution.py:180
  16.0 8.0 %collective-permute-start.3 = (bf16[288,384]{1,0:T(8,128)(2,1)S(1)}, bf16[288,384]{1,0:T(8,128)(2,1)S(1)}, u32[]{:S(2)}, u32[]{:S(2)}) collective-permute-start(bf16[288,384]{1,0:T(8,128)(2,1)S(1)} %get-tuple-element.67), channel_id=1, source_target_pairs={{0,96},{32,0},{64,32},{96,64},{1,97},{33,1},{65,33},{97,65},{2,98}... | collective-permute-start | bytes 663560 | tf_op jit(solution)/shard_map/ppermute | solution.py:52
  18.2 11.2 %collective-permute-start.2 = (bf16[288,384]{1,0:T(8,128)(2,1)S(1)}, bf16[288,384]{1,0:T(8,128)(2,1)}, u32[]{:S(2)}, u32[]{:S(2)}) collective-permute-start(bf16[288,384]{1,0:T(8,128)(2,1)S(1)} %get-tuple-element.67), channel_id=1, source_target_pairs={{0,64},{32,96},{64,0},{96,32},{1,65},{33,97},{65,1},{97,33},{2,66}... | collective-permute-start | bytes 663560 | tf_op jit(solution)/shard_map/ppermute | solution.py:52
  19.1 11.1 %collective-permute-start.1 = (bf16[288,384]{1,0:T(8,128)(2,1)S(1)}, bf16[288,384]{1,0:T(8,128)(2,1)}, u32[]{:S(2)}, u32[]{:S(2)}) collective-permute-start(bf16[288,384]{1,0:T(8,128)(2,1)S(1)} %get-tuple-element.67), channel_id=1, source_target_pairs={{0,32},{32,64},{64,96},{96,0},{1,33},{33,65},{65,97},{97,1},{2,34}... | collective-permute-start | bytes 663560 | tf_op jit(solution)/shard_map/ppermute | solution.py:52
  33.0 6.0 %copy-start.23 = (f32[384]{0:T(512)}, f32[384]{0:T(512)S(1)}, u32[]{:S(2)}) copy-start(f32[384]{0:T(512)S(1)} %get-tuple-element.27) | copy-start | bytes 4612
  33.7 5.4 %copy-start.27 = (f32[256]{0:T(256)}, f32[256]{0:T(256)S(1)}, u32[]{:S(2)}) copy-start(f32[256]{0:T(256)S(1)} %get-tuple-element.52) | copy-start | bytes 3076
  39.0 31.2 %all-to-all-start = ((bf16[32,8,1280]{2,1,0:T(8,128)(2,1)}), bf16[32,8,1280]{2,1,0:T(8,128)(2,1)S(1)}, u32[]{:S(2)}, u32[]{:S(2)}) async-start(bf16[32,8,1280]{2,1,0:T(8,128)(2,1)} %fusion.6), calls=%async_computation | async-start | bytes 1310720 | tf_op jit(solution)/shard_map/all_to_all | solution.py:47
  51.1 9.3 %collective-permute-start.6 = (bf16[256,384]{1,0:T(8,128)(2,1)}, bf16[256,384]{1,0:T(8,128)(2,1)}, u32[]{:S(2)}, u32[]{:S(2)}) collective-permute-start(bf16[256,384]{1,0:T(8,128)(2,1)} %slice.627), channel_id=1, source_target_pairs={{0,64},{32,96},{64,0},{96,32},{1,65},{33,97},{65,1},{97,33},{2,66}... | collective-permute-start | bytes 589832 | tf_op jit(solution)/shard_map/ppermute | solution.py:52
  53.4 10.5 %collective-permute-start.5 = (bf16[256,384]{1,0:T(8,128)(2,1)}, bf16[256,384]{1,0:T(8,128)(2,1)}, u32[]{:S(2)}, u32[]{:S(2)}) collective-permute-start(bf16[256,384]{1,0:T(8,128)(2,1)} %slice.627), channel_id=1, source_target_pairs={{0,32},{32,64},{64,96},{96,0},{1,33},{33,65},{65,97},{97,1},{2,34}... | collective-permute-start | bytes 589832 | tf_op jit(solution)/shard_map/ppermute | solution.py:52
  55.4 8.6 %collective-permute-start.7 = (bf16[256,384]{1,0:T(8,128)(2,1)}, bf16[256,384]{1,0:T(8,128)(2,1)}, u32[]{:S(2)}, u32[]{:S(2)}) collective-permute-start(bf16[256,384]{1,0:T(8,128)(2,1)} %slice.627), channel_id=1, source_target_pairs={{0,96},{32,0},{64,32},{96,64},{1,97},{33,1},{65,33},{97,65},{2,98}... | collective-permute-start | bytes 589832 | tf_op jit(solution)/shard_map/ppermute | solution.py:52
  72.6 24.6 %all-to-all-start.1 = ((bf16[32,8,1280]{2,1,0:T(8,128)(2,1)}), bf16[32,8,1280]{2,1,0:T(8,128)(2,1)S(1)}, u32[]{:S(2)}, u32[]{:S(2)}) async-start(bf16[32,8,1280]{2,1,0:T(8,128)(2,1)} %broadcast_in_dim.12), calls=%async_computation.1 | async-start | bytes 1310720 | tf_op jit(solution)/shard_map/all_to_all | solution.py:41
  77.8 20.3 %collective-permute-start.8 = (bf16[1280,384]{1,0:T(8,128)(2,1)}, bf16[1280,384]{1,0:T(8,128)(2,1)}, u32[]{:S(2)}, u32[]{:S(2)}) collective-permute-start(bf16[1280,384]{1,0:T(8,128)(2,1)} %copy-done.2), channel_id=1, source_target_pairs={{0,128},{128,0},{1,129},{129,1},{2,130},{130,2},{3,131},{131,3},{4... | collective-permute-start | bytes 2949128 | tf_op jit(solution)/shard_map/ppermute | solution.py:180
  99.8 8.5 %collective-permute-start.11 = (bf16[288,384]{1,0:T(8,128)(2,1)S(1)}, bf16[288,384]{1,0:T(8,128)(2,1)}, u32[]{:S(2)}, u32[]{:S(2)}) collective-permute-start(bf16[288,384]{1,0:T(8,128)(2,1)S(1)} %maximum_add_fusion), channel_id=1, source_target_pairs={{0,96},{32,0},{64,32},{96,64},{1,97},{33,1},{65,33},{97,65},{2,98}... | collective-permute-start | bytes 663560 | tf_op jit(solution)/shard_map/ppermute | solution.py:52
  103.7 8.4 %collective-permute-start.10 = (bf16[288,384]{1,0:T(8,128)(2,1)S(1)}, bf16[288,384]{1,0:T(8,128)(2,1)}, u32[]{:S(2)}, u32[]{:S(2)}) collective-permute-start(bf16[288,384]{1,0:T(8,128)(2,1)S(1)} %maximum_add_fusion), channel_id=1, source_target_pairs={{0,64},{32,96},{64,0},{96,32},{1,65},{33,97},{65,1},{97,33},{2,66}... | collective-permute-start | bytes 663560 | tf_op jit(solution)/shard_map/ppermute | solution.py:52
  103.8 10.4 %collective-permute-start.9 = (bf16[288,384]{1,0:T(8,128)(2,1)S(1)}, bf16[288,384]{1,0:T(8,128)(2,1)}, u32[]{:S(2)}, u32[]{:S(2)}) collective-permute-start(bf16[288,384]{1,0:T(8,128)(2,1)S(1)} %maximum_add_fusion), channel_id=1, source_target_pairs={{0,32},{32,64},{64,96},{96,0},{1,33},{33,65},{65,97},{97,1},{2,34}... | collective-permute-start | bytes 663560 | tf_op jit(solution)/shard_map/ppermute | solution.py:52
  105.3 13.3 %collective-permute-start.12 = (bf16[256,1280]{1,0:T(8,128)(2,1)S(1)}, bf16[256,1280]{1,0:T(8,128)(2,1)}, u32[]{:S(2)}, u32[]{:S(2)}) collective-permute-start(bf16[256,1280]{1,0:T(8,128)(2,1)S(1)} %bitcast.73), channel_id=1, source_target_pairs={{0,128},{128,0},{1,129},{129,1},{2,130},{130,2},{3,131},{131,3},{4... | collective-permute-start | bytes 1966088 | tf_op jit(solution)/shard_map/ppermute | solution.py:180
  114.9 3.8 %copy-start.15 = (f32[256,384]{1,0:T(8,128)S(1)}, f32[256,384]{1,0:T(8,128)}, u32[]{:S(2)}) copy-start(f32[256,384]{1,0:T(8,128)} %convert_add_fusion) | copy-start | bytes 1179652
  121.9 27.7 %copy-start.20 = (bf16[8,1280]{1,0:T(8,128)(2,1)S(1)}, bf16[8,1280]{1,0:T(8,128)(2,1)}, u32[]{:S(2)}) copy-start(bf16[8,1280]{1,0:T(8,128)(2,1)} %copy-done.19) | copy-start | bytes 61444
  121.9 26.3 %all-to-all-start.2 = ((bf16[32,8,1408]{2,1,0:T(8,128)(2,1)}), bf16[32,8,1408]{2,1,0:T(8,128)(2,1)}, u32[]{:S(2)}, u32[]{:S(2)}) async-start(bf16[32,8,1408]{2,1,0:T(8,128)(2,1)} %fusion.26), calls=%async_computation.2 | async-start | bytes 1441792 | tf_op jit(solution)/shard_map/all_to_all | solution.py:47
  151.4 26.8 %all-to-all-start.3 = ((bf16[32,8,1280]{2,1,0:T(8,128)(2,1)}), bf16[32,8,1280]{2,1,0:T(8,128)(2,1)}, u32[]{:S(2)}, u32[]{:S(2)}) async-start(bf16[32,8,1280]{2,1,0:T(8,128)(2,1)} %broadcast_in_dim.13), calls=%async_computation.3 | async-start | bytes 1310720 | tf_op jit(solution)/shard_map/all_to_all | solution.py:41
  158.3 1.6 copy-start.10
  160.8 10.3 %collective-permute-start.13 = (bf16[128,1024]{1,0:T(8,128)(2,1)S(1)}, bf16[128,1024]{1,0:T(8,128)(2,1)}, u32[]{:S(2)}, u32[]{:S(2)}) collective-permute-start(bf16[128,1024]{1,0:T(8,128)(2,1)S(1)} %get-tuple-element.63), channel_id=1, source_target_pairs={{0,32},{32,64},{64,96},{96,0},{1,33},{33,65},{65,97},{97,1},{2,34}... | collective-permute-start | bytes 786440 | tf_op jit(solution)/shard_map/ppermute | solution.py:52
  162.3 8.8 %collective-permute-start.15 = (bf16[128,1024]{1,0:T(8,128)(2,1)S(1)}, bf16[128,1024]{1,0:T(8,128)(2,1)}, u32[]{:S(2)}, u32[]{:S(2)}) collective-permute-start(bf16[128,1024]{1,0:T(8,128)(2,1)S(1)} %get-tuple-element.64), channel_id=1, source_target_pairs={{0,96},{32,0},{64,32},{96,64},{1,97},{33,1},{65,33},{97,65},{2,98}... | collective-permute-start | bytes 786440 | tf_op jit(solution)/shard_map/ppermute | solution.py:52
  163.8 12.2 %collective-permute-start.14 = (bf16[128,1024]{1,0:T(8,128)(2,1)S(1)}, bf16[128,1024]{1,0:T(8,128)(2,1)}, u32[]{:S(2)}, u32[]{:S(2)}) collective-permute-start(bf16[128,1024]{1,0:T(8,128)(2,1)S(1)} %get-tuple-element.65), channel_id=1, source_target_pairs={{0,64},{32,96},{64,0},{96,32},{1,65},{33,97},{65,1},{97,33},{2,66}... | collective-permute-start | bytes 786440 | tf_op jit(solution)/shard_map/ppermute | solution.py:52
  178.1 12.1 %copy-start.14 = (f32[256,384]{1,0:T(8,128)S(1)}, f32[256,384]{1,0:T(8,128)}, u32[]{:S(2)}) copy-start(f32[256,384]{1,0:T(8,128)} %copy-done.13) | copy-start | bytes 1179652
  178.1 12.1 %copy-start.22 = (f32[384]{0:T(512)S(1)}, f32[384]{0:T(512)}, u32[]{:S(2)}) copy-start(f32[384]{0:T(512)} %get-tuple-element.26) | copy-start | bytes 4612
  178.1 12.1 %copy-start.24 = (f32[384]{0:T(512)S(1)}, f32[384]{0:T(512)}, u32[]{:S(2)}) copy-start(f32[384]{0:T(512)} %copy-done.23) | copy-start | bytes 4612
  180.1 7.0 %collective-permute-start.18 = (bf16[256,384]{1,0:T(8,128)(2,1)S(1)}, bf16[256,384]{1,0:T(8,128)(2,1)S(1)}, u32[]{:S(2)}, u32[]{:S(2)}) collective-permute-start(bf16[256,384]{1,0:T(8,128)(2,1)S(1)} %convolution_convert_fusion.3), channel_id=1, source_target_pairs={{0,96},{32,0},{64,32},{96,64},{1,97},{33,1},{65,33},{97,65},{2,98}... | collective-permute-start | bytes 589832 | tf_op jit(solution)/shard_map/ppermute | solution.py:52
  181.4 7.8 %collective-permute-start.17 = (bf16[256,384]{1,0:T(8,128)(2,1)S(1)}, bf16[256,384]{1,0:T(8,128)(2,1)S(1)}, u32[]{:S(2)}, u32[]{:S(2)}) collective-permute-start(bf16[256,384]{1,0:T(8,128)(2,1)S(1)} %convolution_convert_fusion.3), channel_id=1, source_target_pairs={{0,64},{32,96},{64,0},{96,32},{1,65},{33,97},{65,1},{97,33},{2,66}... | collective-permute-start | bytes 589832 | tf_op jit(solution)/shard_map/ppermute | solution.py:52
  183.3 7.0 %collective-permute-start.16 = (bf16[256,384]{1,0:T(8,128)(2,1)S(1)}, bf16[256,384]{1,0:T(8,128)(2,1)S(1)}, u32[]{:S(2)}, u32[]{:S(2)}) collective-permute-start(bf16[256,384]{1,0:T(8,128)(2,1)S(1)} %convolution_convert_fusion.3), channel_id=1, source_target_pairs={{0,32},{32,64},{64,96},{96,0},{1,33},{33,65},{65,97},{97,1},{2,34}... | collective-permute-start | bytes 589832 | tf_op jit(solution)/shard_map/ppermute | solution.py:52
  192.7 10.2 %copy-start.28 = (f32[256]{0:T(256)S(1)}, f32[256]{0:T(256)}, u32[]{:S(2)}) copy-start(f32[256]{0:T(256)} %copy-done.27) | copy-start | bytes 3076
  192.7 10.3 %copy-start.29 = (f32[256]{0:T(256)S(1)}, f32[256]{0:T(256)}, u32[]{:S(2)}) copy-start(f32[256]{0:T(256)} %get-tuple-element.57) | copy-start | bytes 3076
  193.7 26.7 %all-to-all-start.4 = ((bf16[32,8,1408]{2,1,0:T(8,128)(2,1)}), bf16[32,8,1408]{2,1,0:T(8,128)(2,1)S(1)}, u32[]{:S(2)}, u32[]{:S(2)}) async-start(bf16[32,8,1408]{2,1,0:T(8,128)(2,1)} %fusion.28), calls=%async_computation.4 | async-start | bytes 1441792 | tf_op jit(solution)/shard_map/all_to_all | solution.py:47
  242.4 2.0 copy-start.25
  244.4 3.6 %collective-permute-start.19 = (bf16[256,1280]{1,0:T(8,128)(2,1)}, bf16[256,1280]{1,0:T(8,128)(2,1)}, u32[]{:S(2)}, u32[]{:S(2)}) collective-permute-start(bf16[256,1280]{1,0:T(8,128)(2,1)} %bitcast_select_fusion), channel_id=1, source_target_pairs={{0,128},{128,0},{1,129},{129,1},{2,130},{130,2},{3,131},{131,3},{4... | collective-permute-start | bytes 1966088 | tf_op jit(solution)/shard_map/ppermute | solution.py:180
  244.4 3.5 %copy-start.11 = (bf16[512,1280]{1,0:T(8,128)(2,1)S(1)}, bf16[512,1280]{1,0:T(8,128)(2,1)}, u32[]{:S(2)}) copy-start(bf16[512,1280]{1,0:T(8,128)(2,1)} %copy-done.10) | copy-start | bytes 3932164
  250.1 2.9 %copy-start.17 = (bf16[256,1024]{1,0:T(8,128)(2,1)S(1)}, bf16[256,1024]{1,0:T(8,128)(2,1)}, u32[]{:S(2)}) copy-start(bf16[256,1024]{1,0:T(8,128)(2,1)} %fusion.16) | copy-start | bytes 1572868
  253.6 17.9 %copy-start.12 = (f32[128,1024]{1,0:T(8,128)S(1)}, f32[128,1024]{1,0:T(8,128)}, u32[]{:S(2)}) copy-start(f32[128,1024]{1,0:T(8,128)} %add_add_fusion.1) | copy-start | bytes 1572868
  253.6 17.9 %copy-start.26 = (f32[1,1024]{1,0:T(1,128)S(1)}, f32[1,1024]{1,0:T(1,128)}, u32[]{:S(2)}) copy-start(f32[1,1024]{1,0:T(1,128)} %param.15) | copy-start | bytes 12292
  253.6 10.0 %collective-permute-start.20 = (bf16[128,1152]{1,0:T(8,128)(2,1)S(1)}, bf16[128,1152]{1,0:T(8,128)(2,1)S(1)}, u32[]{:S(2)}, u32[]{:S(2)}) collective-permute-start(bf16[128,1152]{1,0:T(8,128)(2,1)S(1)} %get-tuple-element.58), channel_id=1, source_target_pairs={{0,32},{32,64},{64,96},{96,0},{1,33},{33,65},{65,97},{97,1},{2,34}... | collective-permute-start | bytes 884744 | tf_op jit(solution)/shard_map/ppermute | solution.py:52
  255.1 9.5 %collective-permute-start.22 = (bf16[128,1152]{1,0:T(8,128)(2,1)S(1)}, bf16[128,1152]{1,0:T(8,128)(2,1)S(1)}, u32[]{:S(2)}, u32[]{:S(2)}) collective-permute-start(bf16[128,1152]{1,0:T(8,128)(2,1)S(1)} %get-tuple-element.59), channel_id=1, source_target_pairs={{0,96},{32,0},{64,32},{96,64},{1,97},{33,1},{65,33},{97,65},{2,98}... | collective-permute-start | bytes 884744 | tf_op jit(solution)/shard_map/ppermute | solution.py:52
  255.7 15.5 %collective-permute-start.21 = (bf16[128,1152]{1,0:T(8,128)(2,1)S(1)}, bf16[128,1152]{1,0:T(8,128)(2,1)S(1)}, u32[]{:S(2)}, u32[]{:S(2)}) collective-permute-start(bf16[128,1152]{1,0:T(8,128)(2,1)S(1)} %get-tuple-element.60), channel_id=1, source_target_pairs={{0,64},{32,96},{64,0},{96,32},{1,65},{33,97},{65,1},{97,33},{2,66}... | collective-permute-start | bytes 884744 | tf_op jit(solution)/shard_map/ppermute | solution.py:52
  (10 other events, 7.3 us)

commit v3 on v2

--- a/solution.py
+++ b/solution.py
@@ -72,7 +72,17 @@
 
 
 def start_kernel(
-    core_ref,
+    tokens_hbm,
+    cot_hbm,
+    in_w_hbm,
+    out_w_hbm,
+    gain_hbm,
+    bias_hbm,
+    in_bias_hbm,
+    out_bias_hbm,
+    gained_ref,
+    mine_ref,
+    send_ref,
     tokens_ref,
     cot_ref,
     in_w_ref,
@@ -81,12 +91,26 @@
     bias_ref,
     in_bias_ref,
     out_bias_ref,
-    gained_ref,
-    mine_ref,
-    send_ref,
+    sems,
 ):
     width, hid = in_w_ref.shape
     half = tokens_ref.shape[0] // 2
+    first = lax.axis_index("section") == 0
+    pairs = (
+        (gain_hbm, gain_ref),
+        (in_w_hbm, in_w_ref),
+        (bias_hbm, bias_ref),
+        (in_bias_hbm, in_bias_ref),
+        (out_bias_hbm, out_bias_ref),
+        (tokens_hbm, tokens_ref),
+        (cot_hbm, cot_ref),
+        (out_w_hbm, out_w_ref),
+    )
+    copies = [pltpu.make_async_copy(a, b, sems.at[k]) for k, (a, b) in enumerate(pairs)]
+    for copy in copies:
+        copy.start()
+    for copy in copies[:5]:
+        copy.wait()
     gain = jnp.broadcast_to(gain_ref[...], (128, width)).T
     for at in range(0, hid, 128):
         columns = slice(at, at + 128)
@@ -113,35 +137,114 @@
     mine_ref[half : half + 32, :] = packed
     send_ref[half : half + 32, :] = packed
 
-    @pl.when(core_ref[0] == 0)
+    for copy in copies[5:]:
+        copy.wait()
+
+    @pl.when(first)
     def _():
         for start, target in ((0, mine_ref), (half, send_ref)):
             rows = tokens_ref[start : start + half, :]
             mean = jnp.sum(rows.astype(F32), axis=1, keepdims=True) / width
             target[:half, :] = (dot(rows, gained) - mean * column_sum).astype(BF16)
 
-    @pl.when(core_ref[0] != 0)
+    @pl.when(jnp.logical_not(first))
     def _():
         for start, target in ((half, mine_ref), (0, send_ref)):
             rows = cot_ref[start : start + half, :]
             target[:half, :] = dot_t(rows, out_w_ref[...]).astype(BF16)
 
 
-def start_products(core, tokens, cotangent, in_w, out_w, gain, bias, in_bias, out_bias):
+def in_vmem(kernel, out_shape, *args, flops=0):
+    return pl.pallas_call(
+        kernel,
+        out_shape=out_shape,
+        in_specs=[pl.BlockSpec(memory_space=pltpu.VMEM)] * len(args),
+        out_specs=tuple(pl.BlockSpec(memory_space=pltpu.VMEM) for _ in out_shape),
+        compiler_params=pltpu.CompilerParams(vmem_limit_bytes=32 * 1024 * 1024),
+        cost_estimate=pl.CostEstimate(flops=flops, bytes_accessed=4_000_000, transcendentals=0),
+    )(*args)
+
+
+def start_products(*args):
+    tokens, _, in_w = args[:3]
     width, hid = in_w.shape
     half = tokens.shape[0] // 2
     part = jax.ShapeDtypeStruct((half + 32, hid), BF16)
     return pl.pallas_call(
         start_kernel,
         out_shape=(jax.ShapeDtypeStruct((width, hid), BF16), part, part),
-        in_specs=[pl.BlockSpec(memory_space=pltpu.SMEM)]
-        + [pl.BlockSpec(memory_space=pltpu.VMEM)] * 8,
+        in_specs=[pl.BlockSpec(memory_space=pl.ANY)] * len(args),
         out_specs=(pl.BlockSpec(memory_space=pltpu.VMEM),) * 3,
+        scratch_shapes=[pltpu.VMEM(arg.shape, arg.dtype) for arg in args]
+        + [pltpu.SemaphoreType.DMA((len(args),))],
         compiler_params=pltpu.CompilerParams(vmem_limit_bytes=40 * 1024 * 1024),
         cost_estimate=pl.CostEstimate(
             flops=4 * half * width * hid, bytes_accessed=7_000_000, transcendentals=0
         ),
-    )(core.reshape(1), tokens, cotangent, in_w, out_w, gain, bias, in_bias, out_bias)
+    )(*args)
+
+
+def read_hidden(parts):
+    half = parts[0].shape[0] - 32
+    lower = [part[half : half + 32, :].astype(F32) for part in parts]
+    vectors = [low[:8] + low[8:16] + low[16:24] for low in lower]
+    means = [(low[24:25] + low[25:26] + low[26:27])[:, :half] for low in lower]
+    squares = [(low[27:28] + low[28:29] + low[29:30])[:, :half] for low in lower]
+    count = len(parts)
+    mean = sum(means) / count
+    aparts = [local_mean - mean for local_mean in means]
+    variance = sum(squares) / D + sum(apart * apart for apart in aparts) / count
+    rows = [lax.rsqrt(variance + EPSILON), mean] + aparts
+    rows.append(jnp.zeros((128 - len(rows), half), F32))
+    columns = jnp.concatenate(rows, axis=0).T
+    total = parts[0][:half, :].astype(F32)
+    for part in parts[1:]:
+        total = total + part[:half, :].astype(F32)
+    for place, vector in enumerate(vectors):
+        total = total + columns[:, 2 + place : 3 + place] * vector[:1]
+    pre = total * columns[:, :1]
+    summed = sum(vectors)
+    return pre, pre + (summed[1:2] + vectors[0][2:3]), columns, summed
+
+
+def forward_kernel(*refs):
+    parts, (out_w_ref, y_ref, pre_ref, hidden_ref, columns_ref, sums_ref) = refs[:-6], refs[-6:]
+    pre, hidden, columns, sums = read_hidden(parts)
+    pre_ref[...] = pre
+    hidden_ref[...] = hidden
+    columns_ref[...] = columns
+    sums_ref[...] = sums
+    act = 0.5 * hidden * (1.0 + lax.erf(hidden * SQRT_HALF))
+    y_ref[...] = dot(act.astype(BF16), out_w_ref[...]).astype(BF16)
+
+
+def write_grad(grad_act, hidden, pre, sums, weight, y_ref):
+    width = weight.shape[0]
+    grad_hidden = (grad_act * gelu_slope(hidden)).astype(BF16)
+    grad_f = grad_hidden.astype(F32)
+    total = jnp.sum(grad_f * sums, axis=1, keepdims=True)
+    cross = jnp.sum(grad_f * pre, axis=1, keepdims=True)
+    lane = lax.broadcasted_iota(jnp.int32, (grad_f.shape[0], 128), 1)
+    extra = jnp.zeros(lane.shape, F32)
+    for index, term in enumerate(split3(total) + split3(cross)):
+        extra = jnp.where(lane == index, term.astype(F32), extra)
+    y_ref[:, :width] = dot_t(grad_hidden, weight).astype(BF16)
+    y_ref[:, width:] = extra.astype(BF16)
+
+
+def turn_kernel(*refs):
+    parts, (grad_act_ref, weight_ref, y_ref, columns_ref) = refs[:-4], refs[-4:]
+    pre, hidden, columns, sums = read_hidden(parts)
+    columns_ref[...] = columns
+    write_grad(grad_act_ref[...], hidden, pre, sums[:1], weight_ref[...], y_ref)
+
+
+def backward_kernel(*refs):
+    parts, (hidden_ref, pre_ref, sums_ref, weight_ref, y_ref) = refs[:-5], refs[-5:]
+    grad_act = parts[0][...].astype(F32)
+    for part in parts[1:]:
+        grad_act = grad_act + part[...].astype(F32)
+    write_grad(grad_act, hidden_ref[...], pre_ref[...], sums_ref[:1, :], weight_ref[...], y_ref)
 
 
 def unpack_vectors(part, half):
@@ -196,23 +299,16 @@
 
     def with_stats(part, local_mean, square):
         stats = jnp.stack(split3(local_mean) + split3(square))
-        stats = stats.reshape(-1, hid)
-        return part + jnp.pad(stats, ((half + 24, 8 - stats.shape[0]), (0, 0)))
-
-    def row_stats(parts):
-        means, squares = [], []
-        for part in parts:
-            count = 6 * half // hid
-            stats = part[half + 24 : half + 24 + count].reshape(6, half).astype(F32)
-            means.append(stats[0] + stats[1] + stats[2])
-            squares.append(stats[3] + stats[4] + stats[5])
-        mean = sum(means) / dp_count
-        aparts = [local_mean - mean for local_mean in means]
-        variance = sum(squares) / D + sum(apart * apart for apart in aparts) / dp_count
-        return mean, lax.rsqrt(variance + EPSILON), aparts
+        return part + jnp.pad(stats, ((half + 24, 2), (0, hid - half)))
+
+    part_shape = jax.ShapeDtypeStruct((half, hid), F32)
+    columns_shape = jax.ShapeDtypeStruct((half, 128), F32)
+    y_shape = jax.ShapeDtypeStruct((half, width), BF16)
+    grad_shape = jax.ShapeDtypeStruct((half, width + 128), BF16)
+    flops = 2 * half * hid * width
 
     gained, mine, send = start_products(
-        core, tokens, cotangent, in_w, out_w, ln_gain, ln_bias, in_bias, out_bias
+        tokens, cotangent, in_w, out_w, ln_gain, ln_bias, in_bias, out_bias
     )
     there = other(send)
     tokens_half = lax.dynamic_slice_in_dim(tokens, core * half, half, 0)
@@ -225,20 +321,14 @@
     gained_0, gained_1 = pick(gained, gained_there), pick(gained_there, gained)
     out_w0 = pick(out_w, other(out_w))
 
-    def gathered(part, in_b):
-        got = gather_ring(part, "dp")
-        mean, inv, aparts = row_stats(got)
-        vectors = [unpack_vectors(g, half) for g in got]
-        sums = [v[0] for v in vectors]
-        total = sum(g[:half].astype(F32) for g in got)
-        total = total + sum(apart[:, None] * s[None] for apart, s in zip(aparts, sums))
-        pre = total * inv[:, None]
-        shift = sum(v[1] for v in vectors) + in_b
-        return pre, pre + shift[None], mean, inv, sum(sums)
-
-    pre_0, hidden_0, mean_0, inv_0, sums_0 = gathered(part_0, vectors_0[2])
-    act_0 = jax.nn.gelu(hidden_0, approximate=False).astype(BF16)
-    mlp = exchange(dot(act_0, out_w0).astype(BF16), "latent")
+    y_0, pre_0, hidden_0, columns_0, sums_0 = in_vmem(
+        forward_kernel,
+        (y_shape, part_shape, part_shape, columns_shape, jax.ShapeDtypeStruct((8, hid), F32)),
+        *gather_ring(part_0, "dp"),
+        out_w0,
+        flops=flops,
+    )
+    mlp = exchange(y_0, "latent")
     tokens_rows = own_rows(tokens_half).astype(F32)
     bias_row = vectors_0[3:7].reshape(-1)[:width]
     resid_rows = (tokens_rows + jnp.sum(mlp.astype(F32), axis=0) + bias_row[None]).astype(BF16)
@@ -250,42 +340,34 @@
     part_1 = dot(resid_half, gained_1) - local_mean[:, None] * vectors_1[0][None]
     part_1 = jnp.concatenate([part_1.astype(BF16), part_grad[half:]], axis=0)
     resid_there = other(resid_half)
-    pre_1, hidden_1, mean_1, inv_1, sums_1 = gathered(
-        with_stats(part_1, local_mean, square), vectors_1[2]
-    )
-    hidden_1, resid_there = lax.optimization_barrier((hidden_1, resid_there))
-
-    def backward(grad_act, hidden, pre, weight, sums, resid, mean, inv, grad_rows):
-        grad_hidden = (grad_act * gelu_slope(hidden)).astype(BF16)
-        grad_f = grad_hidden.astype(F32)
-        total = jnp.sum(grad_f * sums[None], axis=1)
-        cross = jnp.sum(grad_f * pre, axis=1)
-        extra = jnp.stack(split3(total) + split3(cross), axis=1)
-        extra = jnp.pad(extra, ((0, 0), (0, 128 - extra.shape[1])))
-        partial = dot_t(grad_hidden, weight).astype(BF16)
-        summed = exchange(jnp.concatenate([partial, extra], axis=1), "latent")
-        summed = jnp.sum(summed.astype(F32), axis=0)
+    parts_1 = gather_ring(with_stats(part_1, local_mean, square), "dp")
+    parts_1, resid_there = lax.optimization_barrier((parts_1, resid_there))
+
+    def norm_grad(y, columns, resid, grad_rows):
+        summed = jnp.sum(exchange(y, "latent").astype(F32), axis=0)
         grad_norm, extra = summed[:, :width], summed[:, width : width + 6] / D
         mean_grad = (extra[:, 0] + extra[:, 1] + extra[:, 2])[:, None]
         mean_cross = (extra[:, 3] + extra[:, 4] + extra[:, 5])[:, None]
-        inv_rows = own_rows(inv)[:, None]
-        normed = (resid - own_rows(mean)[:, None]) * inv_rows
-        grad_resid = inv_rows * (grad_norm - mean_grad - normed * mean_cross)
+        columns = own_rows(columns)
+        inv, mean = columns[:, :1], columns[:, 1:2]
+        normed = (resid - mean) * inv
+        grad_resid = inv * (grad_norm - mean_grad - normed * mean_cross)
         new_rows = (grad_rows + grad_resid).astype(BF16)
         return new_rows, spread(new_rows, "latent").reshape(half, width)
 
+    y_1, columns_1 = in_vmem(
+        turn_kernel, (grad_shape, columns_shape), *parts_1, grad_act_1, gained_1, flops=flops
+    )
     cot_rows = own_rows(cot_half).astype(F32)
-    grad_rows_1, grad_half_1 = backward(
-        grad_act_1, hidden_1, pre_1, gained_1, sums_1, resid_rows.astype(F32), mean_1, inv_1, cot_rows
-    )
+    grad_rows_1, grad_half_1 = norm_grad(y_1, columns_1, resid_rows.astype(F32), cot_rows)
     resid_all = pick(tokens, jnp.concatenate([resid_there, resid_half], axis=0))
     pre_codes = scatter_ring(dot(resid_all, enc_weight[0]).astype(BF16), "dp")
     grad_half_1, pre_codes = lax.optimization_barrier((grad_half_1, pre_codes))
-    grad_act_0 = total_ring(dot_t(grad_half_1, out_w0).astype(BF16), "dp")
-    _, grad_half_0 = backward(
-        grad_act_0, hidden_0, pre_0, gained_0, sums_0, tokens_rows, mean_0, inv_0,
-        grad_rows_1.astype(F32),
-    )
+    parts_0 = gather_ring(dot_t(grad_half_1, out_w0).astype(BF16), "dp")
+    (y_2,) = in_vmem(
+        backward_kernel, (grad_shape,), *parts_0, hidden_0, pre_0, sums_0, gained_0, flops=flops
+    )
+    _, grad_half_0 = norm_grad(y_2, columns_0, tokens_rows, grad_rows_1.astype(F32))
 
     codes = jnp.maximum(pre_codes + enc_bias[0][None], 0.0).astype(BF16)
     resid_own = lax.dynamic_slice_in_dim(resid_all, core * half, half, 0)

time: 290 us -> 291 us (level)
  local copies, waits for them, and re-layouts: 16.6 us -> 25.7 us
  matrix products: 18.5 us -> 12 us
  other arithmetic: 37.4 us -> 31.7 us
  Pallas kernels: 1.5 us -> 6.64 us
    ppermute x18, waiting for transfers between devices: 49.4 us -> 54.9 us  [turn(): lax.ppermute(values, axis, [(i, (i + by) % count) for i in range(count)])]
    select_n x4 -> x6, other arithmetic: 5.31 us -> 9.57 us  [pick(): return jnp.where(first, mine_if_first, mine_if_second)]
    pallas_call x0 -> x3, Pallas kernels: none -> 4.26 us  [in_vmem(): pl.pallas_call(kernel, out_shape=out_shape, in_specs=[pl.BlockSpec(memory...]
    all_to_all x2, waiting for transfers between devices: 18.5 us -> 14.8 us  [spread(): return lax.all_to_all(copies, axis, 0, 0)]
    convert_element_type x10 -> x2, other arithmetic: 5.24 us -> 1.75 us  [norm_grad(): new_rows = (grad_rows + grad_resid).astype(BF16)]
    dot_general x5 -> x3, matrix products: 11.9 us -> 8.43 us  [dot_t(): lax.dot_general(left, right, CONTRACT_LAST, preferred_element_type=F32)]
    add x12 -> x3, other arithmetic: 3.88 us -> 0.4 us  [the longest x2 0.37 us: norm_grad(): mean_grad = (extra[:, 0] + extra[:, 1] + extra[:, 2])[:, None]]
    dot_general x3 -> x2, matrix products: 6.62 us -> 3.54 us  [dot(): return jnp.dot(left, right, preferred_element_type=F32)]
where the time goes in v3:
time: 291 us; the launch traced here: 289 us
  waiting for transfers between devices  110 us (38%)
  starting transfers between devices  67.2 us (23%)
  blocking collectives  34.9 us (12%)
  other arithmetic  31.7 us (11%)
  local copies, waits for them, and re-layouts  25.7 us (9%)
  matrix products  12 us (4%)
  Pallas kernels  6.64 us (2%)
    ppermute x18, waiting for transfers between devices, turn(): lax.ppermute(values, axis, [(i, (i + by) % count) for i in range(count)])  54.9 us
    all_to_all x3, waiting for transfers between devices, exchange(): lax.all_to_all(values.reshape(count, rows, values.shape[1]), axis, 0, 0)  40.3 us
    all_to_all x2, blocking collectives, spread(): return lax.all_to_all(copies, axis, 0, 0)  34.9 us
    ppermute x18, starting transfers between devices, turn(): lax.ppermute(values, axis, [(i, (i + by) % count) for i in range(count)])  28.5 us
    all_to_all x3, starting transfers between devices, exchange(): lax.all_to_all(values.reshape(count, rows, values.shape[1]), axis, 0, 0)  26 us
    all_to_all x2, waiting for transfers between devices, spread(): return lax.all_to_all(copies, axis, 0, 0)  14.8 us
    unnamed x58, local copies, waits for them, and re-layouts  13.6 us
    all_to_all x2, starting transfers between devices, spread(): return lax.all_to_all(copies, axis, 0, 0)  12.1 us
  transfers between devices with their start and end apart: 28, of which 19 were waited for; matrix products, arithmetic and copies ran while one was open for 11% of the time, Pallas kernels for 1%

profile of v3, /device:TPU:8, one launch (start us, length us, event | category | flops | bytes accessed | tf_op | source)
XLA Modules:
  0.0 289.3 jit_solution(13479595912751713453)
XLA Ops:
  8.7 2.4 shard_map.131
  15.9 2.2 collective-permute-start.3
  19.0 1.9 collective-permute-start.1
  22.2 1.7 collective-permute-done.3.refs_3_
  23.9 5.3 %collective-permute-done.2.refs_2_ = bf16[288,384]{1,0:T(8,128)(2,1)S(1)} collective-permute-done((bf16[288,384]{1,0:T(8,128)(2,1)S(1)}, bf16[288,384]{1,0:T(8,128)(2,1)S(1)}, u32[]{:S(2)}, u32[]{:S(2)}) %collective-permute-start.2) | collective-permute-done | bytes 221216 | tf_op jit(solution)/shard_map/ppermute | solution.py:52
  30.0 1.7 shard_map.132
  33.4 11.4 %all-to-all-start = ((bf16[32,8,1280]{2,1,0:T(8,128)(2,1)}), bf16[32,8,1280]{2,1,0:T(8,128)(2,1)}, u32[]{:S(2)}, u32[]{:S(2)}) async-start(bf16[32,8,1280]{2,1,0:T(8,128)(2,1)} %bitcast.4), calls=%async_computation | async-start | bytes 1310720 | tf_op jit(solution)/shard_map/all_to_all | solution.py:47
  45.0 1.6 slice.148
  46.6 2.3 collective-permute-start.6
  48.9 2.0 collective-permute-start.5
  51.6 4.6 %collective-permute-done.6 = bf16[256,384]{1,0:T(8,128)(2,1)} collective-permute-done((bf16[256,384]{1,0:T(8,128)(2,1)}, bf16[256,384]{1,0:T(8,128)(2,1)}, u32[]{:S(2)}, u32[]{:S(2)}) %collective-permute-start.6) | collective-permute-done | bytes 196640 | tf_op jit(solution)/shard_map/ppermute | solution.py:52
  56.1 3.8 %collective-permute-done.5 = bf16[256,384]{1,0:T(8,128)(2,1)} collective-permute-done((bf16[256,384]{1,0:T(8,128)(2,1)}, bf16[256,384]{1,0:T(8,128)(2,1)}, u32[]{:S(2)}, u32[]{:S(2)}) %collective-permute-start.5) | collective-permute-done | bytes 196640 | tf_op jit(solution)/shard_map/ppermute | solution.py:52
  61.2 3.1 %all-to-all-done = bf16[32,8,1280]{2,1,0:T(8,128)(2,1)} async-done(((bf16[32,8,1280]{2,1,0:T(8,128)(2,1)}), bf16[32,8,1280]{2,1,0:T(8,128)(2,1)}, u32[]{:S(2)}, u32[]{:S(2)}) %all-to-all-start) | async-done | bytes 655392 | tf_op jit(solution)/shard_map/all_to_all | solution.py:47
  67.8 6.8 %all-to-all-start.1 = ((bf16[32,8,1280]{2,1,0:T(8,128)(2,1)}), bf16[32,8,1280]{2,1,0:T(8,128)(2,1)}, u32[]{:S(2)}, u32[]{:S(2)}) async-start(bf16[32,8,1280]{2,1,0:T(8,128)(2,1)} %broadcast_in_dim.12), calls=%async_computation.1 | async-start | bytes 1310720 | tf_op jit(solution)/shard_map/all_to_all | solution.py:41
  77.3 3.0 %broadcast_select_fusion = (bf16[1280,384]{1,0:T(8,128)(2,1)}, bf16[1280,384]{1,0:T(8,128)(2,1)}) fusion(bf16[1280,384]{1,0:T(8,128)(2,1)} %copy-done.8, bf16[1280,384]{1,0:T(8,128)(2,1)} %collective-permute-done.8, pred[]{:T(512)S(6)} %eq.12), kind=kLoop, calls=%fused_computation.27 | loop fusion | flops 983040 | bytes 3932161 | tf_op jit(solution)/shard_map/jit(_where)/select_n | solution.py:286
  80.3 14.8 %all-to-all-done.1 = bf16[32,8,1280]{2,1,0:T(8,128)(2,1)} async-done(((bf16[32,8,1280]{2,1,0:T(8,128)(2,1)}), bf16[32,8,1280]{2,1,0:T(8,128)(2,1)}, u32[]{:S(2)}, u32[]{:S(2)}) %all-to-all-start.1) | async-done | bytes 655392 | tf_op jit(solution)/shard_map/all_to_all | solution.py:41
  97.8 2.0 fusion.12
  105.1 2.0 fusion.19
  107.1 2.9 %collective-permute-start.11 = (bf16[288,384]{1,0:T(8,128)(2,1)S(1)}, bf16[288,384]{1,0:T(8,128)(2,1)S(1)}, u32[]{:S(2)}, u32[]{:S(2)}) collective-permute-start(bf16[288,384]{1,0:T(8,128)(2,1)S(1)} %maximum_add_fusion.refs_0_), channel_id=1, source_target_pairs={{0,96},{32,0},{64,32},{96,64},{1,97},{33,1},{65,33},{97,65},{2,98}... | collective-permute-start | bytes 663560 | tf_op jit(solution)/shard_map/ppermute | solution.py:52
  110.1 2.0 collective-permute-start.9
  112.1 3.7 %collective-permute-done.11.refs_3_ = bf16[288,384]{1,0:T(8,128)(2,1)S(1)} collective-permute-done((bf16[288,384]{1,0:T(8,128)(2,1)S(1)}, bf16[288,384]{1,0:T(8,128)(2,1)S(1)}, u32[]{:S(2)}, u32[]{:S(2)}) %collective-permute-start.11) | collective-permute-done | bytes 221216 | tf_op jit(solution)/shard_map/ppermute | solution.py:52
  115.8 4.8 %collective-permute-done.10.refs_2_ = bf16[288,384]{1,0:T(8,128)(2,1)S(1)} collective-permute-done((bf16[288,384]{1,0:T(8,128)(2,1)S(1)}, bf16[288,384]{1,0:T(8,128)(2,1)S(1)}, u32[]{:S(2)}, u32[]{:S(2)}) %collective-permute-start.10) | collective-permute-done | bytes 221216 | tf_op jit(solution)/shard_map/ppermute | solution.py:52
  124.1 5.1 %all-to-all-start.2 = ((bf16[32,8,1408]{2,1,0:T(8,128)(2,1)}), bf16[32,8,1408]{2,1,0:T(8,128)(2,1)}, u32[]{:S(2)}, u32[]{:S(2)}) async-start(bf16[32,8,1408]{2,1,0:T(8,128)(2,1)} %bitcast.48), calls=%async_computation.2 | async-start | bytes 1441792 | tf_op jit(solution)/shard_map/all_to_all | solution.py:47
  130.2 20.1 %all-to-all-done.2 = bf16[32,8,1408]{2,1,0:T(8,128)(2,1)} async-done(((bf16[32,8,1408]{2,1,0:T(8,128)(2,1)}), bf16[32,8,1408]{2,1,0:T(8,128)(2,1)}, u32[]{:S(2)}, u32[]{:S(2)}) %all-to-all-start.2) | async-done | bytes 720928 | tf_op jit(solution)/shard_map/all_to_all | solution.py:47
  154.1 5.3 %all-to-all-start.3 = ((bf16[32,8,1280]{2,1,0:T(8,128)(2,1)}), bf16[32,8,1280]{2,1,0:T(8,128)(2,1)}, u32[]{:S(2)}, u32[]{:S(2)}) async-start(bf16[32,8,1280]{2,1,0:T(8,128)(2,1)} %broadcast_in_dim.13), calls=%async_computation.3 | async-start | bytes 1310720 | tf_op jit(solution)/shard_map/all_to_all | solution.py:41
  159.4 2.0 maximum_select_fusion
  161.4 1.6 fusion.6
  164.1 2.0 collective-permute-start.13
  167.6 2.1 collective-permute-start.14
  169.7 5.5 %collective-permute-done.13 = bf16[128,1024]{1,0:T(8,128)(2,1)} collective-permute-done((bf16[128,1024]{1,0:T(8,128)(2,1)}, bf16[128,1024]{1,0:T(8,128)(2,1)}, u32[]{:S(2)}, u32[]{:S(2)}) %collective-permute-start.13) | collective-permute-done | bytes 262176 | tf_op jit(solution)/shard_map/ppermute | solution.py:52
  175.2 4.9 %collective-permute-done.14 = bf16[128,1024]{1,0:T(8,128)(2,1)} collective-permute-done((bf16[128,1024]{1,0:T(8,128)(2,1)S(1)}, bf16[128,1024]{1,0:T(8,128)(2,1)}, u32[]{:S(2)}, u32[]{:S(2)}) %collective-permute-start.14) | collective-permute-done | bytes 262176 | tf_op jit(solution)/shard_map/ppermute | solution.py:52
  180.1 2.2 add_add_fusion.1
  182.3 2.0 convolution_convert_fusion.refs_0_
  185.5 1.9 collective-permute-start.17
  187.4 2.5 collective-permute-start.16
  190.6 2.4 collective-permute-done.17.refs_2_
  194.6 1.5 shard_map.134
  196.1 9.5 %all-to-all-start.4 = ((bf16[32,8,1408]{2,1,0:T(8,128)(2,1)}), bf16[32,8,1408]{2,1,0:T(8,128)(2,1)S(1)}, u32[]{:S(2)}, u32[]{:S(2)}) async-start(bf16[32,8,1408]{2,1,0:T(8,128)(2,1)} %bitcast.10), calls=%async_computation.4 | async-start | bytes 1441792 | tf_op jit(solution)/shard_map/all_to_all | solution.py:47
  205.8 17.2 %all-to-all-done.4 = bf16[32,8,1408]{2,1,0:T(8,128)(2,1)S(1)} async-done(((bf16[32,8,1408]{2,1,0:T(8,128)(2,1)}), bf16[32,8,1408]{2,1,0:T(8,128)(2,1)S(1)}, u32[]{:S(2)}, u32[]{:S(2)}) %all-to-all-start.4) | async-done | bytes 720928 | tf_op jit(solution)/shard_map/all_to_all | solution.py:47
  224.2 21.1 %all_to_all.35 = bf16[32,8,1280]{2,1,0:T(8,128)(2,1)S(1)} all-to-all(bf16[32,8,1280]{2,1,0:T(8,128)(2,1)S(1)} %broadcast_in_dim.14), channel_id=1, replica_groups=mesh['section'=2,'dp'=4,'latent'=32] {'latent'}, dimensions={0} | all-to-all | bytes 1310720 | tf_op jit(solution)/shard_map/all_to_all | solution.py:41
  245.3 2.0 bitcast_select_fusion
  247.4 3.5 %fusion.13 = bf16[256,1024]{1,0:T(8,128)(2,1)} fusion(bf16[1,1024,1280]{2,1,0:T(8,128)(2,1)} %param.16, bf16[256,1280]{1,0:T(8,128)(2,1)} %bitcast.7, bf16[32,8,1280]{2,1,0:T(8,128)(2,1)S(1)} %all_to_all.35, pred[]{:T(512)S(6)} %eq.12), kind=kOutput, calls=%fused_computation.21 | convolution fusion | flops 671678464 | bytes 4456449 | tf_op jit(solution)/shard_map/dot_general | solution.py:35
  250.9 1.7 multiply_reduce_fusion.1
  253.1 2.9 fusion.16
  256.5 1.5 collective-permute-start.20
  259.6 6.9 %collective-permute-done.20 = bf16[128,1152]{1,0:T(8,128)(2,1)S(1)} collective-permute-done((bf16[128,1152]{1,0:T(8,128)(2,1)S(1)}, bf16[128,1152]{1,0:T(8,128)(2,1)S(1)}, u32[]{:S(2)}, u32[]{:S(2)}) %collective-permute-start.20) | collective-permute-done | bytes 294944 | tf_op jit(solution)/shard_map/ppermute | solution.py:52
  266.5 7.4 %collective-permute-done.22 = bf16[128,1152]{1,0:T(8,128)(2,1)S(1)} collective-permute-done((bf16[128,1152]{1,0:T(8,128)(2,1)S(1)}, bf16[128,1152]{1,0:T(8,128)(2,1)S(1)}, u32[]{:S(2)}, u32[]{:S(2)}) %collective-permute-start.22) | collective-permute-done | bytes 294944 | tf_op jit(solution)/shard_map/ppermute | solution.py:52
  275.0 13.8 %all_to_all.36 = f32[32,1,128]{2,1,0:T(1,128)S(1)} all-to-all(f32[32,1,128]{2,1,0:T(1,128)S(1)} %broadcast_in_dim.16), channel_id=1, replica_groups=mesh['section'=2,'dp'=4,'latent'=32] {'latent'}, dimensions={0} | all-to-all | bytes 32768 | tf_op jit(solution)/shard_map/all_to_all | solution.py:41
  (150 shorter events, 53.5 us)
Async XLA Ops:
  0.6 160.7 %copy-start = (bf16[1,1280,1024]{2,1,0:T(8,128)(2,1)S(1)}, bf16[1,1280,1024]{2,1,0:T(8,128)(2,1)}, u32[]{:S(2)}) copy-start(bf16[1,1280,1024]{2,1,0:T(8,128)(2,1)} %param.14) | copy-start | bytes 7864324
  0.6 20.2 %collective-permute-start.4 = (bf16[384,1280]{1,0:T(8,128)(2,1)}, bf16[384,1280]{1,0:T(8,128)(2,1)}, u32[]{:S(2)}, u32[]{:S(2)}) collective-permute-start(bf16[384,1280]{1,0:T(8,128)(2,1)} %bitcast.45), channel_id=1, source_target_pairs={{0,128},{128,0},{1,129},{129,1},{2,130},{130,2},{3,131},{131,3},{4... | collective-permute-start | bytes 2949128 | tf_op jit(solution)/shard_map/ppermute | solution.py:283
  0.8 1.5 copy-start.1
  2.2 1.2 copy-start.3
  3.4 1.3 copy-start.6
  4.7 1.2 copy-start.7
  11.1 1.0 copy-start.8
  12.0 3.1 %collective-permute-start = (bf16[288,384]{1,0:T(8,128)(2,1)S(1)}, bf16[288,384]{1,0:T(8,128)(2,1)S(1)}, u32[]{:S(2)}, u32[]{:S(2)}) collective-permute-start(bf16[288,384]{1,0:T(8,128)(2,1)S(1)} %get-tuple-element.22), channel_id=1, source_target_pairs={{0,128},{128,0},{1,129},{129,1},{2,130},{130,2},{3,131},{131,3},{4... | collective-permute-start | bytes 663560 | tf_op jit(solution)/shard_map/ppermute | solution.py:283
  15.9 7.9 %collective-permute-start.3 = (bf16[288,384]{1,0:T(8,128)(2,1)S(1)}, bf16[288,384]{1,0:T(8,128)(2,1)S(1)}, u32[]{:S(2)}, u32[]{:S(2)}) collective-permute-start(bf16[288,384]{1,0:T(8,128)(2,1)S(1)} %get-tuple-element.61.refs_0_), channel_id=1, source_target_pairs={{0,96},{32,0},{64,32},{96,64},{1,97},{33,1},{65,33},{97,65},{2,98}... | collective-permute-start | bytes 663560 | tf_op jit(solution)/shard_map/ppermute | solution.py:52
  18.1 11.1 %collective-permute-start.2 = (bf16[288,384]{1,0:T(8,128)(2,1)S(1)}, bf16[288,384]{1,0:T(8,128)(2,1)S(1)}, u32[]{:S(2)}, u32[]{:S(2)}) collective-permute-start(bf16[288,384]{1,0:T(8,128)(2,1)S(1)} %get-tuple-element.61.refs_0_), channel_id=1, source_target_pairs={{0,64},{32,96},{64,0},{96,32},{1,65},{33,97},{65,1},{97,33},{2,66}... | collective-permute-start | bytes 663560 | tf_op jit(solution)/shard_map/ppermute | solution.py:52
  19.0 11.0 %collective-permute-start.1 = (bf16[288,384]{1,0:T(8,128)(2,1)S(1)}, bf16[288,384]{1,0:T(8,128)(2,1)S(1)}, u32[]{:S(2)}, u32[]{:S(2)}) collective-permute-start(bf16[288,384]{1,0:T(8,128)(2,1)S(1)} %get-tuple-element.61.refs_0_), channel_id=1, source_target_pairs={{0,32},{32,64},{64,96},{96,0},{1,33},{33,65},{65,97},{97,1},{2,34}... | collective-permute-start | bytes 663560 | tf_op jit(solution)/shard_map/ppermute | solution.py:52
  31.7 1.0 copy-start.2
  33.4 30.9 %all-to-all-start = ((bf16[32,8,1280]{2,1,0:T(8,128)(2,1)}), bf16[32,8,1280]{2,1,0:T(8,128)(2,1)}, u32[]{:S(2)}, u32[]{:S(2)}) async-start(bf16[32,8,1280]{2,1,0:T(8,128)(2,1)} %bitcast.4), calls=%async_computation | async-start | bytes 1310720 | tf_op jit(solution)/shard_map/all_to_all | solution.py:47
  44.9 32.4 %collective-permute-start.8 = (bf16[1280,384]{1,0:T(8,128)(2,1)}, bf16[1280,384]{1,0:T(8,128)(2,1)}, u32[]{:S(2)}, u32[]{:S(2)}) collective-permute-start(bf16[1280,384]{1,0:T(8,128)(2,1)} %copy-done.8), channel_id=1, source_target_pairs={{0,128},{128,0},{1,129},{129,1},{2,130},{130,2},{3,131},{131,3},{4... | collective-permute-start | bytes 2949128 | tf_op jit(solution)/shard_map/ppermute | solution.py:283
  46.6 9.5 %collective-permute-start.6 = (bf16[256,384]{1,0:T(8,128)(2,1)}, bf16[256,384]{1,0:T(8,128)(2,1)}, u32[]{:S(2)}, u32[]{:S(2)}) collective-permute-start(bf16[256,384]{1,0:T(8,128)(2,1)} %slice.148), channel_id=1, source_target_pairs={{0,64},{32,96},{64,0},{96,32},{1,65},{33,97},{65,1},{97,33},{2,66}... | collective-permute-start | bytes 589832 | tf_op jit(solution)/shard_map/ppermute | solution.py:52
  48.9 11.0 %collective-permute-start.5 = (bf16[256,384]{1,0:T(8,128)(2,1)}, bf16[256,384]{1,0:T(8,128)(2,1)}, u32[]{:S(2)}, u32[]{:S(2)}) collective-permute-start(bf16[256,384]{1,0:T(8,128)(2,1)} %slice.148), channel_id=1, source_target_pairs={{0,32},{32,64},{64,96},{96,0},{1,33},{33,65},{65,97},{97,1},{2,34}... | collective-permute-start | bytes 589832 | tf_op jit(solution)/shard_map/ppermute | solution.py:52
  50.9 9.0 %collective-permute-start.7 = (bf16[256,384]{1,0:T(8,128)(2,1)}, bf16[256,384]{1,0:T(8,128)(2,1)}, u32[]{:S(2)}, u32[]{:S(2)}) collective-permute-start(bf16[256,384]{1,0:T(8,128)(2,1)} %slice.148), channel_id=1, source_target_pairs={{0,96},{32,0},{64,32},{96,64},{1,97},{33,1},{65,33},{97,65},{2,98}... | collective-permute-start | bytes 589832 | tf_op jit(solution)/shard_map/ppermute | solution.py:52
  67.8 27.3 %all-to-all-start.1 = ((bf16[32,8,1280]{2,1,0:T(8,128)(2,1)}), bf16[32,8,1280]{2,1,0:T(8,128)(2,1)}, u32[]{:S(2)}, u32[]{:S(2)}) async-start(bf16[32,8,1280]{2,1,0:T(8,128)(2,1)} %broadcast_in_dim.12), calls=%async_computation.1 | async-start | bytes 1310720 | tf_op jit(solution)/shard_map/all_to_all | solution.py:41
  102.4 19.2 %collective-permute-start.12 = (bf16[256,1280]{1,0:T(8,128)(2,1)}, bf16[256,1280]{1,0:T(8,128)(2,1)}, u32[]{:S(2)}, u32[]{:S(2)}) collective-permute-start(bf16[256,1280]{1,0:T(8,128)(2,1)} %bitcast.5), channel_id=1, source_target_pairs={{0,128},{128,0},{1,129},{129,1},{2,130},{130,2},{3,131},{131,3},{4... | collective-permute-start | bytes 1966088 | tf_op jit(solution)/shard_map/ppermute | solution.py:283
  105.1 2.0 copy-start.26
  105.1 16.5 %copy-start.5 = (bf16[1280,384]{1,0:T(8,128)(2,1)S(1)}, bf16[1280,384]{1,0:T(8,128)(2,1)}, u32[]{:S(2)}) copy-start(bf16[1280,384]{1,0:T(8,128)(2,1)} %get-tuple-element.51.refs_5_) | copy-start | bytes 2949124
  107.1 8.7 %collective-permute-start.11 = (bf16[288,384]{1,0:T(8,128)(2,1)S(1)}, bf16[288,384]{1,0:T(8,128)(2,1)S(1)}, u32[]{:S(2)}, u32[]{:S(2)}) collective-permute-start(bf16[288,384]{1,0:T(8,128)(2,1)S(1)} %maximum_add_fusion.refs_0_), channel_id=1, source_target_pairs={{0,96},{32,0},{64,32},{96,64},{1,97},{33,1},{65,33},{97,65},{2,98}... | collective-permute-start | bytes 663560 | tf_op jit(solution)/shard_map/ppermute | solution.py:52
  110.1 10.6 %collective-permute-start.10 = (bf16[288,384]{1,0:T(8,128)(2,1)S(1)}, bf16[288,384]{1,0:T(8,128)(2,1)S(1)}, u32[]{:S(2)}, u32[]{:S(2)}) collective-permute-start(bf16[288,384]{1,0:T(8,128)(2,1)S(1)} %maximum_add_fusion.refs_0_), channel_id=1, source_target_pairs={{0,64},{32,96},{64,0},{96,32},{1,65},{33,97},{65,1},{97,33},{2,66}... | collective-permute-start | bytes 663560 | tf_op jit(solution)/shard_map/ppermute | solution.py:52
  110.1 11.5 %collective-permute-start.9 = (bf16[288,384]{1,0:T(8,128)(2,1)S(1)}, bf16[288,384]{1,0:T(8,128)(2,1)S(1)}, u32[]{:S(2)}, u32[]{:S(2)}) collective-permute-start(bf16[288,384]{1,0:T(8,128)(2,1)S(1)} %maximum_add_fusion.refs_0_), channel_id=1, source_target_pairs={{0,32},{32,64},{64,96},{96,0},{1,33},{33,65},{65,97},{97,1},{2,34}... | collective-permute-start | bytes 663560 | tf_op jit(solution)/shard_map/ppermute | solution.py:52
  124.1 27.6 %copy-start.25 = (bf16[8,1280]{1,0:T(8,128)(2,1)S(1)}, bf16[8,1280]{1,0:T(8,128)(2,1)}, u32[]{:S(2)}) copy-start(bf16[8,1280]{1,0:T(8,128)(2,1)} %copy-done.24) | copy-start | bytes 61444
  124.1 26.1 %all-to-all-start.2 = ((bf16[32,8,1408]{2,1,0:T(8,128)(2,1)}), bf16[32,8,1408]{2,1,0:T(8,128)(2,1)}, u32[]{:S(2)}, u32[]{:S(2)}) async-start(bf16[32,8,1408]{2,1,0:T(8,128)(2,1)} %bitcast.48), calls=%async_computation.2 | async-start | bytes 1441792 | tf_op jit(solution)/shard_map/all_to_all | solution.py:47
  154.1 28.2 %all-to-all-start.3 = ((bf16[32,8,1280]{2,1,0:T(8,128)(2,1)}), bf16[32,8,1280]{2,1,0:T(8,128)(2,1)}, u32[]{:S(2)}, u32[]{:S(2)}) async-start(bf16[32,8,1280]{2,1,0:T(8,128)(2,1)} %broadcast_in_dim.13), calls=%async_computation.3 | async-start | bytes 1310720 | tf_op jit(solution)/shard_map/all_to_all | solution.py:41
  161.4 1.6 copy-start.17
  163.0 1.2 copy-start.20
  164.1 11.0 %collective-permute-start.13 = (bf16[128,1024]{1,0:T(8,128)(2,1)}, bf16[128,1024]{1,0:T(8,128)(2,1)}, u32[]{:S(2)}, u32[]{:S(2)}) collective-permute-start(bf16[128,1024]{1,0:T(8,128)(2,1)} %get-tuple-element.57), channel_id=1, source_target_pairs={{0,32},{32,64},{64,96},{96,0},{1,33},{33,65},{65,97},{97,1},{2,34}... | collective-permute-start | bytes 786440 | tf_op jit(solution)/shard_map/ppermute | solution.py:52
  166.2 9.0 %collective-permute-start.15 = (bf16[128,1024]{1,0:T(8,128)(2,1)}, bf16[128,1024]{1,0:T(8,128)(2,1)}, u32[]{:S(2)}, u32[]{:S(2)}) collective-permute-start(bf16[128,1024]{1,0:T(8,128)(2,1)} %get-tuple-element.58), channel_id=1, source_target_pairs={{0,96},{32,0},{64,32},{96,64},{1,97},{33,1},{65,33},{97,65},{2,98}... | collective-permute-start | bytes 786440 | tf_op jit(solution)/shard_map/ppermute | solution.py:52
  167.6 12.5 %collective-permute-start.14 = (bf16[128,1024]{1,0:T(8,128)(2,1)S(1)}, bf16[128,1024]{1,0:T(8,128)(2,1)}, u32[]{:S(2)}, u32[]{:S(2)}) collective-permute-start(bf16[128,1024]{1,0:T(8,128)(2,1)S(1)} %get-tuple-element.59), channel_id=1, source_target_pairs={{0,64},{32,96},{64,0},{96,32},{1,65},{33,97},{65,1},{97,33},{2,66}... | collective-permute-start | bytes 786440 | tf_op jit(solution)/shard_map/ppermute | solution.py:52
  182.2 12.3 %copy-start.11 = (f32[256,384]{1,0:T(8,128)S(1)}, f32[256,384]{1,0:T(8,128)}, u32[]{:S(2)}) copy-start(f32[256,384]{1,0:T(8,128)} %copy-done.10) | copy-start | bytes 1179652
  182.3 12.3 %copy-start.4 = (bf16[1280,384]{1,0:T(8,128)(2,1)S(1)}, bf16[1280,384]{1,0:T(8,128)(2,1)}, u32[]{:S(2)}) copy-start(bf16[1280,384]{1,0:T(8,128)(2,1)} %get-tuple-element.50.refs_7_) | copy-start | bytes 2949124
  184.3 6.3 %collective-permute-start.18 = (bf16[256,384]{1,0:T(8,128)(2,1)S(1)}, bf16[256,384]{1,0:T(8,128)(2,1)S(1)}, u32[]{:S(2)}, u32[]{:S(2)}) collective-permute-start(bf16[256,384]{1,0:T(8,128)(2,1)S(1)} %convolution_convert_fusion.refs_0_), channel_id=1, source_target_pairs={{0,96},{32,0},{64,32},{96,64},{1,97},{33,1},{65,33},{97,65},{2,98}... | collective-permute-start | bytes 589832 | tf_op jit(solution)/shard_map/ppermute | solution.py:52
  185.5 7.5 %collective-permute-start.17 = (bf16[256,384]{1,0:T(8,128)(2,1)S(1)}, bf16[256,384]{1,0:T(8,128)(2,1)S(1)}, u32[]{:S(2)}, u32[]{:S(2)}) collective-permute-start(bf16[256,384]{1,0:T(8,128)(2,1)S(1)} %convolution_convert_fusion.refs_0_), channel_id=1, source_target_pairs={{0,64},{32,96},{64,0},{96,32},{1,65},{33,97},{65,1},{97,33},{2,66}... | collective-permute-start | bytes 589832 | tf_op jit(solution)/shard_map/ppermute | solution.py:52
  187.4 7.1 %collective-permute-start.16 = (bf16[256,384]{1,0:T(8,128)(2,1)S(1)}, bf16[256,384]{1,0:T(8,128)(2,1)S(1)}, u32[]{:S(2)}, u32[]{:S(2)}) collective-permute-start(bf16[256,384]{1,0:T(8,128)(2,1)S(1)} %convolution_convert_fusion.refs_0_), channel_id=1, source_target_pairs={{0,32},{32,64},{64,96},{96,0},{1,33},{33,65},{65,97},{97,1},{2,34}... | collective-permute-start | bytes 589832 | tf_op jit(solution)/shard_map/ppermute | solution.py:52
  196.1 27.2 %copy-start.23 = (bf16[8,1280]{1,0:T(8,128)(2,1)S(1)}, bf16[8,1280]{1,0:T(8,128)(2,1)}, u32[]{:S(2)}) copy-start(bf16[8,1280]{1,0:T(8,128)(2,1)} %copy-done.22) | copy-start | bytes 61444
  196.1 26.8 %all-to-all-start.4 = ((bf16[32,8,1408]{2,1,0:T(8,128)(2,1)}), bf16[32,8,1408]{2,1,0:T(8,128)(2,1)S(1)}, u32[]{:S(2)}, u32[]{:S(2)}) async-start(bf16[32,8,1408]{2,1,0:T(8,128)(2,1)} %bitcast.10), calls=%async_computation.4 | async-start | bytes 1441792 | tf_op jit(solution)/shard_map/all_to_all | solution.py:47
  245.3 2.0 copy-start.27
  247.3 3.6 %collective-permute-start.19 = (bf16[256,1280]{1,0:T(8,128)(2,1)}, bf16[256,1280]{1,0:T(8,128)(2,1)}, u32[]{:S(2)}, u32[]{:S(2)}) collective-permute-start(bf16[256,1280]{1,0:T(8,128)(2,1)} %bitcast_select_fusion), channel_id=1, source_target_pairs={{0,128},{128,0},{1,129},{129,1},{2,130},{130,2},{3,131},{131,3},{4... | collective-permute-start | bytes 1966088 | tf_op jit(solution)/shard_map/ppermute | solution.py:283
  247.4 3.6 %copy-start.18 = (bf16[512,1280]{1,0:T(8,128)(2,1)S(1)}, bf16[512,1280]{1,0:T(8,128)(2,1)}, u32[]{:S(2)}) copy-start(bf16[512,1280]{1,0:T(8,128)(2,1)} %copy-done.17) | copy-start | bytes 3932164
  253.1 2.9 copy-start.21
  256.5 17.6 %copy-start.19 = (f32[128,1024]{1,0:T(8,128)S(1)}, f32[128,1024]{1,0:T(8,128)}, u32[]{:S(2)}) copy-start(f32[128,1024]{1,0:T(8,128)} %add_add_fusion.1) | copy-start | bytes 1572868
  256.5 17.6 %copy-start.28 = (f32[1,1024]{1,0:T(1,128)S(1)}, f32[1,1024]{1,0:T(1,128)}, u32[]{:S(2)}) copy-start(f32[1,1024]{1,0:T(1,128)} %param.15) | copy-start | bytes 12292
  256.5 10.0 %collective-permute-start.20 = (bf16[128,1152]{1,0:T(8,128)(2,1)S(1)}, bf16[128,1152]{1,0:T(8,128)(2,1)S(1)}, u32[]{:S(2)}, u32[]{:S(2)}) collective-permute-start(bf16[128,1152]{1,0:T(8,128)(2,1)S(1)} %get-tuple-element.52), channel_id=1, source_target_pairs={{0,32},{32,64},{64,96},{96,0},{1,33},{33,65},{65,97},{97,1},{2,34}... | collective-permute-start | bytes 884744 | tf_op jit(solution)/shard_map/ppermute | solution.py:52
  258.0 15.9 %collective-permute-start.22 = (bf16[128,1152]{1,0:T(8,128)(2,1)S(1)}, bf16[128,1152]{1,0:T(8,128)(2,1)S(1)}, u32[]{:S(2)}, u32[]{:S(2)}) collective-permute-start(bf16[128,1152]{1,0:T(8,128)(2,1)S(1)} %get-tuple-element.53), channel_id=1, source_target_pairs={{0,96},{32,0},{64,32},{96,64},{1,97},{33,1},{65,33},{97,65},{2,98}... | collective-permute-start | bytes 884744 | tf_op jit(solution)/shard_map/ppermute | solution.py:52
  258.6 15.2 %collective-permute-start.21 = (bf16[128,1152]{1,0:T(8,128)(2,1)S(1)}, bf16[128,1152]{1,0:T(8,128)(2,1)S(1)}, u32[]{:S(2)}, u32[]{:S(2)}) collective-permute-start(bf16[128,1152]{1,0:T(8,128)(2,1)S(1)} %get-tuple-element.54), channel_id=1, source_target_pairs={{0,64},{32,96},{64,0},{96,32},{1,65},{33,97},{65,1},{97,33},{2,66}... | collective-permute-start | bytes 884744 | tf_op jit(solution)/shard_map/ppermute | solution.py:52
  (9 other events, 6.2 us)

commit v4 on v3

--- a/solution.py
+++ b/solution.py
@@ -154,12 +154,13 @@
             target[:half, :] = dot_t(rows, out_w_ref[...]).astype(BF16)
 
 
-def in_vmem(kernel, out_shape, *args, flops=0):
+def in_vmem(kernel, out_shape, *args, flops=0, scratch=()):
     return pl.pallas_call(
         kernel,
         out_shape=out_shape,
         in_specs=[pl.BlockSpec(memory_space=pltpu.VMEM)] * len(args),
         out_specs=tuple(pl.BlockSpec(memory_space=pltpu.VMEM) for _ in out_shape),
+        scratch_shapes=scratch,
         compiler_params=pltpu.CompilerParams(vmem_limit_bytes=32 * 1024 * 1024),
         cost_estimate=pl.CostEstimate(flops=flops, bytes_accessed=4_000_000, transcendentals=0),
     )(*args)
@@ -173,7 +174,7 @@
     return pl.pallas_call(
         start_kernel,
         out_shape=(jax.ShapeDtypeStruct((width, hid), BF16), part, part),
-        in_specs=[pl.BlockSpec(memory_space=pl.ANY)] * len(args),
+        in_specs=[pl.BlockSpec(memory_space=pltpu.HBM)] * len(args),
         out_specs=(pl.BlockSpec(memory_space=pltpu.VMEM),) * 3,
         scratch_shapes=[pltpu.VMEM(arg.shape, arg.dtype) for arg in args]
         + [pltpu.SemaphoreType.DMA((len(args),))],
@@ -224,10 +225,7 @@
     grad_f = grad_hidden.astype(F32)
     total = jnp.sum(grad_f * sums, axis=1, keepdims=True)
     cross = jnp.sum(grad_f * pre, axis=1, keepdims=True)
-    lane = lax.broadcasted_iota(jnp.int32, (grad_f.shape[0], 128), 1)
-    extra = jnp.zeros(lane.shape, F32)
-    for index, term in enumerate(split3(total) + split3(cross)):
-        extra = jnp.where(lane == index, term.astype(F32), extra)
+    extra = columns_of(split3(total) + split3(cross), grad_f.shape[0])
     y_ref[:, :width] = dot_t(grad_hidden, weight).astype(BF16)
     y_ref[:, width:] = extra.astype(BF16)
 
@@ -245,6 +243,78 @@
     for part in parts[1:]:
         grad_act = grad_act + part[...].astype(F32)
     write_grad(grad_act, hidden_ref[...], pre_ref[...], sums_ref[:1, :], weight_ref[...], y_ref)
+
+
+def columns_of(terms, rows):
+    lane = lax.broadcasted_iota(jnp.int32, (rows, 128), 1)
+    columns = jnp.zeros(lane.shape, F32)
+    for index, term in enumerate(terms):
+        columns = jnp.where(lane == index, term.astype(F32), columns)
+    return columns
+
+
+def expand_kernel(resid_ref, weight_ref, below_ref, part_ref):
+    half, width = resid_ref.shape
+    hid = weight_ref.shape[1]
+    resid = resid_ref[...]
+    resid_f = resid.astype(F32)
+    mean = jnp.sum(resid_f, axis=1, keepdims=True) / width
+    centred = resid_f - mean
+    square = jnp.sum(centred * centred, axis=1, keepdims=True)
+    low = below_ref[half : half + 32, :].astype(F32)
+    column_sum = low[:1] + low[8:9] + low[16:17]
+    part_ref[:half, :] = (dot(resid, weight_ref[...]) - mean * column_sum).astype(BF16)
+    stats = columns_of(split3(mean) + split3(square), half).T[:8]
+    stats = jnp.concatenate([stats, jnp.zeros((8, hid - half), F32)], axis=1)
+    part_ref[half : half + 32, :] = jnp.concatenate([low[:24], stats], axis=0).astype(BF16)
+
+
+def write_copies(rows, rows_ref, copies_ref):
+    rows_ref[...] = rows
+    for place in range(copies_ref.shape[0]):
+        copies_ref[place] = rows
+
+
+def total_of(y_ref):
+    total = y_ref[0].astype(F32)
+    for place in range(1, y_ref.shape[0]):
+        total = total + y_ref[place].astype(F32)
+    return total
+
+
+def share_kernel(y_ref, resid_ref, bias_ref, rows_ref, copies_ref):
+    rows = resid_ref[...] + total_of(y_ref) + bias_ref[...]
+    write_copies(rows.astype(BF16), rows_ref, copies_ref)
+
+
+def norm_kernel(y_ref, columns_ref, resid_ref, grad_ref, rows_ref, copies_ref):
+    width = resid_ref.shape[1]
+    summed = total_of(y_ref)
+    grad_norm, extra = summed[:, :width], summed[:, width:] / D
+    mean_grad = extra[:, :1] + extra[:, 1:2] + extra[:, 2:3]
+    mean_cross = extra[:, 3:4] + extra[:, 4:5] + extra[:, 5:6]
+    inv, mean = columns_ref[:, :1], columns_ref[:, 1:2]
+    normed = (resid_ref[...] - mean) * inv
+    grad_resid = inv * (grad_norm - mean_grad - normed * mean_cross)
+    write_copies((grad_ref[...] + grad_resid).astype(BF16), rows_ref, copies_ref)
+
+
+def effect_kernel(own_ref, rest_ref, resid_ref, weight_ref, bias_ref, *refs):
+    outs, grads_ref = refs[:-1], refs[-1]
+    half = own_ref.shape[0]
+    core, place = lax.axis_index("section"), lax.axis_index("dp")
+    grads_ref[pl.ds(pl.multiple_of(core * half, half), half), :] = own_ref[...]
+    grads_ref[pl.ds(pl.multiple_of((1 - core) * half, half), half), :] = rest_ref[...]
+    latents = weight_ref.shape[0]
+    block = outs[0].shape[0]
+    for by, out in enumerate(outs):
+        start = pl.multiple_of(lax.rem(place + by, len(outs)) * block, block)
+        grad = grads_ref[pl.ds(start, block), :]
+        out[:, :latents] = dot_t(grad, weight_ref[...]).astype(BF16)
+        resid = resid_ref[pl.ds(start, block), :].astype(F32)
+        error = (resid - bias_ref[...]) * grad.astype(F32)
+        error = jnp.sum(error, axis=1, keepdims=True) / lax.axis_size("latent")
+        out[:, latents:] = columns_of(split3(error), block).astype(BF16)
 
 
 def unpack_vectors(part, half):
@@ -328,32 +398,36 @@
         out_w0,
         flops=flops,
     )
-    mlp = exchange(y_0, "latent")
     tokens_rows = own_rows(tokens_half).astype(F32)
-    bias_row = vectors_0[3:7].reshape(-1)[:width]
-    resid_rows = (tokens_rows + jnp.sum(mlp.astype(F32), axis=0) + bias_row[None]).astype(BF16)
+    bias_row = vectors_0[3:7].reshape(1, -1)[:, :width]
+    row_shapes = (
+        jax.ShapeDtypeStruct((share, width), BF16),
+        jax.ShapeDtypeStruct((latent_count, share, width), BF16),
+    )
+    resid_rows, copies = in_vmem(
+        share_kernel, row_shapes, exchange(y_0, "latent"), tokens_rows, bias_row
+    )
     grad_act_1 = total_ring(part_grad[:half], "dp")
-    resid_rows, grad_act_1 = lax.optimization_barrier((resid_rows, grad_act_1))
-    resid_half = spread(resid_rows, "latent").reshape(half, width)
-
-    local_mean, square = row_parts(resid_half)
-    part_1 = dot(resid_half, gained_1) - local_mean[:, None] * vectors_1[0][None]
-    part_1 = jnp.concatenate([part_1.astype(BF16), part_grad[half:]], axis=0)
+    copies, grad_act_1 = lax.optimization_barrier((copies, grad_act_1))
+    resid_half = lax.all_to_all(copies, "latent", 0, 0).reshape(half, width)
+
+    (part_1,) = in_vmem(
+        expand_kernel,
+        (jax.ShapeDtypeStruct((half + 32, hid), BF16),),
+        resid_half,
+        gained_1,
+        part_grad,
+        flops=flops,
+    )
     resid_there = other(resid_half)
-    parts_1 = gather_ring(with_stats(part_1, local_mean, square), "dp")
+    parts_1 = gather_ring(part_1, "dp")
     parts_1, resid_there = lax.optimization_barrier((parts_1, resid_there))
 
     def norm_grad(y, columns, resid, grad_rows):
-        summed = jnp.sum(exchange(y, "latent").astype(F32), axis=0)
-        grad_norm, extra = summed[:, :width], summed[:, width : width + 6] / D
-        mean_grad = (extra[:, 0] + extra[:, 1] + extra[:, 2])[:, None]
-        mean_cross = (extra[:, 3] + extra[:, 4] + extra[:, 5])[:, None]
-        columns = own_rows(columns)
-        inv, mean = columns[:, :1], columns[:, 1:2]
-        normed = (resid - mean) * inv
-        grad_resid = inv * (grad_norm - mean_grad - normed * mean_cross)
-        new_rows = (grad_rows + grad_resid).astype(BF16)
-        return new_rows, spread(new_rows, "latent").reshape(half, width)
+        rows, copies = in_vmem(
+            norm_kernel, row_shapes, exchange(y, "latent"), own_rows(columns), resid, grad_rows
+        )
+        return rows, lax.all_to_all(copies, "latent", 0, 0).reshape(half, width)
 
     y_1, columns_1 = in_vmem(
         turn_kernel, (grad_shape, columns_shape), *parts_1, grad_act_1, gained_1, flops=flops
@@ -370,19 +444,20 @@
     _, grad_half_0 = norm_grad(y_2, columns_0, tokens_rows, grad_rows_1.astype(F32))
 
     codes = jnp.maximum(pre_codes + enc_bias[0][None], 0.0).astype(BF16)
-    resid_own = lax.dynamic_slice_in_dim(resid_all, core * half, half, 0)
-    resid_rest = lax.dynamic_slice_in_dim(resid_all, (1 - core) * half, half, 0)
-
-    def attributed(grad, resid):
-        error = (resid.astype(F32) - dec_bias[0][None]) * grad.astype(F32)
-        error = jnp.stack(split3(jnp.sum(error, axis=1) / latent_count), axis=1)
-        error = jnp.pad(error, ((0, 0), (0, 128 - error.shape[1])))
-        return jnp.concatenate([dot_t(grad, dec_weight[0]).astype(BF16), error], axis=1)
-
-    rest = attributed(other(pick(grad_half_1, grad_half_0)), resid_rest)
-    own = attributed(pick(grad_half_0, grad_half_1), resid_own)
-    parts = pick(jnp.concatenate([own, rest], axis=0), jnp.concatenate([rest, own], axis=0))
-    summed = scatter_ring(parts, "dp")
+    parts = in_vmem(
+        effect_kernel,
+        (jax.ShapeDtypeStruct((block, codes.shape[1] + 128), BF16),) * dp_count,
+        pick(grad_half_0, grad_half_1),
+        other(pick(grad_half_1, grad_half_0)),
+        resid_all,
+        dec_weight[0],
+        dec_bias,
+        flops=2 * all_rows * width * codes.shape[1],
+        scratch=[pltpu.VMEM((all_rows, width), BF16)],
+    )
+    summed = parts[0].astype(F32) + sum(
+        turn(parts[by], "dp", by).astype(F32) for by in range(1, dp_count)
+    )
     latents = codes.shape[1]
     effect = codes.astype(F32) * summed[:, :latents]
     error = jnp.sum(summed[:, latents : latents + 3], axis=1) - jnp.sum(effect, axis=1)

time: 291 us -> 287 us (0.986)
  other arithmetic: 31.7 us -> 17.6 us
  waiting for transfers between devices: 110 us -> 122 us
  matrix products: 12 us -> 3.6 us
  Pallas kernels: 6.64 us -> 11.6 us
  local copies, waits for them, and re-layouts: 25.7 us -> 21.3 us
  blocking collectives: 34.9 us -> 38.9 us
    all_to_all x0 -> x1, blocking collectives: none -> 24.6 us  [norm_grad(): return (rows, lax.all_to_all(copies, 'latent', 0, 0).reshape(half, width))]
    all_to_all x2 -> x1, blocking collectives: 34.9 us -> 14.3 us  [spread(): return lax.all_to_all(copies, axis, 0, 0)]
    dot_general x3 -> x1, matrix products: 8.43 us -> 2.04 us  [dot_t(): lax.dot_general(left, right, CONTRACT_LAST, preferred_element_type=F32)]
    unnamed x58 -> x75, local copies, waits for them, and re-layouts: 13.6 us -> 19.8 us
    all_to_all x3, waiting for transfers between devices: 40.3 us -> 46.5 us  [exchange(): lax.all_to_all(values.reshape(count, rows, values.shape[1]), axis, 0, 0)]
    pallas_call x3 -> x8, Pallas kernels: 4.26 us -> 9.18 us  [in_vmem(): pl.pallas_call(kernel, out_shape=out_shape, in_specs=[pl.BlockSpec(memory...]
    all_to_all x2, waiting for transfers between devices: 14.8 us -> 19.3 us  [the longest x1 19.3 us: on_device(): resid_half = lax.all_to_all(copies, 'latent', 0, 0).reshape(half, width)]
    reduce_sum x4 -> x0, other arithmetic: 4.24 us -> none  [the longest x1 1.71 us: attributed(): error = jnp.stack(split3(jnp.sum(error, axis=1) / latent_count), axis=1)]
  transfers between devices with their start and end apart: 28 -> 28, of which waited for: 19 -> 23; matrix products, arithmetic and copies ran while one was open for 11% -> 6% of each run, Pallas kernels for 1% -> 1%
where the time goes in v4:
time: 287 us; the launch traced here: 284 us
  waiting for transfers between devices  122 us (43%)
  starting transfers between devices  67.6 us (24%)
  blocking collectives  38.9 us (14%)
  local copies, waits for them, and re-layouts  21.3 us (7%)
  other arithmetic  17.6 us (6%)
  Pallas kernels  11.6 us (4%)
  matrix products  3.6 us (1%)
    ppermute x18, waiting for transfers between devices, turn(): lax.ppermute(values, axis, [(i, (i + by) % count) for i in range(count)])  54 us
    all_to_all x3, waiting for transfers between devices, exchange(): lax.all_to_all(values.reshape(count, rows, values.shape[1]), axis, 0, 0)  46.5 us
    ppermute x18, starting transfers between devices, turn(): lax.ppermute(values, axis, [(i, (i + by) % count) for i in range(count)])  31.5 us
    all_to_all x3, starting transfers between devices, exchange(): lax.all_to_all(values.reshape(count, rows, values.shape[1]), axis, 0, 0)  25 us
    all_to_all x1, blocking collectives, norm_grad(): return (rows, lax.all_to_all(copies, 'latent', 0, 0).reshape(half, width))  24.6 us
    unnamed x75, local copies, waits for them, and re-layouts  19.8 us
    all_to_all x1, waiting for transfers between devices, on_device(): resid_half = lax.all_to_all(copies, 'latent', 0, 0).reshape(half, width)  19.3 us
    all_to_all x1, blocking collectives, spread(): return lax.all_to_all(copies, axis, 0, 0)  14.3 us
  transfers between devices with their start and end apart: 28, of which 23 were waited for; matrix products, arithmetic and copies ran while one was open for 6% of the time, Pallas kernels for 1%

profile of v4, /device:TPU:8, one launch (start us, length us, event | category | flops | bytes accessed | tf_op | source)
XLA Modules:
  0.0 283.6 jit_solution(10617919399685083895)
XLA Ops:
  0.8 1.5 copy-done.1
  8.7 2.4 shard_map.131
  13.7 1.4 fusion.6
  16.9 1.7 collective-permute-start.1
  18.5 2.6 collective-permute-start.2
  23.2 2.1 collective-permute-done.1.refs_1_
  25.3 3.1 %collective-permute-done.2.refs_2_ = bf16[288,384]{1,0:T(8,128)(2,1)S(1)} collective-permute-done((bf16[288,384]{1,0:T(8,128)(2,1)S(1)}, bf16[288,384]{1,0:T(8,128)(2,1)S(1)}, u32[]{:S(2)}, u32[]{:S(2)}) %collective-permute-start.2) | collective-permute-done | bytes 221216 | tf_op jit(solution)/shard_map/ppermute | solution.py:52
  28.4 3.6 %collective-permute-done.3.refs_3_ = bf16[288,384]{1,0:T(8,128)(2,1)S(1)} collective-permute-done((bf16[288,384]{1,0:T(8,128)(2,1)S(1)}, bf16[288,384]{1,0:T(8,128)(2,1)S(1)}, u32[]{:S(2)}, u32[]{:S(2)}) %collective-permute-start.3) | collective-permute-done | bytes 221216 | tf_op jit(solution)/shard_map/ppermute | solution.py:52
  37.4 10.6 %all-to-all-start = ((bf16[32,8,1280]{2,1,0:T(8,128)(2,1)}), bf16[32,8,1280]{2,1,0:T(8,128)(2,1)S(1)}, u32[]{:S(2)}, u32[]{:S(2)}) async-start(bf16[32,8,1280]{2,1,0:T(8,128)(2,1)} %bitcast.40), calls=%async_computation | async-start | bytes 1310720 | tf_op jit(solution)/shard_map/all_to_all | solution.py:47
  49.8 2.0 collective-permute-start.6
  51.7 1.7 collective-permute-start.5
  54.2 1.9 collective-permute-done.7
  56.0 3.7 %collective-permute-done.6 = bf16[256,384]{1,0:T(8,128)(2,1)S(1)} collective-permute-done((bf16[256,384]{1,0:T(8,128)(2,1)S(1)}, bf16[256,384]{1,0:T(8,128)(2,1)S(1)}, u32[]{:S(2)}, u32[]{:S(2)}) %collective-permute-start.6) | collective-permute-done | bytes 196640 | tf_op jit(solution)/shard_map/ppermute | solution.py:52
  61.7 6.1 %all-to-all-done.y_ref = bf16[32,8,1280]{2,1,0:T(8,128)(2,1)S(1)} async-done(((bf16[32,8,1280]{2,1,0:T(8,128)(2,1)}), bf16[32,8,1280]{2,1,0:T(8,128)(2,1)S(1)}, u32[]{:S(2)}, u32[]{:S(2)}) %all-to-all-start) | async-done | bytes 655392 | tf_op jit(solution)/shard_map/all_to_all | solution.py:47
  69.4 5.0 %all-to-all-start.1 = ((bf16[32,8,1280]{2,1,0:T(8,128)(2,1)}), bf16[32,8,1280]{2,1,0:T(8,128)(2,1)S(1)}, u32[]{:S(2)}, u32[]{:S(2)}) async-start(bf16[32,8,1280]{2,1,0:T(8,128)(2,1)} %copy-done.17), calls=%async_computation.1 | async-start | bytes 1310720 | tf_op jit(solution)/shard_map/all_to_all | solution.py:412
  74.4 19.3 %all-to-all-done.1 = bf16[32,8,1280]{2,1,0:T(8,128)(2,1)S(1)} async-done(((bf16[32,8,1280]{2,1,0:T(8,128)(2,1)}), bf16[32,8,1280]{2,1,0:T(8,128)(2,1)S(1)}, u32[]{:S(2)}, u32[]{:S(2)}) %all-to-all-start.1) | async-done | bytes 655392 | tf_op jit(solution)/shard_map/all_to_all | solution.py:412
  93.7 2.6 broadcast_select_fusion
  98.3 3.2 %collective-permute-start.10 = (bf16[288,384]{1,0:T(8,128)(2,1)S(1)}, bf16[288,384]{1,0:T(8,128)(2,1)S(1)}, u32[]{:S(2)}, u32[]{:S(2)}) collective-permute-start(bf16[288,384]{1,0:T(8,128)(2,1)S(1)} %shard_map.134.refs_0_), channel_id=1, source_target_pairs={{0,64},{32,96},{64,0},{96,32},{1,65},{33,97},{65,1},{97,33},{2,66}... | collective-permute-start | bytes 663560 | tf_op jit(solution)/shard_map/ppermute | solution.py:52
  102.4 3.3 %collective-permute-done.9.refs_1_ = bf16[288,384]{1,0:T(8,128)(2,1)S(1)} collective-permute-done((bf16[288,384]{1,0:T(8,128)(2,1)S(1)}, bf16[288,384]{1,0:T(8,128)(2,1)S(1)}, u32[]{:S(2)}, u32[]{:S(2)}) %collective-permute-start.9) | collective-permute-done | bytes 221216 | tf_op jit(solution)/shard_map/ppermute | solution.py:52
  105.8 2.4 collective-permute-done.10.refs_2_
  108.1 4.0 %collective-permute-done.11.refs_3_ = bf16[288,384]{1,0:T(8,128)(2,1)S(1)} collective-permute-done((bf16[288,384]{1,0:T(8,128)(2,1)S(1)}, bf16[288,384]{1,0:T(8,128)(2,1)S(1)}, u32[]{:S(2)}, u32[]{:S(2)}) %collective-permute-start.11) | collective-permute-done | bytes 221216 | tf_op jit(solution)/shard_map/ppermute | solution.py:52
  114.6 5.2 %all-to-all-start.2 = ((bf16[32,8,1408]{2,1,0:T(8,128)(2,1)}), bf16[32,8,1408]{2,1,0:T(8,128)(2,1)}, u32[]{:S(2)}, u32[]{:S(2)}) async-start(bf16[32,8,1408]{2,1,0:T(8,128)(2,1)} %bitcast.39), calls=%async_computation.2 | async-start | bytes 1441792 | tf_op jit(solution)/shard_map/all_to_all | solution.py:47
  121.4 20.1 %all-to-all-done.2.y_ref = bf16[32,8,1408]{2,1,0:T(8,128)(2,1)} async-done(((bf16[32,8,1408]{2,1,0:T(8,128)(2,1)}), bf16[32,8,1408]{2,1,0:T(8,128)(2,1)}, u32[]{:S(2)}, u32[]{:S(2)}) %all-to-all-start.2) | async-done | bytes 720928 | tf_op jit(solution)/shard_map/all_to_all | solution.py:47
  141.5 1.3 shard_map.136
  143.7 5.2 %all-to-all-start.3 = ((bf16[32,8,1280]{2,1,0:T(8,128)(2,1)}), bf16[32,8,1280]{2,1,0:T(8,128)(2,1)}, u32[]{:S(2)}, u32[]{:S(2)}) async-start(bf16[32,8,1280]{2,1,0:T(8,128)(2,1)} %copy-done.15), calls=%async_computation.3 | async-start | bytes 1310720 | tf_op jit(solution)/shard_map/all_to_all | solution.py:430
  149.0 1.8 maximum_select_fusion.resid_ref
  150.8 1.6 fusion.2
  154.5 1.5 collective-permute-start.14
  156.0 2.6 collective-permute-start.13
  158.7 3.0 %collective-permute-done.15 = bf16[128,1024]{1,0:T(8,128)(2,1)} collective-permute-done((bf16[128,1024]{1,0:T(8,128)(2,1)S(1)}, bf16[128,1024]{1,0:T(8,128)(2,1)}, u32[]{:S(2)}, u32[]{:S(2)}) %collective-permute-start.15) | collective-permute-done | bytes 262176 | tf_op jit(solution)/shard_map/ppermute | solution.py:52
  161.7 4.6 %collective-permute-done.14 = bf16[128,1024]{1,0:T(8,128)(2,1)} collective-permute-done((bf16[128,1024]{1,0:T(8,128)(2,1)S(1)}, bf16[128,1024]{1,0:T(8,128)(2,1)}, u32[]{:S(2)}, u32[]{:S(2)}) %collective-permute-start.14) | collective-permute-done | bytes 262176 | tf_op jit(solution)/shard_map/ppermute | solution.py:52
  167.3 2.2 add_add_fusion.1
  169.5 2.0 convolution_convert_fusion.refs_0_
  171.5 1.5 collective-permute-start.16
  173.0 3.6 %collective-permute-start.17 = (bf16[256,384]{1,0:T(8,128)(2,1)S(1)}, bf16[256,384]{1,0:T(8,128)(2,1)S(1)}, u32[]{:S(2)}, u32[]{:S(2)}) collective-permute-start(bf16[256,384]{1,0:T(8,128)(2,1)S(1)} %convolution_convert_fusion.refs_0_), channel_id=1, source_target_pairs={{0,64},{32,96},{64,0},{96,32},{1,65},{33,97},{65,1},{97,33},{2,66}... | collective-permute-start | bytes 589832 | tf_op jit(solution)/shard_map/ppermute | solution.py:52
  176.8 3.5 %collective-permute-done.16.refs_1_ = bf16[256,384]{1,0:T(8,128)(2,1)S(1)} collective-permute-done((bf16[256,384]{1,0:T(8,128)(2,1)S(1)}, bf16[256,384]{1,0:T(8,128)(2,1)S(1)}, u32[]{:S(2)}, u32[]{:S(2)}) %collective-permute-start.16) | collective-permute-done | bytes 196640 | tf_op jit(solution)/shard_map/ppermute | solution.py:52
  180.3 2.1 collective-permute-done.17.refs_2_
  182.4 2.7 collective-permute-done.18.refs_3_
  186.8 9.2 %all-to-all-start.4 = ((bf16[32,8,1408]{2,1,0:T(8,128)(2,1)}), bf16[32,8,1408]{2,1,0:T(8,128)(2,1)S(1)}, u32[]{:S(2)}, u32[]{:S(2)}) async-start(bf16[32,8,1408]{2,1,0:T(8,128)(2,1)} %bitcast.36), calls=%async_computation.4 | async-start | bytes 1441792 | tf_op jit(solution)/shard_map/all_to_all | solution.py:47
  196.6 20.3 %all-to-all-done.4.y_ref = bf16[32,8,1408]{2,1,0:T(8,128)(2,1)S(1)} async-done(((bf16[32,8,1408]{2,1,0:T(8,128)(2,1)}), bf16[32,8,1408]{2,1,0:T(8,128)(2,1)S(1)}, u32[]{:S(2)}, u32[]{:S(2)}) %all-to-all-start.4) | async-done | bytes 720928 | tf_op jit(solution)/shard_map/all_to_all | solution.py:47
  217.7 24.6 %all_to_all.35 = bf16[32,8,1280]{2,1,0:T(8,128)(2,1)S(1)} all-to-all(bf16[32,8,1280]{2,1,0:T(8,128)(2,1)S(1)} %get-tuple-element.53), channel_id=1, replica_groups=mesh['section'=2,'dp'=4,'latent'=32] {'latent'}, dimensions={0} | all-to-all | bytes 1310720 | tf_op jit(solution)/shard_map/all_to_all | solution.py:430
  244.0 2.1 collective-permute-done.19.rest_ref
  246.1 3.7 %shard_map.139 = (bf16[128,1152]{1,0:T(8,128)(2,1)S(1)}, bf16[128,1152]{1,0:T(8,128)(2,1)S(1)}, bf16[128,1152]{1,0:T(8,128)(2,1)S(1)}, bf16[128,1152]{1,0:T(8,128)(2,1)S(1)}) custom-call(bf16[256,1280]{1,0:T(8,128)(2,1)S(1)} %get-tuple-element.61.own_ref, bf16[256,1280]{1,0:T(8,128)(2,1)S(1)} %collective-permute-done.19.rest_ref, ...), custom_call_target="tpu_custom_call" | custom-call | flops 1342177280 | bytes 4000000 | tf_op jit(solution)/shard_map/pallas_call | solution.py:158
  250.6 2.6 collective-permute-start.21
  253.2 2.5 collective-permute-start.20
  255.7 3.2 %collective-permute-done.22 = bf16[128,1152]{1,0:T(8,128)(2,1)S(1)} collective-permute-done((bf16[128,1152]{1,0:T(8,128)(2,1)S(1)}, bf16[128,1152]{1,0:T(8,128)(2,1)S(1)}, u32[]{:S(2)}, u32[]{:S(2)}) %collective-permute-start.22) | collective-permute-done | bytes 294944 | tf_op jit(solution)/shard_map/ppermute | solution.py:52
  258.9 7.8 %collective-permute-done.21 = bf16[128,1152]{1,0:T(8,128)(2,1)S(1)} collective-permute-done((bf16[128,1152]{1,0:T(8,128)(2,1)S(1)}, bf16[128,1152]{1,0:T(8,128)(2,1)S(1)}, u32[]{:S(2)}, u32[]{:S(2)}) %collective-permute-start.21) | collective-permute-done | bytes 294944 | tf_op jit(solution)/shard_map/ppermute | solution.py:52
  268.7 14.3 %all_to_all.36 = f32[32,1,128]{2,1,0:T(1,128)S(1)} all-to-all(f32[32,1,128]{2,1,0:T(1,128)S(1)} %broadcast_in_dim.13), channel_id=1, replica_groups=mesh['section'=2,'dp'=4,'latent'=32] {'latent'}, dimensions={0} | all-to-all | bytes 32768 | tf_op jit(solution)/shard_map/all_to_all | solution.py:41
  (128 shorter events, 43.3 us)
Async XLA Ops:
  0.6 150.1 %copy-start = (bf16[1,1280,1024]{2,1,0:T(8,128)(2,1)S(1)}, bf16[1,1280,1024]{2,1,0:T(8,128)(2,1)}, u32[]{:S(2)}) copy-start(bf16[1,1280,1024]{2,1,0:T(8,128)(2,1)} %param.14) | copy-start | bytes 7864324
  0.6 21.2 %collective-permute-start.4 = (bf16[384,1280]{1,0:T(8,128)(2,1)}, bf16[384,1280]{1,0:T(8,128)(2,1)}, u32[]{:S(2)}, u32[]{:S(2)}) collective-permute-start(bf16[384,1280]{1,0:T(8,128)(2,1)} %bitcast.34), channel_id=1, source_target_pairs={{0,128},{128,0},{1,129},{129,1},{2,130},{130,2},{3,131},{131,3},{4... | collective-permute-start | bytes 2949128 | tf_op jit(solution)/shard_map/ppermute | solution.py:353
  0.8 1.5 copy-start.1
  2.2 1.2 copy-start.5
  3.4 1.3 copy-start.10
  4.7 1.2 copy-start.11
  12.0 3.1 %collective-permute-start = (bf16[288,384]{1,0:T(8,128)(2,1)S(1)}, bf16[288,384]{1,0:T(8,128)(2,1)S(1)}, u32[]{:S(2)}, u32[]{:S(2)}) collective-permute-start(bf16[288,384]{1,0:T(8,128)(2,1)S(1)} %get-tuple-element.31), channel_id=1, source_target_pairs={{0,128},{128,0},{1,129},{129,1},{2,130},{130,2},{3,131},{131,3},{4... | collective-permute-start | bytes 663560 | tf_op jit(solution)/shard_map/ppermute | solution.py:353
  16.9 15.1 %copy-start.13 = (bf16[288,384]{1,0:T(8,128)(2,1)}, bf16[288,384]{1,0:T(8,128)(2,1)S(1)}, u32[]{:S(2)}) copy-start(bf16[288,384]{1,0:T(8,128)(2,1)S(1)} %get-tuple-element.68.refs_0_) | copy-start | bytes 663556
  16.9 8.4 %collective-permute-start.1 = (bf16[288,384]{1,0:T(8,128)(2,1)S(1)}, bf16[288,384]{1,0:T(8,128)(2,1)S(1)}, u32[]{:S(2)}, u32[]{:S(2)}) collective-permute-start(bf16[288,384]{1,0:T(8,128)(2,1)S(1)} %get-tuple-element.68.refs_0_), channel_id=1, source_target_pairs={{0,32},{32,64},{64,96},{96,0},{1,33},{33,65},{65,97},{97,1},{2,34}... | collective-permute-start | bytes 663560 | tf_op jit(solution)/shard_map/ppermute | solution.py:52
  18.5 9.9 %collective-permute-start.2 = (bf16[288,384]{1,0:T(8,128)(2,1)S(1)}, bf16[288,384]{1,0:T(8,128)(2,1)S(1)}, u32[]{:S(2)}, u32[]{:S(2)}) collective-permute-start(bf16[288,384]{1,0:T(8,128)(2,1)S(1)} %get-tuple-element.68.refs_0_), channel_id=1, source_target_pairs={{0,64},{32,96},{64,0},{96,32},{1,65},{33,97},{65,1},{97,33},{2,66}... | collective-permute-start | bytes 663560 | tf_op jit(solution)/shard_map/ppermute | solution.py:52
  21.2 10.8 %collective-permute-start.3 = (bf16[288,384]{1,0:T(8,128)(2,1)S(1)}, bf16[288,384]{1,0:T(8,128)(2,1)S(1)}, u32[]{:S(2)}, u32[]{:S(2)}) collective-permute-start(bf16[288,384]{1,0:T(8,128)(2,1)S(1)} %get-tuple-element.68.refs_0_), channel_id=1, source_target_pairs={{0,96},{32,0},{64,32},{96,64},{1,97},{33,1},{65,33},{97,65},{2,98}... | collective-permute-start | bytes 663560 | tf_op jit(solution)/shard_map/ppermute | solution.py:52
  32.8 1.0 copy-start.2
  37.4 30.3 %all-to-all-start = ((bf16[32,8,1280]{2,1,0:T(8,128)(2,1)}), bf16[32,8,1280]{2,1,0:T(8,128)(2,1)S(1)}, u32[]{:S(2)}, u32[]{:S(2)}) async-start(bf16[32,8,1280]{2,1,0:T(8,128)(2,1)} %bitcast.40), calls=%async_computation | async-start | bytes 1310720 | tf_op jit(solution)/shard_map/all_to_all | solution.py:47
  48.9 7.1 %collective-permute-start.7 = (bf16[256,384]{1,0:T(8,128)(2,1)S(1)}, bf16[256,384]{1,0:T(8,128)(2,1)S(1)}, u32[]{:S(2)}, u32[]{:S(2)}) collective-permute-start(bf16[256,384]{1,0:T(8,128)(2,1)S(1)} %slice.44), channel_id=1, source_target_pairs={{0,96},{32,0},{64,32},{96,64},{1,97},{33,1},{65,33},{97,65},{2,98}... | collective-permute-start | bytes 589832 | tf_op jit(solution)/shard_map/ppermute | solution.py:52
  49.8 10.0 %collective-permute-start.6 = (bf16[256,384]{1,0:T(8,128)(2,1)S(1)}, bf16[256,384]{1,0:T(8,128)(2,1)S(1)}, u32[]{:S(2)}, u32[]{:S(2)}) collective-permute-start(bf16[256,384]{1,0:T(8,128)(2,1)S(1)} %slice.44), channel_id=1, source_target_pairs={{0,64},{32,96},{64,0},{96,32},{1,65},{33,97},{65,1},{97,33},{2,66}... | collective-permute-start | bytes 589832 | tf_op jit(solution)/shard_map/ppermute | solution.py:52
  51.7 9.1 %collective-permute-start.5 = (bf16[256,384]{1,0:T(8,128)(2,1)S(1)}, bf16[256,384]{1,0:T(8,128)(2,1)S(1)}, u32[]{:S(2)}, u32[]{:S(2)}) collective-permute-start(bf16[256,384]{1,0:T(8,128)(2,1)S(1)} %slice.44), channel_id=1, source_target_pairs={{0,32},{32,64},{64,96},{96,0},{1,33},{33,65},{65,97},{97,1},{2,34}... | collective-permute-start | bytes 589832 | tf_op jit(solution)/shard_map/ppermute | solution.py:52
  69.4 24.4 %all-to-all-start.1 = ((bf16[32,8,1280]{2,1,0:T(8,128)(2,1)}), bf16[32,8,1280]{2,1,0:T(8,128)(2,1)S(1)}, u32[]{:S(2)}, u32[]{:S(2)}) async-start(bf16[32,8,1280]{2,1,0:T(8,128)(2,1)} %copy-done.17), calls=%async_computation.1 | async-start | bytes 1310720 | tf_op jit(solution)/shard_map/all_to_all | solution.py:412
  74.3 19.4 %collective-permute-start.8 = (bf16[1280,384]{1,0:T(8,128)(2,1)}, bf16[1280,384]{1,0:T(8,128)(2,1)}, u32[]{:S(2)}, u32[]{:S(2)}) collective-permute-start(bf16[1280,384]{1,0:T(8,128)(2,1)} %copy-done.12), channel_id=1, source_target_pairs={{0,128},{128,0},{1,129},{129,1},{2,130},{130,2},{3,131},{131,3},{4... | collective-permute-start | bytes 2949128 | tf_op jit(solution)/shard_map/ppermute | solution.py:353
  93.7 18.4 %collective-permute-start.12 = (bf16[256,1280]{1,0:T(8,128)(2,1)S(1)}, bf16[256,1280]{1,0:T(8,128)(2,1)}, u32[]{:S(2)}, u32[]{:S(2)}) collective-permute-start(bf16[256,1280]{1,0:T(8,128)(2,1)S(1)} %bitcast.31), channel_id=1, source_target_pairs={{0,128},{128,0},{1,129},{129,1},{2,130},{130,2},{3,131},{131,3},{4... | collective-permute-start | bytes 1966088 | tf_op jit(solution)/shard_map/ppermute | solution.py:353
  96.4 15.8 %copy-start.9 = (f32[256,384]{1,0:T(8,128)S(1)}, f32[256,384]{1,0:T(8,128)}, u32[]{:S(2)}) copy-start(f32[256,384]{1,0:T(8,128)} %convert_add_fusion.refs_4_) | copy-start | bytes 1179652
  97.0 8.7 %collective-permute-start.9 = (bf16[288,384]{1,0:T(8,128)(2,1)S(1)}, bf16[288,384]{1,0:T(8,128)(2,1)S(1)}, u32[]{:S(2)}, u32[]{:S(2)}) collective-permute-start(bf16[288,384]{1,0:T(8,128)(2,1)S(1)} %shard_map.134.refs_0_), channel_id=1, source_target_pairs={{0,32},{32,64},{64,96},{96,0},{1,33},{33,65},{65,97},{97,1},{2,34}... | collective-permute-start | bytes 663560 | tf_op jit(solution)/shard_map/ppermute | solution.py:52
  98.3 9.8 %collective-permute-start.10 = (bf16[288,384]{1,0:T(8,128)(2,1)S(1)}, bf16[288,384]{1,0:T(8,128)(2,1)S(1)}, u32[]{:S(2)}, u32[]{:S(2)}) collective-permute-start(bf16[288,384]{1,0:T(8,128)(2,1)S(1)} %shard_map.134.refs_0_), channel_id=1, source_target_pairs={{0,64},{32,96},{64,0},{96,32},{1,65},{33,97},{65,1},{97,33},{2,66}... | collective-permute-start | bytes 663560 | tf_op jit(solution)/shard_map/ppermute | solution.py:52
  101.5 10.6 %collective-permute-start.11 = (bf16[288,384]{1,0:T(8,128)(2,1)S(1)}, bf16[288,384]{1,0:T(8,128)(2,1)S(1)}, u32[]{:S(2)}, u32[]{:S(2)}) collective-permute-start(bf16[288,384]{1,0:T(8,128)(2,1)S(1)} %shard_map.134.refs_0_), channel_id=1, source_target_pairs={{0,96},{32,0},{64,32},{96,64},{1,97},{33,1},{65,33},{97,65},{2,98}... | collective-permute-start | bytes 663560 | tf_op jit(solution)/shard_map/ppermute | solution.py:52
  114.6 6.1 %copy-start.23 = (bf16[8,1280]{1,0:T(8,128)(2,1)S(1)}, bf16[8,1280]{1,0:T(8,128)(2,1)}, u32[]{:S(2)}) copy-start(bf16[8,1280]{1,0:T(8,128)(2,1)} %copy-done.22) | copy-start | bytes 61444
  114.6 26.9 %all-to-all-start.2 = ((bf16[32,8,1408]{2,1,0:T(8,128)(2,1)}), bf16[32,8,1408]{2,1,0:T(8,128)(2,1)}, u32[]{:S(2)}, u32[]{:S(2)}) async-start(bf16[32,8,1408]{2,1,0:T(8,128)(2,1)} %bitcast.39), calls=%async_computation.2 | async-start | bytes 1441792 | tf_op jit(solution)/shard_map/all_to_all | solution.py:47
  143.7 25.7 %all-to-all-start.3 = ((bf16[32,8,1280]{2,1,0:T(8,128)(2,1)}), bf16[32,8,1280]{2,1,0:T(8,128)(2,1)}, u32[]{:S(2)}, u32[]{:S(2)}) async-start(bf16[32,8,1280]{2,1,0:T(8,128)(2,1)} %copy-done.15), calls=%async_computation.3 | async-start | bytes 1310720 | tf_op jit(solution)/shard_map/all_to_all | solution.py:430
  150.8 1.6 copy-start.3
  152.4 1.0 copy-start.34
  153.3 8.3 %collective-permute-start.15 = (bf16[128,1024]{1,0:T(8,128)(2,1)S(1)}, bf16[128,1024]{1,0:T(8,128)(2,1)}, u32[]{:S(2)}, u32[]{:S(2)}) collective-permute-start(bf16[128,1024]{1,0:T(8,128)(2,1)S(1)} %get-tuple-element.65), channel_id=1, source_target_pairs={{0,96},{32,0},{64,32},{96,64},{1,97},{33,1},{65,33},{97,65},{2,98}... | collective-permute-start | bytes 786440 | tf_op jit(solution)/shard_map/ppermute | solution.py:52
  154.5 11.8 %collective-permute-start.14 = (bf16[128,1024]{1,0:T(8,128)(2,1)S(1)}, bf16[128,1024]{1,0:T(8,128)(2,1)}, u32[]{:S(2)}, u32[]{:S(2)}) collective-permute-start(bf16[128,1024]{1,0:T(8,128)(2,1)S(1)} %get-tuple-element.66), channel_id=1, source_target_pairs={{0,64},{32,96},{64,0},{96,32},{1,65},{33,97},{65,1},{97,33},{2,66}... | collective-permute-start | bytes 786440 | tf_op jit(solution)/shard_map/ppermute | solution.py:52
  156.0 11.3 %collective-permute-start.13 = (bf16[128,1024]{1,0:T(8,128)(2,1)S(1)}, bf16[128,1024]{1,0:T(8,128)(2,1)}, u32[]{:S(2)}, u32[]{:S(2)}) collective-permute-start(bf16[128,1024]{1,0:T(8,128)(2,1)S(1)} %get-tuple-element.64), channel_id=1, source_target_pairs={{0,32},{32,64},{64,96},{96,0},{1,33},{33,65},{65,97},{97,1},{2,34}... | collective-permute-start | bytes 786440 | tf_op jit(solution)/shard_map/ppermute | solution.py:52
  169.4 15.7 %copy-start.19 = (f32[256,384]{1,0:T(8,128)S(1)}, f32[256,384]{1,0:T(8,128)}, u32[]{:S(2)}) copy-start(f32[256,384]{1,0:T(8,128)} %copy-done.18) | copy-start | bytes 1179652
  169.4 15.7 %copy-start.21 = (f32[256,384]{1,0:T(8,128)S(1)}, f32[256,384]{1,0:T(8,128)}, u32[]{:S(2)}) copy-start(f32[256,384]{1,0:T(8,128)} %copy-done.20) | copy-start | bytes 1179652
  169.4 15.7 %copy-start.25 = (f32[8,384]{1,0:T(8,128)S(1)}, f32[8,384]{1,0:T(8,128)}, u32[]{:S(2)}) copy-start(f32[8,384]{1,0:T(8,128)} %copy-done.24) | copy-start | bytes 36868
  169.4 15.7 %copy-start.6 = (bf16[1280,384]{1,0:T(8,128)(2,1)S(1)}, bf16[1280,384]{1,0:T(8,128)(2,1)}, u32[]{:S(2)}) copy-start(bf16[1280,384]{1,0:T(8,128)(2,1)} %get-tuple-element.58.refs_7_) | copy-start | bytes 2949124
  171.5 8.8 %collective-permute-start.16 = (bf16[256,384]{1,0:T(8,128)(2,1)S(1)}, bf16[256,384]{1,0:T(8,128)(2,1)S(1)}, u32[]{:S(2)}, u32[]{:S(2)}) collective-permute-start(bf16[256,384]{1,0:T(8,128)(2,1)S(1)} %convolution_convert_fusion.refs_0_), channel_id=1, source_target_pairs={{0,32},{32,64},{64,96},{96,0},{1,33},{33,65},{65,97},{97,1},{2,34}... | collective-permute-start | bytes 589832 | tf_op jit(solution)/shard_map/ppermute | solution.py:52
  173.0 9.4 %collective-permute-start.17 = (bf16[256,384]{1,0:T(8,128)(2,1)S(1)}, bf16[256,384]{1,0:T(8,128)(2,1)S(1)}, u32[]{:S(2)}, u32[]{:S(2)}) collective-permute-start(bf16[256,384]{1,0:T(8,128)(2,1)S(1)} %convolution_convert_fusion.refs_0_), channel_id=1, source_target_pairs={{0,64},{32,96},{64,0},{96,32},{1,65},{33,97},{65,1},{97,33},{2,66}... | collective-permute-start | bytes 589832 | tf_op jit(solution)/shard_map/ppermute | solution.py:52
  176.6 8.5 %collective-permute-start.18 = (bf16[256,384]{1,0:T(8,128)(2,1)S(1)}, bf16[256,384]{1,0:T(8,128)(2,1)S(1)}, u32[]{:S(2)}, u32[]{:S(2)}) collective-permute-start(bf16[256,384]{1,0:T(8,128)(2,1)S(1)} %convolution_convert_fusion.refs_0_), channel_id=1, source_target_pairs={{0,96},{32,0},{64,32},{96,64},{1,97},{33,1},{65,33},{97,65},{2,98}... | collective-permute-start | bytes 589832 | tf_op jit(solution)/shard_map/ppermute | solution.py:52
  186.8 30.2 %all-to-all-start.4 = ((bf16[32,8,1408]{2,1,0:T(8,128)(2,1)}), bf16[32,8,1408]{2,1,0:T(8,128)(2,1)S(1)}, u32[]{:S(2)}, u32[]{:S(2)}) async-start(bf16[32,8,1408]{2,1,0:T(8,128)(2,1)} %bitcast.36), calls=%async_computation.4 | async-start | bytes 1441792 | tf_op jit(solution)/shard_map/all_to_all | solution.py:47
  217.7 28.3 %copy-start.8 = (bf16[1,1024,1280]{2,1,0:T(8,128)(2,1)S(1)}, bf16[1,1024,1280]{2,1,0:T(8,128)(2,1)}, u32[]{:S(2)}) copy-start(bf16[1,1024,1280]{2,1,0:T(8,128)(2,1)} %param.16) | copy-start | bytes 7864324
  242.4 3.7 %copy-start.4 = (bf16[512,1280]{1,0:T(8,128)(2,1)S(1)}, bf16[512,1280]{1,0:T(8,128)(2,1)}, u32[]{:S(2)}) copy-start(bf16[512,1280]{1,0:T(8,128)(2,1)} %copy-done.3) | copy-start | bytes 3932164
  242.4 3.7 %copy-start.29 = (f32[1,1280]{1,0:T(1,128)S(1)}, f32[1,1280]{1,0:T(1,128)}, u32[]{:S(2)}) copy-start(f32[1,1280]{1,0:T(1,128)} %bias_ref.1) | copy-start | bytes 15364
  243.6 2.4 collective-permute-start.19
  249.8 18.1 %copy-start.33 = (f32[128,1024]{1,0:T(8,128)S(1)}, f32[128,1024]{1,0:T(8,128)}, u32[]{:S(2)}) copy-start(f32[128,1024]{1,0:T(8,128)} %add_add_fusion.1) | copy-start | bytes 1572868
  249.8 18.1 %copy-start.36 = (f32[1,1024]{1,0:T(1,128)S(1)}, f32[1,1024]{1,0:T(1,128)}, u32[]{:S(2)}) copy-start(f32[1,1024]{1,0:T(1,128)} %param.15) | copy-start | bytes 12292
  249.8 9.1 %collective-permute-start.22 = (bf16[128,1152]{1,0:T(8,128)(2,1)S(1)}, bf16[128,1152]{1,0:T(8,128)(2,1)S(1)}, u32[]{:S(2)}, u32[]{:S(2)}) collective-permute-start(bf16[128,1152]{1,0:T(8,128)(2,1)S(1)} %get-tuple-element.57), channel_id=1, source_target_pairs={{0,96},{32,0},{64,32},{96,64},{1,97},{33,1},{65,33},{97,65},{2,98}... | collective-permute-start | bytes 884744 | tf_op jit(solution)/shard_map/ppermute | solution.py:52
  250.6 16.2 %collective-permute-start.21 = (bf16[128,1152]{1,0:T(8,128)(2,1)S(1)}, bf16[128,1152]{1,0:T(8,128)(2,1)S(1)}, u32[]{:S(2)}, u32[]{:S(2)}) collective-permute-start(bf16[128,1152]{1,0:T(8,128)(2,1)S(1)} %get-tuple-element.56), channel_id=1, source_target_pairs={{0,64},{32,96},{64,0},{96,32},{1,65},{33,97},{65,1},{97,33},{2,66}... | collective-permute-start | bytes 884744 | tf_op jit(solution)/shard_map/ppermute | solution.py:52
  253.2 14.4 %collective-permute-start.20 = (bf16[128,1152]{1,0:T(8,128)(2,1)S(1)}, bf16[128,1152]{1,0:T(8,128)(2,1)S(1)}, u32[]{:S(2)}, u32[]{:S(2)}) collective-permute-start(bf16[128,1152]{1,0:T(8,128)(2,1)S(1)} %get-tuple-element.55), channel_id=1, source_target_pairs={{0,32},{32,64},{64,96},{96,0},{1,33},{33,65},{65,97},{97,1},{2,34}... | collective-permute-start | bytes 884744 | tf_op jit(solution)/shard_map/ppermute | solution.py:52
  (17 other events, 12.7 us)

commit v5 on v4

--- a/solution.py
+++ b/solution.py
@@ -161,7 +161,7 @@
         in_specs=[pl.BlockSpec(memory_space=pltpu.VMEM)] * len(args),
         out_specs=tuple(pl.BlockSpec(memory_space=pltpu.VMEM) for _ in out_shape),
         scratch_shapes=scratch,
-        compiler_params=pltpu.CompilerParams(vmem_limit_bytes=32 * 1024 * 1024),
+        compiler_params=pltpu.CompilerParams(vmem_limit_bytes=14 * 1024 * 1024),
         cost_estimate=pl.CostEstimate(flops=flops, bytes_accessed=4_000_000, transcendentals=0),
     )(*args)
 
@@ -174,11 +174,11 @@
     return pl.pallas_call(
         start_kernel,
         out_shape=(jax.ShapeDtypeStruct((width, hid), BF16), part, part),
-        in_specs=[pl.BlockSpec(memory_space=pltpu.HBM)] * len(args),
+        in_specs=[pl.BlockSpec(memory_space=pl.ANY)] * len(args),
         out_specs=(pl.BlockSpec(memory_space=pltpu.VMEM),) * 3,
         scratch_shapes=[pltpu.VMEM(arg.shape, arg.dtype) for arg in args]
         + [pltpu.SemaphoreType.DMA((len(args),))],
-        compiler_params=pltpu.CompilerParams(vmem_limit_bytes=40 * 1024 * 1024),
+        compiler_params=pltpu.CompilerParams(vmem_limit_bytes=58 * 1024 * 1024),
         cost_estimate=pl.CostEstimate(
             flops=4 * half * width * hid, bytes_accessed=7_000_000, transcendentals=0
         ),
@@ -205,16 +205,18 @@
         total = total + columns[:, 2 + place : 3 + place] * vector[:1]
     pre = total * columns[:, :1]
     summed = sum(vectors)
-    return pre, pre + (summed[1:2] + vectors[0][2:3]), columns, summed
+    shift = summed[1:2] + vectors[0][2:3]
+    return pre, shift, columns, summed
 
 
 def forward_kernel(*refs):
-    parts, (out_w_ref, y_ref, pre_ref, hidden_ref, columns_ref, sums_ref) = refs[:-6], refs[-6:]
-    pre, hidden, columns, sums = read_hidden(parts)
-    pre_ref[...] = pre
-    hidden_ref[...] = hidden
-    columns_ref[...] = columns
-    sums_ref[...] = sums
+    parts, (out_w_ref, y_ref, state_ref) = refs[:-3], refs[-3:]
+    pre, shift, columns, sums = read_hidden(parts)
+    hidden = pre + shift
+    half, hid = pre.shape
+    state_ref[:half, :hid] = pre
+    state_ref[:half, hid:] = columns
+    state_ref[half : half + 8, :hid] = jnp.concatenate([sums[:1], shift, sums[2:]], axis=0)
     act = 0.5 * hidden * (1.0 + lax.erf(hidden * SQRT_HALF))
     y_ref[...] = dot(act.astype(BF16), out_w_ref[...]).astype(BF16)
 
@@ -232,17 +234,19 @@
 
 def turn_kernel(*refs):
     parts, (grad_act_ref, weight_ref, y_ref, columns_ref) = refs[:-4], refs[-4:]
-    pre, hidden, columns, sums = read_hidden(parts)
+    pre, shift, columns, sums = read_hidden(parts)
     columns_ref[...] = columns
-    write_grad(grad_act_ref[...], hidden, pre, sums[:1], weight_ref[...], y_ref)
+    write_grad(grad_act_ref[...], pre + shift, pre, sums[:1], weight_ref[...], y_ref)
 
 
 def backward_kernel(*refs):
-    parts, (hidden_ref, pre_ref, sums_ref, weight_ref, y_ref) = refs[:-5], refs[-5:]
+    parts, (state_ref, weight_ref, y_ref) = refs[:-3], refs[-3:]
+    half, hid = parts[0].shape
     grad_act = parts[0][...].astype(F32)
     for part in parts[1:]:
         grad_act = grad_act + part[...].astype(F32)
-    write_grad(grad_act, hidden_ref[...], pre_ref[...], sums_ref[:1, :], weight_ref[...], y_ref)
+    pre, vectors = state_ref[:half, :hid], state_ref[half : half + 8, :hid]
+    write_grad(grad_act, pre + vectors[1:2], pre, vectors[:1], weight_ref[...], y_ref)
 
 
 def columns_of(terms, rows):
@@ -269,8 +273,7 @@
     part_ref[half : half + 32, :] = jnp.concatenate([low[:24], stats], axis=0).astype(BF16)
 
 
-def write_copies(rows, rows_ref, copies_ref):
-    rows_ref[...] = rows
+def write_copies(rows, copies_ref):
     for place in range(copies_ref.shape[0]):
         copies_ref[place] = rows
 
@@ -282,12 +285,12 @@
     return total
 
 
-def share_kernel(y_ref, resid_ref, bias_ref, rows_ref, copies_ref):
+def share_kernel(y_ref, resid_ref, bias_ref, copies_ref):
     rows = resid_ref[...] + total_of(y_ref) + bias_ref[...]
-    write_copies(rows.astype(BF16), rows_ref, copies_ref)
-
-
-def norm_kernel(y_ref, columns_ref, resid_ref, grad_ref, rows_ref, copies_ref):
+    write_copies(rows.astype(BF16), copies_ref)
+
+
+def norm_kernel(y_ref, columns_ref, resid_ref, grad_ref, copies_ref):
     width = resid_ref.shape[1]
     summed = total_of(y_ref)
     grad_norm, extra = summed[:, :width], summed[:, width:] / D
@@ -296,7 +299,7 @@
     inv, mean = columns_ref[:, :1], columns_ref[:, 1:2]
     normed = (resid_ref[...] - mean) * inv
     grad_resid = inv * (grad_norm - mean_grad - normed * mean_cross)
-    write_copies((grad_ref[...] + grad_resid).astype(BF16), rows_ref, copies_ref)
+    write_copies((grad_ref[...] + grad_resid).astype(BF16), copies_ref)
 
 
 def effect_kernel(own_ref, rest_ref, resid_ref, weight_ref, bias_ref, *refs):
@@ -371,7 +374,6 @@
         stats = jnp.stack(split3(local_mean) + split3(square))
         return part + jnp.pad(stats, ((half + 24, 2), (0, hid - half)))
 
-    part_shape = jax.ShapeDtypeStruct((half, hid), F32)
     columns_shape = jax.ShapeDtypeStruct((half, 128), F32)
     y_shape = jax.ShapeDtypeStruct((half, width), BF16)
     grad_shape = jax.ShapeDtypeStruct((half, width + 128), BF16)
@@ -391,24 +393,22 @@
     gained_0, gained_1 = pick(gained, gained_there), pick(gained_there, gained)
     out_w0 = pick(out_w, other(out_w))
 
-    y_0, pre_0, hidden_0, columns_0, sums_0 = in_vmem(
+    y_0, state_0 = in_vmem(
         forward_kernel,
-        (y_shape, part_shape, part_shape, columns_shape, jax.ShapeDtypeStruct((8, hid), F32)),
+        (y_shape, jax.ShapeDtypeStruct((half + 8, hid + 128), F32)),
         *gather_ring(part_0, "dp"),
         out_w0,
         flops=flops,
     )
     tokens_rows = own_rows(tokens_half).astype(F32)
     bias_row = vectors_0[3:7].reshape(1, -1)[:, :width]
-    row_shapes = (
-        jax.ShapeDtypeStruct((share, width), BF16),
-        jax.ShapeDtypeStruct((latent_count, share, width), BF16),
-    )
-    resid_rows, copies = in_vmem(
+    row_shapes = (jax.ShapeDtypeStruct((latent_count, share, width), BF16),)
+    (copies,) = in_vmem(
         share_kernel, row_shapes, exchange(y_0, "latent"), tokens_rows, bias_row
     )
     grad_act_1 = total_ring(part_grad[:half], "dp")
     copies, grad_act_1 = lax.optimization_barrier((copies, grad_act_1))
+    resid_rows = copies[0]
     resid_half = lax.all_to_all(copies, "latent", 0, 0).reshape(half, width)
 
     (part_1,) = in_vmem(
@@ -424,10 +424,10 @@
     parts_1, resid_there = lax.optimization_barrier((parts_1, resid_there))
 
     def norm_grad(y, columns, resid, grad_rows):
-        rows, copies = in_vmem(
+        (copies,) = in_vmem(
             norm_kernel, row_shapes, exchange(y, "latent"), own_rows(columns), resid, grad_rows
         )
-        return rows, lax.all_to_all(copies, "latent", 0, 0).reshape(half, width)
+        return copies[0], lax.all_to_all(copies, "latent", 0, 0).reshape(half, width)
 
     y_1, columns_1 = in_vmem(
         turn_kernel, (grad_shape, columns_shape), *parts_1, grad_act_1, gained_1, flops=flops
@@ -439,9 +439,9 @@
     grad_half_1, pre_codes = lax.optimization_barrier((grad_half_1, pre_codes))
     parts_0 = gather_ring(dot_t(grad_half_1, out_w0).astype(BF16), "dp")
     (y_2,) = in_vmem(
-        backward_kernel, (grad_shape,), *parts_0, hidden_0, pre_0, sums_0, gained_0, flops=flops
-    )
-    _, grad_half_0 = norm_grad(y_2, columns_0, tokens_rows, grad_rows_1.astype(F32))
+        backward_kernel, (grad_shape,), *parts_0, state_0, gained_0, flops=flops
+    )
+    _, grad_half_0 = norm_grad(y_2, state_0[:half, hid:], tokens_rows, grad_rows_1.astype(F32))
 
     codes = jnp.maximum(pre_codes + enc_bias[0][None], 0.0).astype(BF16)
     parts = in_vmem(

time: 287 us -> 262 us (0.913)
  local copies, waits for them, and re-layouts: 21.3 us -> 8.09 us
  waiting for transfers between devices: 122 us -> 116 us
  blocking collectives: 38.9 us -> 35.1 us
    unnamed x75 -> x43, local copies, waits for them, and re-layouts: 19.8 us -> 7.03 us
    all_to_all x3, waiting for transfers between devices: 46.5 us -> 41.3 us  [exchange(): lax.all_to_all(values.reshape(count, rows, values.shape[1]), axis, 0, 0)]
    all_to_all x1, blocking collectives: 24.6 us -> 21.1 us  [norm_grad(): lax.all_to_all(copies, 'latent', 0, 0).reshape(half, width)]
  transfers between devices with their start and end apart: 28 -> 28, of which waited for: 23 -> 21; matrix products, arithmetic and copies ran while one was open for 6% -> 7% of each run, Pallas kernels for 1% -> 2%
where the time goes in v5:
time: 262 us; the launch traced here: 261 us
  waiting for transfers between devices  116 us (44%)
  starting transfers between devices  66 us (25%)
  blocking collectives  35.1 us (13%)
  other arithmetic  18.1 us (7%)
  Pallas kernels  13.2 us (5%)
  local copies, waits for them, and re-layouts  8.09 us (3%)
  matrix products  3.59 us (1%)
    ppermute x18, waiting for transfers between devices, turn(): lax.ppermute(values, axis, [(i, (i + by) % count) for i in range(count)])  53.4 us
    all_to_all x3, waiting for transfers between devices, exchange(): lax.all_to_all(values.reshape(count, rows, values.shape[1]), axis, 0, 0)  41.3 us
    ppermute x18, starting transfers between devices, turn(): lax.ppermute(values, axis, [(i, (i + by) % count) for i in range(count)])  29.6 us
    all_to_all x3, starting transfers between devices, exchange(): lax.all_to_all(values.reshape(count, rows, values.shape[1]), axis, 0, 0)  25.4 us
    all_to_all x1, blocking collectives, norm_grad(): lax.all_to_all(copies, 'latent', 0, 0).reshape(half, width)  21.1 us
    all_to_all x1, waiting for transfers between devices, on_device(): resid_half = lax.all_to_all(copies, 'latent', 0, 0).reshape(half, width)  19.3 us
    all_to_all x1, blocking collectives, spread(): return lax.all_to_all(copies, axis, 0, 0)  14 us
    pallas_call x8, Pallas kernels, in_vmem(): pl.pallas_call(kernel, out_shape=out_shape, in_specs=[pl.BlockSpec(memory...  8.69 us
  transfers between devices with their start and end apart: 28, of which 21 were waited for; matrix products, arithmetic and copies ran while one was open for 7% of the time, Pallas kernels for 2%

profile of v5, /device:TPU:8, one launch (start us, length us, event | category | flops | bytes accessed | tf_op | source)
XLA Modules:
  0.0 261.3 jit_solution(14030857385805811343)
XLA Ops:
  0.8 4.5 %shard_map.131 = (bf16[1280,384]{1,0:T(8,128)(2,1)}, bf16[288,384]{1,0:T(8,128)(2,1)}, bf16[288,384]{1,0:T(8,128)(2,1)}) custom-call(bf16[512,1280]{1,0:T(8,128)(2,1)} %tokens_hbm.1, bf16[512,1280]{1,0:T(8,128)(2,1)} %cot_hbm.1, bf16[1280,384]{1,0:T(8,128)(2,1)} %bitcast.48, bf16[384,1280]{1,0:T(8,128)(2,1)} %bitcast.47, f32[1,1280]{1,0:T(1,128)} %gain_hbm.1, ...), custom_call_target="tpu_custom_call" | custom-call | flops 503316480 | bytes 7000000 | tf_op jit(solution)/shard_map/pallas_call | solution.py:174
  7.0 1.4 fusion.6
  8.6 2.2 collective-permute-start.3
  11.7 1.9 collective-permute-start.1
  13.6 1.3 broadcast_select_fusion.2.refs_4_
  14.9 1.7 collective-permute-done.3.refs_3_
  16.6 5.3 %collective-permute-done.2.refs_2_ = bf16[288,384]{1,0:T(8,128)(2,1)S(1)} collective-permute-done((bf16[288,384]{1,0:T(8,128)(2,1)S(1)}, bf16[288,384]{1,0:T(8,128)(2,1)S(1)}, u32[]{:S(2)}, u32[]{:S(2)}) %collective-permute-start.2) | collective-permute-done | bytes 221216 | tf_op jit(solution)/shard_map/ppermute | solution.py:52
  26.2 11.3 %all-to-all-start = ((bf16[32,8,1280]{2,1,0:T(8,128)(2,1)}), bf16[32,8,1280]{2,1,0:T(8,128)(2,1)S(1)}, u32[]{:S(2)}, u32[]{:S(2)}) async-start(bf16[32,8,1280]{2,1,0:T(8,128)(2,1)} %bitcast.45), calls=%async_computation | async-start | bytes 1310720 | tf_op jit(solution)/shard_map/all_to_all | solution.py:47
  38.4 2.4 collective-permute-start.6
  40.8 2.0 collective-permute-start.5
  43.6 3.5 %collective-permute-done.6 = bf16[256,384]{1,0:T(8,128)(2,1)S(1)} collective-permute-done((bf16[256,384]{1,0:T(8,128)(2,1)S(1)}, bf16[256,384]{1,0:T(8,128)(2,1)S(1)}, u32[]{:S(2)}, u32[]{:S(2)}) %collective-permute-start.6) | collective-permute-done | bytes 196640 | tf_op jit(solution)/shard_map/ppermute | solution.py:52
  47.1 3.7 %collective-permute-done.5 = bf16[256,384]{1,0:T(8,128)(2,1)S(1)} collective-permute-done((bf16[256,384]{1,0:T(8,128)(2,1)S(1)}, bf16[256,384]{1,0:T(8,128)(2,1)S(1)}, u32[]{:S(2)}, u32[]{:S(2)}) %collective-permute-start.5) | collective-permute-done | bytes 196640 | tf_op jit(solution)/shard_map/ppermute | solution.py:52
  51.6 5.4 %all-to-all-done.y_ref = bf16[32,8,1280]{2,1,0:T(8,128)(2,1)S(1)} async-done(((bf16[32,8,1280]{2,1,0:T(8,128)(2,1)}), bf16[32,8,1280]{2,1,0:T(8,128)(2,1)S(1)}, u32[]{:S(2)}, u32[]{:S(2)}) %all-to-all-start) | async-done | bytes 655392 | tf_op jit(solution)/shard_map/all_to_all | solution.py:47
  58.0 4.9 %all-to-all-start.1 = ((bf16[32,8,1280]{2,1,0:T(8,128)(2,1)}), bf16[32,8,1280]{2,1,0:T(8,128)(2,1)S(1)}, u32[]{:S(2)}, u32[]{:S(2)}) async-start(bf16[32,8,1280]{2,1,0:T(8,128)(2,1)} %copy-done.6), calls=%async_computation.1 | async-start | bytes 1310720 | tf_op jit(solution)/shard_map/all_to_all | solution.py:412
  63.0 19.3 %all-to-all-done.1 = bf16[32,8,1280]{2,1,0:T(8,128)(2,1)S(1)} async-done(((bf16[32,8,1280]{2,1,0:T(8,128)(2,1)}), bf16[32,8,1280]{2,1,0:T(8,128)(2,1)S(1)}, u32[]{:S(2)}, u32[]{:S(2)}) %all-to-all-start.1) | async-done | bytes 655392 | tf_op jit(solution)/shard_map/all_to_all | solution.py:412
  82.3 2.6 %broadcast_select_fusion = (bf16[1280,384]{1,0:T(8,128)(2,1)}, bf16[1280,384]{1,0:T(8,128)(2,1)S(1)}) fusion(bf16[1280,384]{1,0:T(8,128)(2,1)} %get-tuple-element.26, bf16[1280,384]{1,0:T(8,128)(2,1)} %collective-permute-done.8, pred[]{:T(512)S(6)} %eq.8), kind=kLoop, calls=%fused_computation.9 | loop fusion | flops 983040 | bytes 3932161 | tf_op jit(solution)/shard_map/jit(_where)/select_n | solution.py:359
  85.6 4.1 %collective-permute-start.11 = (bf16[288,384]{1,0:T(8,128)(2,1)S(1)}, bf16[288,384]{1,0:T(8,128)(2,1)S(1)}, u32[]{:S(2)}, u32[]{:S(2)}) collective-permute-start(bf16[288,384]{1,0:T(8,128)(2,1)S(1)} %shard_map.134.refs_0_), channel_id=1, source_target_pairs={{0,96},{32,0},{64,32},{96,64},{1,97},{33,1},{65,33},{97,65},{2,98}... | collective-permute-start | bytes 663560 | tf_op jit(solution)/shard_map/ppermute | solution.py:52
  89.8 1.5 collective-permute-start.9
  91.3 4.2 %collective-permute-done.11.refs_3_ = bf16[288,384]{1,0:T(8,128)(2,1)S(1)} collective-permute-done((bf16[288,384]{1,0:T(8,128)(2,1)S(1)}, bf16[288,384]{1,0:T(8,128)(2,1)S(1)}, u32[]{:S(2)}, u32[]{:S(2)}) %collective-permute-start.11) | collective-permute-done | bytes 221216 | tf_op jit(solution)/shard_map/ppermute | solution.py:52
  95.5 4.8 %collective-permute-done.10.refs_2_ = bf16[288,384]{1,0:T(8,128)(2,1)S(1)} collective-permute-done((bf16[288,384]{1,0:T(8,128)(2,1)S(1)}, bf16[288,384]{1,0:T(8,128)(2,1)S(1)}, u32[]{:S(2)}, u32[]{:S(2)}) %collective-permute-start.10) | collective-permute-done | bytes 221216 | tf_op jit(solution)/shard_map/ppermute | solution.py:52
  103.0 5.0 %all-to-all-start.2 = ((bf16[32,8,1408]{2,1,0:T(8,128)(2,1)}), bf16[32,8,1408]{2,1,0:T(8,128)(2,1)}, u32[]{:S(2)}, u32[]{:S(2)}) async-start(bf16[32,8,1408]{2,1,0:T(8,128)(2,1)} %bitcast.44), calls=%async_computation.2 | async-start | bytes 1441792 | tf_op jit(solution)/shard_map/all_to_all | solution.py:47
  109.5 19.9 %all-to-all-done.2.y_ref = bf16[32,8,1408]{2,1,0:T(8,128)(2,1)} async-done(((bf16[32,8,1408]{2,1,0:T(8,128)(2,1)}), bf16[32,8,1408]{2,1,0:T(8,128)(2,1)}, u32[]{:S(2)}, u32[]{:S(2)}) %all-to-all-start.2) | async-done | bytes 720928 | tf_op jit(solution)/shard_map/all_to_all | solution.py:47
  129.5 1.3 shard_map.136
  131.6 5.1 %all-to-all-start.3 = ((bf16[32,8,1280]{2,1,0:T(8,128)(2,1)}), bf16[32,8,1280]{2,1,0:T(8,128)(2,1)}, u32[]{:S(2)}, u32[]{:S(2)}) async-start(bf16[32,8,1280]{2,1,0:T(8,128)(2,1)} %copy-done.7), calls=%async_computation.3 | async-start | bytes 1310720 | tf_op jit(solution)/shard_map/all_to_all | solution.py:430
  136.8 1.8 maximum_select_fusion.resid_ref
  138.6 1.6 fusion.2
  141.1 1.7 collective-permute-start.13
  142.9 1.4 collective-permute-start.15
  144.3 2.1 collective-permute-start.14
  146.4 5.3 %collective-permute-done.13 = bf16[128,1024]{1,0:T(8,128)(2,1)} collective-permute-done((bf16[128,1024]{1,0:T(8,128)(2,1)S(1)}, bf16[128,1024]{1,0:T(8,128)(2,1)}, u32[]{:S(2)}, u32[]{:S(2)}) %collective-permute-start.13) | collective-permute-done | bytes 262176 | tf_op jit(solution)/shard_map/ppermute | solution.py:52
  151.6 4.9 %collective-permute-done.14 = bf16[128,1024]{1,0:T(8,128)(2,1)} collective-permute-done((bf16[128,1024]{1,0:T(8,128)(2,1)S(1)}, bf16[128,1024]{1,0:T(8,128)(2,1)}, u32[]{:S(2)}, u32[]{:S(2)}) %collective-permute-start.14) | collective-permute-done | bytes 262176 | tf_op jit(solution)/shard_map/ppermute | solution.py:52
  156.6 2.1 add_add_fusion.1
  158.7 2.0 convolution_convert_fusion.refs_0_
  162.0 1.9 collective-permute-start.17
  163.9 2.5 collective-permute-start.16
  167.3 2.3 collective-permute-done.17.refs_2_
  169.6 1.5 collective-permute-done.16.refs_1_
  172.6 9.1 %all-to-all-start.4 = ((bf16[32,8,1408]{2,1,0:T(8,128)(2,1)}), bf16[32,8,1408]{2,1,0:T(8,128)(2,1)S(1)}, u32[]{:S(2)}, u32[]{:S(2)}) async-start(bf16[32,8,1408]{2,1,0:T(8,128)(2,1)} %bitcast.42), calls=%async_computation.4 | async-start | bytes 1441792 | tf_op jit(solution)/shard_map/all_to_all | solution.py:47
  183.4 15.9 %all-to-all-done.4.y_ref = bf16[32,8,1408]{2,1,0:T(8,128)(2,1)S(1)} async-done(((bf16[32,8,1408]{2,1,0:T(8,128)(2,1)}), bf16[32,8,1408]{2,1,0:T(8,128)(2,1)S(1)}, u32[]{:S(2)}, u32[]{:S(2)}) %all-to-all-start.4) | async-done | bytes 720928 | tf_op jit(solution)/shard_map/all_to_all | solution.py:47
  199.6 21.1 %all_to_all.35 = bf16[32,8,1280]{2,1,0:T(8,128)(2,1)S(1)} all-to-all(bf16[32,8,1280]{2,1,0:T(8,128)(2,1)S(1)} %shard_map.138), channel_id=1, replica_groups=mesh['section'=2,'dp'=4,'latent'=32] {'latent'}, dimensions={0} | all-to-all | bytes 1310720 | tf_op jit(solution)/shard_map/all_to_all | solution.py:430
  220.7 1.3 bitcast_select_fusion
  222.3 2.1 collective-permute-done.19.rest_ref
  224.4 3.8 %shard_map.139 = (bf16[128,1152]{1,0:T(8,128)(2,1)S(1)}, bf16[128,1152]{1,0:T(8,128)(2,1)S(1)}, bf16[128,1152]{1,0:T(8,128)(2,1)S(1)}, bf16[128,1152]{1,0:T(8,128)(2,1)S(1)}) custom-call(bf16[256,1280]{1,0:T(8,128)(2,1)S(1)} %get-tuple-element.45.own_ref, bf16[256,1280]{1,0:T(8,128)(2,1)S(1)} %collective-permute-done.19.rest_ref, ...), custom_call_target="tpu_custom_call" | custom-call | flops 1342177280 | bytes 4000000 | tf_op jit(solution)/shard_map/pallas_call | solution.py:158
  228.2 1.4 collective-permute-start.20
  231.8 6.3 %collective-permute-done.20 = bf16[128,1152]{1,0:T(8,128)(2,1)S(1)} collective-permute-done((bf16[128,1152]{1,0:T(8,128)(2,1)S(1)}, bf16[128,1152]{1,0:T(8,128)(2,1)S(1)}, u32[]{:S(2)}, u32[]{:S(2)}) %collective-permute-start.20) | collective-permute-done | bytes 294944 | tf_op jit(solution)/shard_map/ppermute | solution.py:52
  238.1 2.9 %collective-permute-done.21 = bf16[128,1152]{1,0:T(8,128)(2,1)S(1)} collective-permute-done((bf16[128,1152]{1,0:T(8,128)(2,1)S(1)}, bf16[128,1152]{1,0:T(8,128)(2,1)S(1)}, u32[]{:S(2)}, u32[]{:S(2)}) %collective-permute-start.21) | collective-permute-done | bytes 294944 | tf_op jit(solution)/shard_map/ppermute | solution.py:52
  241.0 4.7 %collective-permute-done.22 = bf16[128,1152]{1,0:T(8,128)(2,1)S(1)} collective-permute-done((bf16[128,1152]{1,0:T(8,128)(2,1)S(1)}, bf16[128,1152]{1,0:T(8,128)(2,1)S(1)}, u32[]{:S(2)}, u32[]{:S(2)}) %collective-permute-start.22) | collective-permute-done | bytes 294944 | tf_op jit(solution)/shard_map/ppermute | solution.py:52
  246.8 14.0 %all_to_all.36 = f32[32,1,128]{2,1,0:T(1,128)S(1)} all-to-all(f32[32,1,128]{2,1,0:T(1,128)S(1)} %broadcast_in_dim.13), channel_id=1, replica_groups=mesh['section'=2,'dp'=4,'latent'=32] {'latent'}, dimensions={0} | all-to-all | bytes 32768 | tf_op jit(solution)/shard_map/all_to_all | solution.py:41
  (97 shorter events, 27.0 us)
Async XLA Ops:
  0.6 137.9 %copy-start = (bf16[1,1280,1024]{2,1,0:T(8,128)(2,1)S(1)}, bf16[1,1280,1024]{2,1,0:T(8,128)(2,1)}, u32[]{:S(2)}) copy-start(bf16[1,1280,1024]{2,1,0:T(8,128)(2,1)} %param.14) | copy-start | bytes 7864324
  0.6 13.0 %collective-permute-start.4 = (bf16[384,1280]{1,0:T(8,128)(2,1)}, bf16[384,1280]{1,0:T(8,128)(2,1)}, u32[]{:S(2)}, u32[]{:S(2)}) collective-permute-start(bf16[384,1280]{1,0:T(8,128)(2,1)} %bitcast.46), channel_id=1, source_target_pairs={{0,128},{128,0},{1,129},{129,1},{2,130},{130,2},{3,131},{131,3},{4... | collective-permute-start | bytes 2949128 | tf_op jit(solution)/shard_map/ppermute | solution.py:356
  5.3 3.2 %copy-start.19 = (bf16[288,384]{1,0:T(8,128)(2,1)S(1)}, bf16[288,384]{1,0:T(8,128)(2,1)}, u32[]{:S(2)}) copy-start(bf16[288,384]{1,0:T(8,128)(2,1)} %get-tuple-element.22) | copy-start | bytes 663556
  5.3 3.2 %collective-permute-start = (bf16[288,384]{1,0:T(8,128)(2,1)}, bf16[288,384]{1,0:T(8,128)(2,1)S(1)}, u32[]{:S(2)}, u32[]{:S(2)}) collective-permute-start(bf16[288,384]{1,0:T(8,128)(2,1)} %get-tuple-element.23), channel_id=1, source_target_pairs={{0,128},{128,0},{1,129},{129,1},{2,130},{130,2},{3,131},{131,3},{4... | collective-permute-start | bytes 663560 | tf_op jit(solution)/shard_map/ppermute | solution.py:356
  8.6 14.1 %copy-start.10 = (bf16[288,384]{1,0:T(8,128)(2,1)}, bf16[288,384]{1,0:T(8,128)(2,1)S(1)}, u32[]{:S(2)}) copy-start(bf16[288,384]{1,0:T(8,128)(2,1)S(1)} %get-tuple-element.52.refs_0_) | copy-start | bytes 663556
  8.6 8.0 %collective-permute-start.3 = (bf16[288,384]{1,0:T(8,128)(2,1)S(1)}, bf16[288,384]{1,0:T(8,128)(2,1)S(1)}, u32[]{:S(2)}, u32[]{:S(2)}) collective-permute-start(bf16[288,384]{1,0:T(8,128)(2,1)S(1)} %get-tuple-element.52.refs_0_), channel_id=1, source_target_pairs={{0,96},{32,0},{64,32},{96,64},{1,97},{33,1},{65,33},{97,65},{2,98}... | collective-permute-start | bytes 663560 | tf_op jit(solution)/shard_map/ppermute | solution.py:52
  10.8 11.1 %collective-permute-start.2 = (bf16[288,384]{1,0:T(8,128)(2,1)S(1)}, bf16[288,384]{1,0:T(8,128)(2,1)S(1)}, u32[]{:S(2)}, u32[]{:S(2)}) collective-permute-start(bf16[288,384]{1,0:T(8,128)(2,1)S(1)} %get-tuple-element.52.refs_0_), channel_id=1, source_target_pairs={{0,64},{32,96},{64,0},{96,32},{1,65},{33,97},{65,1},{97,33},{2,66}... | collective-permute-start | bytes 663560 | tf_op jit(solution)/shard_map/ppermute | solution.py:52
  11.7 11.0 %collective-permute-start.1 = (bf16[288,384]{1,0:T(8,128)(2,1)S(1)}, bf16[288,384]{1,0:T(8,128)(2,1)S(1)}, u32[]{:S(2)}, u32[]{:S(2)}) collective-permute-start(bf16[288,384]{1,0:T(8,128)(2,1)S(1)} %get-tuple-element.52.refs_0_), channel_id=1, source_target_pairs={{0,32},{32,64},{64,96},{96,0},{1,33},{33,65},{65,97},{97,1},{2,34}... | collective-permute-start | bytes 663560 | tf_op jit(solution)/shard_map/ppermute | solution.py:52
  23.6 1.0 copy-start.1
  25.4 0.9 copy-start.14
  26.2 30.8 %all-to-all-start = ((bf16[32,8,1280]{2,1,0:T(8,128)(2,1)}), bf16[32,8,1280]{2,1,0:T(8,128)(2,1)S(1)}, u32[]{:S(2)}, u32[]{:S(2)}) async-start(bf16[32,8,1280]{2,1,0:T(8,128)(2,1)} %bitcast.45), calls=%async_computation | async-start | bytes 1310720 | tf_op jit(solution)/shard_map/all_to_all | solution.py:47
  38.4 8.7 %collective-permute-start.6 = (bf16[256,384]{1,0:T(8,128)(2,1)S(1)}, bf16[256,384]{1,0:T(8,128)(2,1)S(1)}, u32[]{:S(2)}, u32[]{:S(2)}) collective-permute-start(bf16[256,384]{1,0:T(8,128)(2,1)S(1)} %slice.56), channel_id=1, source_target_pairs={{0,64},{32,96},{64,0},{96,32},{1,65},{33,97},{65,1},{97,33},{2,66}... | collective-permute-start | bytes 589832 | tf_op jit(solution)/shard_map/ppermute | solution.py:52
  40.8 10.0 %collective-permute-start.5 = (bf16[256,384]{1,0:T(8,128)(2,1)S(1)}, bf16[256,384]{1,0:T(8,128)(2,1)S(1)}, u32[]{:S(2)}, u32[]{:S(2)}) collective-permute-start(bf16[256,384]{1,0:T(8,128)(2,1)S(1)} %slice.56), channel_id=1, source_target_pairs={{0,32},{32,64},{64,96},{96,0},{1,33},{33,65},{65,97},{97,1},{2,34}... | collective-permute-start | bytes 589832 | tf_op jit(solution)/shard_map/ppermute | solution.py:52
  42.8 7.9 %collective-permute-start.7 = (bf16[256,384]{1,0:T(8,128)(2,1)S(1)}, bf16[256,384]{1,0:T(8,128)(2,1)S(1)}, u32[]{:S(2)}, u32[]{:S(2)}) collective-permute-start(bf16[256,384]{1,0:T(8,128)(2,1)S(1)} %slice.56), channel_id=1, source_target_pairs={{0,96},{32,0},{64,32},{96,64},{1,97},{33,1},{65,33},{97,65},{2,98}... | collective-permute-start | bytes 589832 | tf_op jit(solution)/shard_map/ppermute | solution.py:52
  57.1 0.9 copy-start.6
  58.0 24.3 %all-to-all-start.1 = ((bf16[32,8,1280]{2,1,0:T(8,128)(2,1)}), bf16[32,8,1280]{2,1,0:T(8,128)(2,1)S(1)}, u32[]{:S(2)}, u32[]{:S(2)}) async-start(bf16[32,8,1280]{2,1,0:T(8,128)(2,1)} %copy-done.6), calls=%async_computation.1 | async-start | bytes 1310720 | tf_op jit(solution)/shard_map/all_to_all | solution.py:412
  62.9 19.4 %collective-permute-start.8 = (bf16[1280,384]{1,0:T(8,128)(2,1)}, bf16[1280,384]{1,0:T(8,128)(2,1)}, u32[]{:S(2)}, u32[]{:S(2)}) collective-permute-start(bf16[1280,384]{1,0:T(8,128)(2,1)} %get-tuple-element.26), channel_id=1, source_target_pairs={{0,128},{128,0},{1,129},{129,1},{2,130},{130,2},{3,131},{131,3},{4... | collective-permute-start | bytes 2949128 | tf_op jit(solution)/shard_map/ppermute | solution.py:356
  82.3 18.8 %collective-permute-start.12 = (bf16[256,1280]{1,0:T(8,128)(2,1)S(1)}, bf16[256,1280]{1,0:T(8,128)(2,1)S(1)}, u32[]{:S(2)}, u32[]{:S(2)}) collective-permute-start(bf16[256,1280]{1,0:T(8,128)(2,1)S(1)} %bitcast.39), channel_id=1, source_target_pairs={{0,128},{128,0},{1,129},{129,1},{2,130},{130,2},{3,131},{131,3},{4... | collective-permute-start | bytes 1966088 | tf_op jit(solution)/shard_map/ppermute | solution.py:356
  84.9 16.2 %copy-start.9 = (f32[256,384]{1,0:T(8,128)S(1)}, f32[256,384]{1,0:T(8,128)}, u32[]{:S(2)}) copy-start(f32[256,384]{1,0:T(8,128)} %convert_add_fusion.refs_4_) | copy-start | bytes 1179652
  85.6 9.9 %collective-permute-start.11 = (bf16[288,384]{1,0:T(8,128)(2,1)S(1)}, bf16[288,384]{1,0:T(8,128)(2,1)S(1)}, u32[]{:S(2)}, u32[]{:S(2)}) collective-permute-start(bf16[288,384]{1,0:T(8,128)(2,1)S(1)} %shard_map.134.refs_0_), channel_id=1, source_target_pairs={{0,96},{32,0},{64,32},{96,64},{1,97},{33,1},{65,33},{97,65},{2,98}... | collective-permute-start | bytes 663560 | tf_op jit(solution)/shard_map/ppermute | solution.py:52
  89.8 10.6 %collective-permute-start.10 = (bf16[288,384]{1,0:T(8,128)(2,1)S(1)}, bf16[288,384]{1,0:T(8,128)(2,1)S(1)}, u32[]{:S(2)}, u32[]{:S(2)}) collective-permute-start(bf16[288,384]{1,0:T(8,128)(2,1)S(1)} %shard_map.134.refs_0_), channel_id=1, source_target_pairs={{0,64},{32,96},{64,0},{96,32},{1,65},{33,97},{65,1},{97,33},{2,66}... | collective-permute-start | bytes 663560 | tf_op jit(solution)/shard_map/ppermute | solution.py:52
  89.8 11.3 %collective-permute-start.9 = (bf16[288,384]{1,0:T(8,128)(2,1)S(1)}, bf16[288,384]{1,0:T(8,128)(2,1)S(1)}, u32[]{:S(2)}, u32[]{:S(2)}) collective-permute-start(bf16[288,384]{1,0:T(8,128)(2,1)S(1)} %shard_map.134.refs_0_), channel_id=1, source_target_pairs={{0,32},{32,64},{64,96},{96,0},{1,33},{33,65},{65,97},{97,1},{2,34}... | collective-permute-start | bytes 663560 | tf_op jit(solution)/shard_map/ppermute | solution.py:52
  101.1 1.0 copy-start.18
  102.1 0.9 copy-start.13
  103.0 26.5 %all-to-all-start.2 = ((bf16[32,8,1408]{2,1,0:T(8,128)(2,1)}), bf16[32,8,1408]{2,1,0:T(8,128)(2,1)}, u32[]{:S(2)}, u32[]{:S(2)}) async-start(bf16[32,8,1408]{2,1,0:T(8,128)(2,1)} %bitcast.44), calls=%async_computation.2 | async-start | bytes 1441792 | tf_op jit(solution)/shard_map/all_to_all | solution.py:47
  130.8 0.8 copy-start.7
  131.6 27.1 %all-to-all-start.3 = ((bf16[32,8,1280]{2,1,0:T(8,128)(2,1)}), bf16[32,8,1280]{2,1,0:T(8,128)(2,1)}, u32[]{:S(2)}, u32[]{:S(2)}) async-start(bf16[32,8,1280]{2,1,0:T(8,128)(2,1)} %copy-done.7), calls=%async_computation.3 | async-start | bytes 1310720 | tf_op jit(solution)/shard_map/all_to_all | solution.py:430
  138.6 1.6 copy-start.2
  140.1 1.0 copy-start.17
  141.1 10.5 %collective-permute-start.13 = (bf16[128,1024]{1,0:T(8,128)(2,1)S(1)}, bf16[128,1024]{1,0:T(8,128)(2,1)}, u32[]{:S(2)}, u32[]{:S(2)}) collective-permute-start(bf16[128,1024]{1,0:T(8,128)(2,1)S(1)} %get-tuple-element.48), channel_id=1, source_target_pairs={{0,32},{32,64},{64,96},{96,0},{1,33},{33,65},{65,97},{97,1},{2,34}... | collective-permute-start | bytes 786440 | tf_op jit(solution)/shard_map/ppermute | solution.py:52
  142.9 8.8 %collective-permute-start.15 = (bf16[128,1024]{1,0:T(8,128)(2,1)S(1)}, bf16[128,1024]{1,0:T(8,128)(2,1)}, u32[]{:S(2)}, u32[]{:S(2)}) collective-permute-start(bf16[128,1024]{1,0:T(8,128)(2,1)S(1)} %get-tuple-element.49), channel_id=1, source_target_pairs={{0,96},{32,0},{64,32},{96,64},{1,97},{33,1},{65,33},{97,65},{2,98}... | collective-permute-start | bytes 786440 | tf_op jit(solution)/shard_map/ppermute | solution.py:52
  144.3 12.2 %collective-permute-start.14 = (bf16[128,1024]{1,0:T(8,128)(2,1)S(1)}, bf16[128,1024]{1,0:T(8,128)(2,1)}, u32[]{:S(2)}, u32[]{:S(2)}) collective-permute-start(bf16[128,1024]{1,0:T(8,128)(2,1)S(1)} %get-tuple-element.50), channel_id=1, source_target_pairs={{0,64},{32,96},{64,0},{96,32},{1,65},{33,97},{65,1},{97,33},{2,66}... | collective-permute-start | bytes 786440 | tf_op jit(solution)/shard_map/ppermute | solution.py:52
  158.7 12.3 %copy-start.12 = (f32[264,512]{1,0:T(8,128)S(1)}, f32[264,512]{1,0:T(8,128)}, u32[]{:S(2)}) copy-start(f32[264,512]{1,0:T(8,128)} %copy-done.11) | copy-start | bytes 1622020
  158.7 12.3 %copy-start.4 = (bf16[1280,384]{1,0:T(8,128)(2,1)S(1)}, bf16[1280,384]{1,0:T(8,128)(2,1)}, u32[]{:S(2)}) copy-start(bf16[1280,384]{1,0:T(8,128)(2,1)} %get-tuple-element.42.refs_5_) | copy-start | bytes 2949124
  160.8 6.5 %collective-permute-start.18 = (bf16[256,384]{1,0:T(8,128)(2,1)S(1)}, bf16[256,384]{1,0:T(8,128)(2,1)S(1)}, u32[]{:S(2)}, u32[]{:S(2)}) collective-permute-start(bf16[256,384]{1,0:T(8,128)(2,1)S(1)} %convolution_convert_fusion.refs_0_), channel_id=1, source_target_pairs={{0,96},{32,0},{64,32},{96,64},{1,97},{33,1},{65,33},{97,65},{2,98}... | collective-permute-start | bytes 589832 | tf_op jit(solution)/shard_map/ppermute | solution.py:52
  162.0 7.5 %collective-permute-start.17 = (bf16[256,384]{1,0:T(8,128)(2,1)S(1)}, bf16[256,384]{1,0:T(8,128)(2,1)S(1)}, u32[]{:S(2)}, u32[]{:S(2)}) collective-permute-start(bf16[256,384]{1,0:T(8,128)(2,1)S(1)} %convolution_convert_fusion.refs_0_), channel_id=1, source_target_pairs={{0,64},{32,96},{64,0},{96,32},{1,65},{33,97},{65,1},{97,33},{2,66}... | collective-permute-start | bytes 589832 | tf_op jit(solution)/shard_map/ppermute | solution.py:52
  163.9 7.1 %collective-permute-start.16 = (bf16[256,384]{1,0:T(8,128)(2,1)S(1)}, bf16[256,384]{1,0:T(8,128)(2,1)S(1)}, u32[]{:S(2)}, u32[]{:S(2)}) collective-permute-start(bf16[256,384]{1,0:T(8,128)(2,1)S(1)} %convolution_convert_fusion.refs_0_), channel_id=1, source_target_pairs={{0,32},{32,64},{64,96},{96,0},{1,33},{33,65},{65,97},{97,1},{2,34}... | collective-permute-start | bytes 589832 | tf_op jit(solution)/shard_map/ppermute | solution.py:52
  171.7 0.9 copy-start.5
  172.6 26.7 %all-to-all-start.4 = ((bf16[32,8,1408]{2,1,0:T(8,128)(2,1)}), bf16[32,8,1408]{2,1,0:T(8,128)(2,1)S(1)}, u32[]{:S(2)}, u32[]{:S(2)}) async-start(bf16[32,8,1408]{2,1,0:T(8,128)(2,1)} %bitcast.42), calls=%async_computation.4 | async-start | bytes 1441792 | tf_op jit(solution)/shard_map/all_to_all | solution.py:47
  199.5 24.8 %copy-start.8 = (bf16[1,1024,1280]{2,1,0:T(8,128)(2,1)S(1)}, bf16[1,1024,1280]{2,1,0:T(8,128)(2,1)}, u32[]{:S(2)}) copy-start(bf16[1,1024,1280]{2,1,0:T(8,128)(2,1)} %param.16) | copy-start | bytes 7864324
  220.7 3.7 %copy-start.3 = (bf16[512,1280]{1,0:T(8,128)(2,1)S(1)}, bf16[512,1280]{1,0:T(8,128)(2,1)}, u32[]{:S(2)}) copy-start(bf16[512,1280]{1,0:T(8,128)(2,1)} %copy-done.2) | copy-start | bytes 3932164
  220.7 3.7 %copy-start.15 = (f32[1,1280]{1,0:T(1,128)S(1)}, f32[1,1280]{1,0:T(1,128)}, u32[]{:S(2)}) copy-start(f32[1,1280]{1,0:T(1,128)} %bias_ref.1) | copy-start | bytes 15364
  221.9 2.4 collective-permute-start.19
  228.1 17.8 %copy-start.16 = (f32[128,1024]{1,0:T(8,128)S(1)}, f32[128,1024]{1,0:T(8,128)}, u32[]{:S(2)}) copy-start(f32[128,1024]{1,0:T(8,128)} %add_add_fusion.1) | copy-start | bytes 1572868
  228.1 17.8 %copy-start.20 = (f32[1,1024]{1,0:T(1,128)S(1)}, f32[1,1024]{1,0:T(1,128)}, u32[]{:S(2)}) copy-start(f32[1,1024]{1,0:T(1,128)} %param.15) | copy-start | bytes 12292
  228.2 9.9 %collective-permute-start.20 = (bf16[128,1152]{1,0:T(8,128)(2,1)S(1)}, bf16[128,1152]{1,0:T(8,128)(2,1)S(1)}, u32[]{:S(2)}, u32[]{:S(2)}) collective-permute-start(bf16[128,1152]{1,0:T(8,128)(2,1)S(1)} %get-tuple-element.39), channel_id=1, source_target_pairs={{0,32},{32,64},{64,96},{96,0},{1,33},{33,65},{65,97},{97,1},{2,34}... | collective-permute-start | bytes 884744 | tf_op jit(solution)/shard_map/ppermute | solution.py:52
  229.6 11.4 %collective-permute-start.21 = (bf16[128,1152]{1,0:T(8,128)(2,1)S(1)}, bf16[128,1152]{1,0:T(8,128)(2,1)S(1)}, u32[]{:S(2)}, u32[]{:S(2)}) collective-permute-start(bf16[128,1152]{1,0:T(8,128)(2,1)S(1)} %get-tuple-element.40), channel_id=1, source_target_pairs={{0,64},{32,96},{64,0},{96,32},{1,65},{33,97},{65,1},{97,33},{2,66}... | collective-permute-start | bytes 884744 | tf_op jit(solution)/shard_map/ppermute | solution.py:52
  230.8 14.8 %collective-permute-start.22 = (bf16[128,1152]{1,0:T(8,128)(2,1)S(1)}, bf16[128,1152]{1,0:T(8,128)(2,1)S(1)}, u32[]{:S(2)}, u32[]{:S(2)}) collective-permute-start(bf16[128,1152]{1,0:T(8,128)(2,1)S(1)} %get-tuple-element.41), channel_id=1, source_target_pairs={{0,96},{32,0},{64,32},{96,64},{1,97},{33,1},{65,33},{97,65},{2,98}... | collective-permute-start | bytes 884744 | tf_op jit(solution)/shard_map/ppermute | solution.py:52
  (1 other events, 0.8 us)

commit v6 on v5

--- a/solution.py
+++ b/solution.py
@@ -423,25 +423,30 @@
     parts_1 = gather_ring(part_1, "dp")
     parts_1, resid_there = lax.optimization_barrier((parts_1, resid_there))
 
-    def norm_grad(y, columns, resid, grad_rows):
-        (copies,) = in_vmem(
-            norm_kernel, row_shapes, exchange(y, "latent"), own_rows(columns), resid, grad_rows
-        )
-        return copies[0], lax.all_to_all(copies, "latent", 0, 0).reshape(half, width)
+    resid_all = pick(tokens, jnp.concatenate([resid_there, resid_half], axis=0))
+    code_parts = dot(resid_all, enc_weight[0]).astype(BF16)
+
+    def norm_grad(y, columns, resid, grad_rows, beside=None):
+        y = exchange(y, "latent")
+        if beside is not None:
+            y, beside = lax.optimization_barrier((y, beside))
+        (copies,) = in_vmem(norm_kernel, row_shapes, y, own_rows(columns), resid, grad_rows)
+        return copies[0], beside, lax.all_to_all(copies, "latent", 0, 0).reshape(half, width)
 
     y_1, columns_1 = in_vmem(
         turn_kernel, (grad_shape, columns_shape), *parts_1, grad_act_1, gained_1, flops=flops
     )
     cot_rows = own_rows(cot_half).astype(F32)
-    grad_rows_1, grad_half_1 = norm_grad(y_1, columns_1, resid_rows.astype(F32), cot_rows)
-    resid_all = pick(tokens, jnp.concatenate([resid_there, resid_half], axis=0))
-    pre_codes = scatter_ring(dot(resid_all, enc_weight[0]).astype(BF16), "dp")
+    grad_rows_1, code_parts, grad_half_1 = norm_grad(
+        y_1, columns_1, resid_rows.astype(F32), cot_rows, code_parts
+    )
+    pre_codes = scatter_ring(code_parts, "dp")
     grad_half_1, pre_codes = lax.optimization_barrier((grad_half_1, pre_codes))
     parts_0 = gather_ring(dot_t(grad_half_1, out_w0).astype(BF16), "dp")
     (y_2,) = in_vmem(
         backward_kernel, (grad_shape,), *parts_0, state_0, gained_0, flops=flops
     )
-    _, grad_half_0 = norm_grad(y_2, state_0[:half, hid:], tokens_rows, grad_rows_1.astype(F32))
+    _, _, grad_half_0 = norm_grad(y_2, state_0[:half, hid:], tokens_rows, grad_rows_1.astype(F32))
 
     codes = jnp.maximum(pre_codes + enc_bias[0][None], 0.0).astype(BF16)
     parts = in_vmem(

time: 262 us -> 261 us (level)
  waiting for transfers between devices: 116 us -> 112 us
    all_to_all x3, waiting for transfers between devices: 41.3 us -> 37.3 us  [exchange(): lax.all_to_all(values.reshape(count, rows, values.shape[1]), axis, 0, 0)]
    unnamed x43 -> x39, local copies, waits for them, and re-layouts: 7.03 us -> 6.35 us
  transfers between devices with their start and end apart: 28 -> 28, of which waited for: 21 -> 22; matrix products, arithmetic and copies ran while one was open for 7% -> 8% of each run, Pallas kernels for 2% -> 2%
where the time goes in v6:
time: 261 us; the launch traced here: 260 us
  waiting for transfers between devices  112 us (43%)
  starting transfers between devices  65.9 us (25%)
  blocking collectives  35.6 us (14%)
  other arithmetic  18.1 us (7%)
  Pallas kernels  14.1 us (5%)
  local copies, waits for them, and re-layouts  8.52 us (3%)
  matrix products  4.56 us (2%)
    ppermute x18, waiting for transfers between devices, turn(): lax.ppermute(values, axis, [(i, (i + by) % count) for i in range(count)])  53.1 us
    all_to_all x3, waiting for transfers between devices, exchange(): lax.all_to_all(values.reshape(count, rows, values.shape[1]), axis, 0, 0)  37.3 us
    ppermute x18, starting transfers between devices, turn(): lax.ppermute(values, axis, [(i, (i + by) % count) for i in range(count)])  29.5 us
    all_to_all x3, starting transfers between devices, exchange(): lax.all_to_all(values.reshape(count, rows, values.shape[1]), axis, 0, 0)  25.5 us
    all_to_all x1, blocking collectives, norm_grad(): lax.all_to_all(copies, 'latent', 0, 0).reshape(half, width)  21.4 us
    all_to_all x1, waiting for transfers between devices, on_device(): resid_half = lax.all_to_all(copies, 'latent', 0, 0).reshape(half, width)  19.3 us
    all_to_all x1, blocking collectives, spread(): return lax.all_to_all(copies, axis, 0, 0)  14.2 us
    pallas_call x8, Pallas kernels, in_vmem(): pl.pallas_call(kernel, out_shape=out_shape, in_specs=[pl.BlockSpec(memory...  9.57 us
  transfers between devices with their start and end apart: 28, of which 22 were waited for; matrix products, arithmetic and copies ran while one was open for 8% of the time, Pallas kernels for 2%

profile of v6, /device:TPU:8, one launch (start us, length us, event | category | flops | bytes accessed | tf_op | source)
XLA Modules:
  0.0 259.7 jit_solution(11479173323126453922)
XLA Ops:
  0.8 4.5 %shard_map.131 = (bf16[1280,384]{1,0:T(8,128)(2,1)}, bf16[288,384]{1,0:T(8,128)(2,1)}, bf16[288,384]{1,0:T(8,128)(2,1)}) custom-call(bf16[512,1280]{1,0:T(8,128)(2,1)} %tokens_hbm.1, bf16[512,1280]{1,0:T(8,128)(2,1)} %cot_hbm.1, bf16[1280,384]{1,0:T(8,128)(2,1)} %bitcast.48, bf16[384,1280]{1,0:T(8,128)(2,1)} %bitcast.47, f32[1,1280]{1,0:T(1,128)} %gain_hbm.1, ...), custom_call_target="tpu_custom_call" | custom-call | flops 503316480 | bytes 7000000 | tf_op jit(solution)/shard_map/pallas_call | solution.py:174
  7.0 1.4 fusion.6
  8.6 2.2 collective-permute-start.3
  11.7 1.9 collective-permute-start.1
  13.6 1.3 broadcast_select_fusion.2.refs_4_
  14.9 1.7 collective-permute-done.3.refs_3_
  16.6 5.3 %collective-permute-done.2.refs_2_ = bf16[288,384]{1,0:T(8,128)(2,1)S(1)} collective-permute-done((bf16[288,384]{1,0:T(8,128)(2,1)S(1)}, bf16[288,384]{1,0:T(8,128)(2,1)S(1)}, u32[]{:S(2)}, u32[]{:S(2)}) %collective-permute-start.2) | collective-permute-done | bytes 221216 | tf_op jit(solution)/shard_map/ppermute | solution.py:52
  26.2 11.3 %all-to-all-start = ((bf16[32,8,1280]{2,1,0:T(8,128)(2,1)}), bf16[32,8,1280]{2,1,0:T(8,128)(2,1)S(1)}, u32[]{:S(2)}, u32[]{:S(2)}) async-start(bf16[32,8,1280]{2,1,0:T(8,128)(2,1)} %bitcast.45), calls=%async_computation | async-start | bytes 1310720 | tf_op jit(solution)/shard_map/all_to_all | solution.py:47
  38.4 2.4 collective-permute-start.6
  40.8 2.0 collective-permute-start.5
  43.6 3.5 %collective-permute-done.6 = bf16[256,384]{1,0:T(8,128)(2,1)S(1)} collective-permute-done((bf16[256,384]{1,0:T(8,128)(2,1)S(1)}, bf16[256,384]{1,0:T(8,128)(2,1)S(1)}, u32[]{:S(2)}, u32[]{:S(2)}) %collective-permute-start.6) | collective-permute-done | bytes 196640 | tf_op jit(solution)/shard_map/ppermute | solution.py:52
  47.1 3.7 %collective-permute-done.5 = bf16[256,384]{1,0:T(8,128)(2,1)S(1)} collective-permute-done((bf16[256,384]{1,0:T(8,128)(2,1)S(1)}, bf16[256,384]{1,0:T(8,128)(2,1)S(1)}, u32[]{:S(2)}, u32[]{:S(2)}) %collective-permute-start.5) | collective-permute-done | bytes 196640 | tf_op jit(solution)/shard_map/ppermute | solution.py:52
  51.6 5.4 %all-to-all-done.y_ref = bf16[32,8,1280]{2,1,0:T(8,128)(2,1)S(1)} async-done(((bf16[32,8,1280]{2,1,0:T(8,128)(2,1)}), bf16[32,8,1280]{2,1,0:T(8,128)(2,1)S(1)}, u32[]{:S(2)}, u32[]{:S(2)}) %all-to-all-start) | async-done | bytes 655392 | tf_op jit(solution)/shard_map/all_to_all | solution.py:47
  58.0 4.9 %all-to-all-start.1 = ((bf16[32,8,1280]{2,1,0:T(8,128)(2,1)}), bf16[32,8,1280]{2,1,0:T(8,128)(2,1)S(1)}, u32[]{:S(2)}, u32[]{:S(2)}) async-start(bf16[32,8,1280]{2,1,0:T(8,128)(2,1)} %copy-done.6), calls=%async_computation.1 | async-start | bytes 1310720 | tf_op jit(solution)/shard_map/all_to_all | solution.py:412
  63.0 19.3 %all-to-all-done.1 = bf16[32,8,1280]{2,1,0:T(8,128)(2,1)S(1)} async-done(((bf16[32,8,1280]{2,1,0:T(8,128)(2,1)}), bf16[32,8,1280]{2,1,0:T(8,128)(2,1)S(1)}, u32[]{:S(2)}, u32[]{:S(2)}) %all-to-all-start.1) | async-done | bytes 655392 | tf_op jit(solution)/shard_map/all_to_all | solution.py:412
  82.3 2.6 %broadcast_select_fusion = (bf16[1280,384]{1,0:T(8,128)(2,1)}, bf16[1280,384]{1,0:T(8,128)(2,1)S(1)}) fusion(bf16[1280,384]{1,0:T(8,128)(2,1)} %get-tuple-element.28, bf16[1280,384]{1,0:T(8,128)(2,1)} %collective-permute-done.8, pred[]{:T(512)S(6)} %eq.8), kind=kLoop, calls=%fused_computation.9 | loop fusion | flops 983040 | bytes 3932161 | tf_op jit(solution)/shard_map/jit(_where)/select_n | solution.py:359
  85.6 4.1 %collective-permute-start.11 = (bf16[288,384]{1,0:T(8,128)(2,1)S(1)}, bf16[288,384]{1,0:T(8,128)(2,1)S(1)}, u32[]{:S(2)}, u32[]{:S(2)}) collective-permute-start(bf16[288,384]{1,0:T(8,128)(2,1)S(1)} %shard_map.134.refs_0_), channel_id=1, source_target_pairs={{0,96},{32,0},{64,32},{96,64},{1,97},{33,1},{65,33},{97,65},{2,98}... | collective-permute-start | bytes 663560 | tf_op jit(solution)/shard_map/ppermute | solution.py:52
  89.7 1.5 collective-permute-start.9
  92.1 3.4 %collective-permute-done.11.refs_3_ = bf16[288,384]{1,0:T(8,128)(2,1)S(1)} collective-permute-done((bf16[288,384]{1,0:T(8,128)(2,1)S(1)}, bf16[288,384]{1,0:T(8,128)(2,1)S(1)}, u32[]{:S(2)}, u32[]{:S(2)}) %collective-permute-start.11) | collective-permute-done | bytes 221216 | tf_op jit(solution)/shard_map/ppermute | solution.py:52
  95.4 4.8 %collective-permute-done.10.refs_2_ = bf16[288,384]{1,0:T(8,128)(2,1)S(1)} collective-permute-done((bf16[288,384]{1,0:T(8,128)(2,1)S(1)}, bf16[288,384]{1,0:T(8,128)(2,1)S(1)}, u32[]{:S(2)}, u32[]{:S(2)}) %collective-permute-start.10) | collective-permute-done | bytes 221216 | tf_op jit(solution)/shard_map/ppermute | solution.py:52
  103.0 5.0 %all-to-all-start.2 = ((bf16[32,8,1408]{2,1,0:T(8,128)(2,1)}), bf16[32,8,1408]{2,1,0:T(8,128)(2,1)}, u32[]{:S(2)}, u32[]{:S(2)}) async-start(bf16[32,8,1408]{2,1,0:T(8,128)(2,1)} %bitcast.44), calls=%async_computation.2 | async-start | bytes 1441792 | tf_op jit(solution)/shard_map/all_to_all | solution.py:47
  108.7 1.8 maximum_select_fusion.resid_ref
  110.5 2.5 fusion.2
  114.1 15.3 %all-to-all-done.2.y_ref = bf16[32,8,1408]{2,1,0:T(8,128)(2,1)} async-done(((bf16[32,8,1408]{2,1,0:T(8,128)(2,1)}), bf16[32,8,1408]{2,1,0:T(8,128)(2,1)}, u32[]{:S(2)}, u32[]{:S(2)}) %all-to-all-start.2) | async-done | bytes 720928 | tf_op jit(solution)/shard_map/all_to_all | solution.py:47
  129.4 2.2 shard_map.136
  131.6 5.1 %all-to-all-start.3 = ((bf16[32,8,1280]{2,1,0:T(8,128)(2,1)}), bf16[32,8,1280]{2,1,0:T(8,128)(2,1)}, u32[]{:S(2)}, u32[]{:S(2)}) async-start(bf16[32,8,1280]{2,1,0:T(8,128)(2,1)} %shard_map.136), calls=%async_computation.3 | async-start | bytes 1310720 | tf_op jit(solution)/shard_map/all_to_all | solution.py:434
  138.0 1.8 collective-permute-start.13
  139.8 1.5 collective-permute-start.15
  141.3 2.0 collective-permute-start.14
  143.3 5.3 %collective-permute-done.13 = bf16[128,1024]{1,0:T(8,128)(2,1)} collective-permute-done((bf16[128,1024]{1,0:T(8,128)(2,1)S(1)}, bf16[128,1024]{1,0:T(8,128)(2,1)}, u32[]{:S(2)}, u32[]{:S(2)}) %collective-permute-start.13) | collective-permute-done | bytes 262176 | tf_op jit(solution)/shard_map/ppermute | solution.py:52
  148.6 5.3 %collective-permute-done.14 = bf16[128,1024]{1,0:T(8,128)(2,1)} collective-permute-done((bf16[128,1024]{1,0:T(8,128)(2,1)S(1)}, bf16[128,1024]{1,0:T(8,128)(2,1)}, u32[]{:S(2)}, u32[]{:S(2)}) %collective-permute-start.14) | collective-permute-done | bytes 262176 | tf_op jit(solution)/shard_map/ppermute | solution.py:52
  153.9 2.1 add_add_fusion.1
  156.1 2.0 convolution_convert_fusion.refs_0_
  158.1 3.3 %collective-permute-start.18 = (bf16[256,384]{1,0:T(8,128)(2,1)S(1)}, bf16[256,384]{1,0:T(8,128)(2,1)S(1)}, u32[]{:S(2)}, u32[]{:S(2)}) collective-permute-start(bf16[256,384]{1,0:T(8,128)(2,1)S(1)} %convolution_convert_fusion.refs_0_), channel_id=1, source_target_pairs={{0,96},{32,0},{64,32},{96,64},{1,97},{33,1},{65,33},{97,65},{2,98}... | collective-permute-start | bytes 589832 | tf_op jit(solution)/shard_map/ppermute | solution.py:52
  161.4 2.3 collective-permute-start.16
  163.7 2.3 collective-permute-done.18.refs_3_
  166.0 2.6 collective-permute-done.17.refs_2_
  170.3 9.2 %all-to-all-start.4 = ((bf16[32,8,1408]{2,1,0:T(8,128)(2,1)}), bf16[32,8,1408]{2,1,0:T(8,128)(2,1)S(1)}, u32[]{:S(2)}, u32[]{:S(2)}) async-start(bf16[32,8,1408]{2,1,0:T(8,128)(2,1)} %bitcast.42), calls=%async_computation.4 | async-start | bytes 1441792 | tf_op jit(solution)/shard_map/all_to_all | solution.py:47
  181.1 16.5 %all-to-all-done.4.y_ref = bf16[32,8,1408]{2,1,0:T(8,128)(2,1)S(1)} async-done(((bf16[32,8,1408]{2,1,0:T(8,128)(2,1)}), bf16[32,8,1408]{2,1,0:T(8,128)(2,1)S(1)}, u32[]{:S(2)}, u32[]{:S(2)}) %all-to-all-start.4) | async-done | bytes 720928 | tf_op jit(solution)/shard_map/all_to_all | solution.py:47
  197.9 21.4 %all_to_all.35 = bf16[32,8,1280]{2,1,0:T(8,128)(2,1)S(1)} all-to-all(bf16[32,8,1280]{2,1,0:T(8,128)(2,1)S(1)} %shard_map.138), channel_id=1, replica_groups=mesh['section'=2,'dp'=4,'latent'=32] {'latent'}, dimensions={0} | all-to-all | bytes 1310720 | tf_op jit(solution)/shard_map/all_to_all | solution.py:434
  219.3 1.3 bitcast_select_fusion
  220.9 2.1 collective-permute-done.19.rest_ref
  223.0 3.8 %shard_map.139 = (bf16[128,1152]{1,0:T(8,128)(2,1)S(1)}, bf16[128,1152]{1,0:T(8,128)(2,1)S(1)}, bf16[128,1152]{1,0:T(8,128)(2,1)S(1)}, bf16[128,1152]{1,0:T(8,128)(2,1)S(1)}) custom-call(bf16[256,1280]{1,0:T(8,128)(2,1)S(1)} %get-tuple-element.49.own_ref, bf16[256,1280]{1,0:T(8,128)(2,1)S(1)} %collective-permute-done.19.rest_ref, ...), custom_call_target="tpu_custom_call" | custom-call | flops 1342177280 | bytes 4000000 | tf_op jit(solution)/shard_map/pallas_call | solution.py:158
  226.8 1.3 collective-permute-start.20
  230.3 6.4 %collective-permute-done.20 = bf16[128,1152]{1,0:T(8,128)(2,1)S(1)} collective-permute-done((bf16[128,1152]{1,0:T(8,128)(2,1)S(1)}, bf16[128,1152]{1,0:T(8,128)(2,1)S(1)}, u32[]{:S(2)}, u32[]{:S(2)}) %collective-permute-start.20) | collective-permute-done | bytes 294944 | tf_op jit(solution)/shard_map/ppermute | solution.py:52
  236.7 2.8 %collective-permute-done.21 = bf16[128,1152]{1,0:T(8,128)(2,1)S(1)} collective-permute-done((bf16[128,1152]{1,0:T(8,128)(2,1)S(1)}, bf16[128,1152]{1,0:T(8,128)(2,1)S(1)}, u32[]{:S(2)}, u32[]{:S(2)}) %collective-permute-start.21) | collective-permute-done | bytes 294944 | tf_op jit(solution)/shard_map/ppermute | solution.py:52
  239.5 4.4 %collective-permute-done.22 = bf16[128,1152]{1,0:T(8,128)(2,1)S(1)} collective-permute-done((bf16[128,1152]{1,0:T(8,128)(2,1)S(1)}, bf16[128,1152]{1,0:T(8,128)(2,1)S(1)}, u32[]{:S(2)}, u32[]{:S(2)}) %collective-permute-start.22) | collective-permute-done | bytes 294944 | tf_op jit(solution)/shard_map/ppermute | solution.py:52
  245.0 14.2 %all_to_all.36 = f32[32,1,128]{2,1,0:T(1,128)S(1)} all-to-all(f32[32,1,128]{2,1,0:T(1,128)S(1)} %broadcast_in_dim.13), channel_id=1, replica_groups=mesh['section'=2,'dp'=4,'latent'=32] {'latent'}, dimensions={0} | all-to-all | bytes 32768 | tf_op jit(solution)/shard_map/all_to_all | solution.py:41
  (93 shorter events, 25.5 us)
Async XLA Ops:
  0.6 109.8 %copy-start = (bf16[1,1280,1024]{2,1,0:T(8,128)(2,1)S(1)}, bf16[1,1280,1024]{2,1,0:T(8,128)(2,1)}, u32[]{:S(2)}) copy-start(bf16[1,1280,1024]{2,1,0:T(8,128)(2,1)} %param.14) | copy-start | bytes 7864324
  0.6 13.0 %collective-permute-start.4 = (bf16[384,1280]{1,0:T(8,128)(2,1)}, bf16[384,1280]{1,0:T(8,128)(2,1)}, u32[]{:S(2)}, u32[]{:S(2)}) collective-permute-start(bf16[384,1280]{1,0:T(8,128)(2,1)} %bitcast.46), channel_id=1, source_target_pairs={{0,128},{128,0},{1,129},{129,1},{2,130},{130,2},{3,131},{131,3},{4... | collective-permute-start | bytes 2949128 | tf_op jit(solution)/shard_map/ppermute | solution.py:356
  5.3 3.2 %copy-start.17 = (bf16[288,384]{1,0:T(8,128)(2,1)S(1)}, bf16[288,384]{1,0:T(8,128)(2,1)}, u32[]{:S(2)}) copy-start(bf16[288,384]{1,0:T(8,128)(2,1)} %get-tuple-element.24) | copy-start | bytes 663556
  5.3 3.2 %collective-permute-start = (bf16[288,384]{1,0:T(8,128)(2,1)}, bf16[288,384]{1,0:T(8,128)(2,1)S(1)}, u32[]{:S(2)}, u32[]{:S(2)}) collective-permute-start(bf16[288,384]{1,0:T(8,128)(2,1)} %get-tuple-element.25), channel_id=1, source_target_pairs={{0,128},{128,0},{1,129},{129,1},{2,130},{130,2},{3,131},{131,3},{4... | collective-permute-start | bytes 663560 | tf_op jit(solution)/shard_map/ppermute | solution.py:356
  8.6 14.1 %copy-start.9 = (bf16[288,384]{1,0:T(8,128)(2,1)}, bf16[288,384]{1,0:T(8,128)(2,1)S(1)}, u32[]{:S(2)}) copy-start(bf16[288,384]{1,0:T(8,128)(2,1)S(1)} %get-tuple-element.56.refs_0_) | copy-start | bytes 663556
  8.6 8.0 %collective-permute-start.3 = (bf16[288,384]{1,0:T(8,128)(2,1)S(1)}, bf16[288,384]{1,0:T(8,128)(2,1)S(1)}, u32[]{:S(2)}, u32[]{:S(2)}) collective-permute-start(bf16[288,384]{1,0:T(8,128)(2,1)S(1)} %get-tuple-element.56.refs_0_), channel_id=1, source_target_pairs={{0,96},{32,0},{64,32},{96,64},{1,97},{33,1},{65,33},{97,65},{2,98}... | collective-permute-start | bytes 663560 | tf_op jit(solution)/shard_map/ppermute | solution.py:52
  10.8 11.1 %collective-permute-start.2 = (bf16[288,384]{1,0:T(8,128)(2,1)S(1)}, bf16[288,384]{1,0:T(8,128)(2,1)S(1)}, u32[]{:S(2)}, u32[]{:S(2)}) collective-permute-start(bf16[288,384]{1,0:T(8,128)(2,1)S(1)} %get-tuple-element.56.refs_0_), channel_id=1, source_target_pairs={{0,64},{32,96},{64,0},{96,32},{1,65},{33,97},{65,1},{97,33},{2,66}... | collective-permute-start | bytes 663560 | tf_op jit(solution)/shard_map/ppermute | solution.py:52
  11.7 11.0 %collective-permute-start.1 = (bf16[288,384]{1,0:T(8,128)(2,1)S(1)}, bf16[288,384]{1,0:T(8,128)(2,1)S(1)}, u32[]{:S(2)}, u32[]{:S(2)}) collective-permute-start(bf16[288,384]{1,0:T(8,128)(2,1)S(1)} %get-tuple-element.56.refs_0_), channel_id=1, source_target_pairs={{0,32},{32,64},{64,96},{96,0},{1,33},{33,65},{65,97},{97,1},{2,34}... | collective-permute-start | bytes 663560 | tf_op jit(solution)/shard_map/ppermute | solution.py:52
  23.6 1.0 copy-start.1
  24.6 0.8 copy-start.10
  25.4 0.8 copy-start.13
  26.2 30.8 %all-to-all-start = ((bf16[32,8,1280]{2,1,0:T(8,128)(2,1)}), bf16[32,8,1280]{2,1,0:T(8,128)(2,1)S(1)}, u32[]{:S(2)}, u32[]{:S(2)}) async-start(bf16[32,8,1280]{2,1,0:T(8,128)(2,1)} %bitcast.45), calls=%async_computation | async-start | bytes 1310720 | tf_op jit(solution)/shard_map/all_to_all | solution.py:47
  38.4 8.7 %collective-permute-start.6 = (bf16[256,384]{1,0:T(8,128)(2,1)S(1)}, bf16[256,384]{1,0:T(8,128)(2,1)S(1)}, u32[]{:S(2)}, u32[]{:S(2)}) collective-permute-start(bf16[256,384]{1,0:T(8,128)(2,1)S(1)} %slice.56), channel_id=1, source_target_pairs={{0,64},{32,96},{64,0},{96,32},{1,65},{33,97},{65,1},{97,33},{2,66}... | collective-permute-start | bytes 589832 | tf_op jit(solution)/shard_map/ppermute | solution.py:52
  40.8 10.0 %collective-permute-start.5 = (bf16[256,384]{1,0:T(8,128)(2,1)S(1)}, bf16[256,384]{1,0:T(8,128)(2,1)S(1)}, u32[]{:S(2)}, u32[]{:S(2)}) collective-permute-start(bf16[256,384]{1,0:T(8,128)(2,1)S(1)} %slice.56), channel_id=1, source_target_pairs={{0,32},{32,64},{64,96},{96,0},{1,33},{33,65},{65,97},{97,1},{2,34}... | collective-permute-start | bytes 589832 | tf_op jit(solution)/shard_map/ppermute | solution.py:52
  42.8 7.9 %collective-permute-start.7 = (bf16[256,384]{1,0:T(8,128)(2,1)S(1)}, bf16[256,384]{1,0:T(8,128)(2,1)S(1)}, u32[]{:S(2)}, u32[]{:S(2)}) collective-permute-start(bf16[256,384]{1,0:T(8,128)(2,1)S(1)} %slice.56), channel_id=1, source_target_pairs={{0,96},{32,0},{64,32},{96,64},{1,97},{33,1},{65,33},{97,65},{2,98}... | collective-permute-start | bytes 589832 | tf_op jit(solution)/shard_map/ppermute | solution.py:52
  57.1 0.8 copy-start.6
  58.0 24.3 %all-to-all-start.1 = ((bf16[32,8,1280]{2,1,0:T(8,128)(2,1)}), bf16[32,8,1280]{2,1,0:T(8,128)(2,1)S(1)}, u32[]{:S(2)}, u32[]{:S(2)}) async-start(bf16[32,8,1280]{2,1,0:T(8,128)(2,1)} %copy-done.6), calls=%async_computation.1 | async-start | bytes 1310720 | tf_op jit(solution)/shard_map/all_to_all | solution.py:412
  62.9 19.4 %collective-permute-start.8 = (bf16[1280,384]{1,0:T(8,128)(2,1)}, bf16[1280,384]{1,0:T(8,128)(2,1)}, u32[]{:S(2)}, u32[]{:S(2)}) collective-permute-start(bf16[1280,384]{1,0:T(8,128)(2,1)} %get-tuple-element.28), channel_id=1, source_target_pairs={{0,128},{128,0},{1,129},{129,1},{2,130},{130,2},{3,131},{131,3},{4... | collective-permute-start | bytes 2949128 | tf_op jit(solution)/shard_map/ppermute | solution.py:356
  82.2 18.8 %collective-permute-start.12 = (bf16[256,1280]{1,0:T(8,128)(2,1)S(1)}, bf16[256,1280]{1,0:T(8,128)(2,1)S(1)}, u32[]{:S(2)}, u32[]{:S(2)}) collective-permute-start(bf16[256,1280]{1,0:T(8,128)(2,1)S(1)} %bitcast.39), channel_id=1, source_target_pairs={{0,128},{128,0},{1,129},{129,1},{2,130},{130,2},{3,131},{131,3},{4... | collective-permute-start | bytes 1966088 | tf_op jit(solution)/shard_map/ppermute | solution.py:356
  84.9 16.2 %copy-start.8 = (f32[256,384]{1,0:T(8,128)S(1)}, f32[256,384]{1,0:T(8,128)}, u32[]{:S(2)}) copy-start(f32[256,384]{1,0:T(8,128)} %convert_add_fusion.refs_4_) | copy-start | bytes 1179652
  85.6 9.9 %collective-permute-start.11 = (bf16[288,384]{1,0:T(8,128)(2,1)S(1)}, bf16[288,384]{1,0:T(8,128)(2,1)S(1)}, u32[]{:S(2)}, u32[]{:S(2)}) collective-permute-start(bf16[288,384]{1,0:T(8,128)(2,1)S(1)} %shard_map.134.refs_0_), channel_id=1, source_target_pairs={{0,96},{32,0},{64,32},{96,64},{1,97},{33,1},{65,33},{97,65},{2,98}... | collective-permute-start | bytes 663560 | tf_op jit(solution)/shard_map/ppermute | solution.py:52
  89.7 10.6 %collective-permute-start.10 = (bf16[288,384]{1,0:T(8,128)(2,1)S(1)}, bf16[288,384]{1,0:T(8,128)(2,1)S(1)}, u32[]{:S(2)}, u32[]{:S(2)}) collective-permute-start(bf16[288,384]{1,0:T(8,128)(2,1)S(1)} %shard_map.134.refs_0_), channel_id=1, source_target_pairs={{0,64},{32,96},{64,0},{96,32},{1,65},{33,97},{65,1},{97,33},{2,66}... | collective-permute-start | bytes 663560 | tf_op jit(solution)/shard_map/ppermute | solution.py:52
  89.7 11.3 %collective-permute-start.9 = (bf16[288,384]{1,0:T(8,128)(2,1)S(1)}, bf16[288,384]{1,0:T(8,128)(2,1)S(1)}, u32[]{:S(2)}, u32[]{:S(2)}) collective-permute-start(bf16[288,384]{1,0:T(8,128)(2,1)S(1)} %shard_map.134.refs_0_), channel_id=1, source_target_pairs={{0,32},{32,64},{64,96},{96,0},{1,33},{33,65},{65,97},{97,1},{2,34}... | collective-permute-start | bytes 663560 | tf_op jit(solution)/shard_map/ppermute | solution.py:52
  101.0 1.0 copy-start.16
  102.1 0.9 copy-start.12
  103.0 26.5 %all-to-all-start.2 = ((bf16[32,8,1408]{2,1,0:T(8,128)(2,1)}), bf16[32,8,1408]{2,1,0:T(8,128)(2,1)}, u32[]{:S(2)}, u32[]{:S(2)}) async-start(bf16[32,8,1408]{2,1,0:T(8,128)(2,1)} %bitcast.44), calls=%async_computation.2 | async-start | bytes 1441792 | tf_op jit(solution)/shard_map/all_to_all | solution.py:47
  113.0 1.1 copy-start.2
  131.6 24.5 %all-to-all-start.3 = ((bf16[32,8,1280]{2,1,0:T(8,128)(2,1)}), bf16[32,8,1280]{2,1,0:T(8,128)(2,1)}, u32[]{:S(2)}, u32[]{:S(2)}) async-start(bf16[32,8,1280]{2,1,0:T(8,128)(2,1)} %shard_map.136), calls=%async_computation.3 | async-start | bytes 1310720 | tf_op jit(solution)/shard_map/all_to_all | solution.py:434
  138.0 10.6 %collective-permute-start.13 = (bf16[128,1024]{1,0:T(8,128)(2,1)S(1)}, bf16[128,1024]{1,0:T(8,128)(2,1)}, u32[]{:S(2)}, u32[]{:S(2)}) collective-permute-start(bf16[128,1024]{1,0:T(8,128)(2,1)S(1)} %get-tuple-element.52), channel_id=1, source_target_pairs={{0,32},{32,64},{64,96},{96,0},{1,33},{33,65},{65,97},{97,1},{2,34}... | collective-permute-start | bytes 786440 | tf_op jit(solution)/shard_map/ppermute | solution.py:52
  139.8 8.8 %collective-permute-start.15 = (bf16[128,1024]{1,0:T(8,128)(2,1)S(1)}, bf16[128,1024]{1,0:T(8,128)(2,1)}, u32[]{:S(2)}, u32[]{:S(2)}) collective-permute-start(bf16[128,1024]{1,0:T(8,128)(2,1)S(1)} %get-tuple-element.53), channel_id=1, source_target_pairs={{0,96},{32,0},{64,32},{96,64},{1,97},{33,1},{65,33},{97,65},{2,98}... | collective-permute-start | bytes 786440 | tf_op jit(solution)/shard_map/ppermute | solution.py:52
  141.3 12.5 %collective-permute-start.14 = (bf16[128,1024]{1,0:T(8,128)(2,1)S(1)}, bf16[128,1024]{1,0:T(8,128)(2,1)}, u32[]{:S(2)}, u32[]{:S(2)}) collective-permute-start(bf16[128,1024]{1,0:T(8,128)(2,1)S(1)} %get-tuple-element.54), channel_id=1, source_target_pairs={{0,64},{32,96},{64,0},{96,32},{1,65},{33,97},{65,1},{97,33},{2,66}... | collective-permute-start | bytes 786440 | tf_op jit(solution)/shard_map/ppermute | solution.py:52
  156.0 12.7 %copy-start.11 = (f32[264,512]{1,0:T(8,128)S(1)}, f32[264,512]{1,0:T(8,128)}, u32[]{:S(2)}) copy-start(f32[264,512]{1,0:T(8,128)} %copy-done.10) | copy-start | bytes 1622020
  156.1 12.5 %copy-start.4 = (bf16[1280,384]{1,0:T(8,128)(2,1)S(1)}, bf16[1280,384]{1,0:T(8,128)(2,1)}, u32[]{:S(2)}) copy-start(bf16[1280,384]{1,0:T(8,128)(2,1)} %get-tuple-element.46.refs_5_) | copy-start | bytes 2949124
  158.1 7.9 %collective-permute-start.18 = (bf16[256,384]{1,0:T(8,128)(2,1)S(1)}, bf16[256,384]{1,0:T(8,128)(2,1)S(1)}, u32[]{:S(2)}, u32[]{:S(2)}) collective-permute-start(bf16[256,384]{1,0:T(8,128)(2,1)S(1)} %convolution_convert_fusion.refs_0_), channel_id=1, source_target_pairs={{0,96},{32,0},{64,32},{96,64},{1,97},{33,1},{65,33},{97,65},{2,98}... | collective-permute-start | bytes 589832 | tf_op jit(solution)/shard_map/ppermute | solution.py:52
  161.4 7.2 %collective-permute-start.17 = (bf16[256,384]{1,0:T(8,128)(2,1)S(1)}, bf16[256,384]{1,0:T(8,128)(2,1)S(1)}, u32[]{:S(2)}, u32[]{:S(2)}) collective-permute-start(bf16[256,384]{1,0:T(8,128)(2,1)S(1)} %convolution_convert_fusion.refs_0_), channel_id=1, source_target_pairs={{0,64},{32,96},{64,0},{96,32},{1,65},{33,97},{65,1},{97,33},{2,66}... | collective-permute-start | bytes 589832 | tf_op jit(solution)/shard_map/ppermute | solution.py:52
  161.4 7.2 %collective-permute-start.16 = (bf16[256,384]{1,0:T(8,128)(2,1)S(1)}, bf16[256,384]{1,0:T(8,128)(2,1)S(1)}, u32[]{:S(2)}, u32[]{:S(2)}) collective-permute-start(bf16[256,384]{1,0:T(8,128)(2,1)S(1)} %convolution_convert_fusion.refs_0_), channel_id=1, source_target_pairs={{0,32},{32,64},{64,96},{96,0},{1,33},{33,65},{65,97},{97,1},{2,34}... | collective-permute-start | bytes 589832 | tf_op jit(solution)/shard_map/ppermute | solution.py:52
  169.4 0.9 copy-start.5
  170.3 27.4 %all-to-all-start.4 = ((bf16[32,8,1408]{2,1,0:T(8,128)(2,1)}), bf16[32,8,1408]{2,1,0:T(8,128)(2,1)S(1)}, u32[]{:S(2)}, u32[]{:S(2)}) async-start(bf16[32,8,1408]{2,1,0:T(8,128)(2,1)} %bitcast.42), calls=%async_computation.4 | async-start | bytes 1441792 | tf_op jit(solution)/shard_map/all_to_all | solution.py:47
  197.9 25.1 %copy-start.7 = (bf16[1,1024,1280]{2,1,0:T(8,128)(2,1)S(1)}, bf16[1,1024,1280]{2,1,0:T(8,128)(2,1)}, u32[]{:S(2)}) copy-start(bf16[1,1024,1280]{2,1,0:T(8,128)(2,1)} %param.16) | copy-start | bytes 7864324
  219.3 3.7 %copy-start.3 = (bf16[512,1280]{1,0:T(8,128)(2,1)S(1)}, bf16[512,1280]{1,0:T(8,128)(2,1)}, u32[]{:S(2)}) copy-start(bf16[512,1280]{1,0:T(8,128)(2,1)} %copy-done.2) | copy-start | bytes 3932164
  219.3 3.7 %copy-start.14 = (f32[1,1280]{1,0:T(1,128)S(1)}, f32[1,1280]{1,0:T(1,128)}, u32[]{:S(2)}) copy-start(f32[1,1280]{1,0:T(1,128)} %bias_ref.1) | copy-start | bytes 15364
  220.6 2.4 collective-permute-start.19
  226.8 17.4 %copy-start.15 = (f32[128,1024]{1,0:T(8,128)S(1)}, f32[128,1024]{1,0:T(8,128)}, u32[]{:S(2)}) copy-start(f32[128,1024]{1,0:T(8,128)} %add_add_fusion.1) | copy-start | bytes 1572868
  226.8 17.4 %copy-start.18 = (f32[1,1024]{1,0:T(1,128)S(1)}, f32[1,1024]{1,0:T(1,128)}, u32[]{:S(2)}) copy-start(f32[1,1024]{1,0:T(1,128)} %param.15) | copy-start | bytes 12292
  226.8 9.9 %collective-permute-start.20 = (bf16[128,1152]{1,0:T(8,128)(2,1)S(1)}, bf16[128,1152]{1,0:T(8,128)(2,1)S(1)}, u32[]{:S(2)}, u32[]{:S(2)}) collective-permute-start(bf16[128,1152]{1,0:T(8,128)(2,1)S(1)} %get-tuple-element.43), channel_id=1, source_target_pairs={{0,32},{32,64},{64,96},{96,0},{1,33},{33,65},{65,97},{97,1},{2,34}... | collective-permute-start | bytes 884744 | tf_op jit(solution)/shard_map/ppermute | solution.py:52
  228.1 11.4 %collective-permute-start.21 = (bf16[128,1152]{1,0:T(8,128)(2,1)S(1)}, bf16[128,1152]{1,0:T(8,128)(2,1)S(1)}, u32[]{:S(2)}, u32[]{:S(2)}) collective-permute-start(bf16[128,1152]{1,0:T(8,128)(2,1)S(1)} %get-tuple-element.44), channel_id=1, source_target_pairs={{0,64},{32,96},{64,0},{96,32},{1,65},{33,97},{65,1},{97,33},{2,66}... | collective-permute-start | bytes 884744 | tf_op jit(solution)/shard_map/ppermute | solution.py:52
  229.1 14.8 %collective-permute-start.22 = (bf16[128,1152]{1,0:T(8,128)(2,1)S(1)}, bf16[128,1152]{1,0:T(8,128)(2,1)S(1)}, u32[]{:S(2)}, u32[]{:S(2)}) collective-permute-start(bf16[128,1152]{1,0:T(8,128)(2,1)S(1)} %get-tuple-element.45), channel_id=1, source_target_pairs={{0,96},{32,0},{64,32},{96,64},{1,97},{33,1},{65,33},{97,65},{2,98}... | collective-permute-start | bytes 884744 | tf_op jit(solution)/shard_map/ppermute | solution.py:52

commit v7 on v6

--- a/solution.py
+++ b/solution.py
@@ -161,7 +161,7 @@
         in_specs=[pl.BlockSpec(memory_space=pltpu.VMEM)] * len(args),
         out_specs=tuple(pl.BlockSpec(memory_space=pltpu.VMEM) for _ in out_shape),
         scratch_shapes=scratch,
-        compiler_params=pltpu.CompilerParams(vmem_limit_bytes=14 * 1024 * 1024),
+        compiler_params=pltpu.CompilerParams(vmem_limit_bytes=9 * 1024 * 1024),
         cost_estimate=pl.CostEstimate(flops=flops, bytes_accessed=4_000_000, transcendentals=0),
     )(*args)
 

time: 261 us -> 261 us (level)
  no operation moved by 1% of the time
where the time goes in v7:
time: 261 us; the launch traced here: 260 us
  waiting for transfers between devices  112 us (43%)
  starting transfers between devices  65.9 us (25%)
  blocking collectives  35.6 us (14%)
  other arithmetic  18.1 us (7%)
  Pallas kernels  14.1 us (5%)
  local copies, waits for them, and re-layouts  8.52 us (3%)
  matrix products  4.55 us (2%)
    ppermute x18, waiting for transfers between devices, turn(): lax.ppermute(values, axis, [(i, (i + by) % count) for i in range(count)])  53.1 us
    all_to_all x3, waiting for transfers between devices, exchange(): lax.all_to_all(values.reshape(count, rows, values.shape[1]), axis, 0, 0)  37.3 us
    ppermute x18, starting transfers between devices, turn(): lax.ppermute(values, axis, [(i, (i + by) % count) for i in range(count)])  29.5 us
    all_to_all x3, starting transfers between devices, exchange(): lax.all_to_all(values.reshape(count, rows, values.shape[1]), axis, 0, 0)  25.5 us
    all_to_all x1, blocking collectives, norm_grad(): lax.all_to_all(copies, 'latent', 0, 0).reshape(half, width)  21.4 us
    all_to_all x1, waiting for transfers between devices, on_device(): resid_half = lax.all_to_all(copies, 'latent', 0, 0).reshape(half, width)  19.3 us
    all_to_all x1, blocking collectives, spread(): return lax.all_to_all(copies, axis, 0, 0)  14.2 us
    pallas_call x8, Pallas kernels, in_vmem(): pl.pallas_call(kernel, out_shape=out_shape, in_specs=[pl.BlockSpec(memory...  9.58 us
  transfers between devices with their start and end apart: 28, of which 22 were waited for; matrix products, arithmetic and copies ran while one was open for 8% of the time, Pallas kernels for 2%

profile of v7, /device:TPU:8, one launch (start us, length us, event | category | flops | bytes accessed | tf_op | source)
XLA Modules:
  0.0 259.7 jit_solution(8810275482780202357)
XLA Ops:
  0.8 4.5 %shard_map.131 = (bf16[1280,384]{1,0:T(8,128)(2,1)}, bf16[288,384]{1,0:T(8,128)(2,1)}, bf16[288,384]{1,0:T(8,128)(2,1)}) custom-call(bf16[512,1280]{1,0:T(8,128)(2,1)} %tokens_hbm.1, bf16[512,1280]{1,0:T(8,128)(2,1)} %cot_hbm.1, bf16[1280,384]{1,0:T(8,128)(2,1)} %bitcast.48, bf16[384,1280]{1,0:T(8,128)(2,1)} %bitcast.47, f32[1,1280]{1,0:T(1,128)} %gain_hbm.1, ...), custom_call_target="tpu_custom_call" | custom-call | flops 503316480 | bytes 7000000 | tf_op jit(solution)/shard_map/pallas_call | solution.py:174
  7.0 1.4 fusion.6
  8.6 2.2 collective-permute-start.3
  11.7 1.9 collective-permute-start.1
  13.6 1.3 broadcast_select_fusion.2.refs_4_
  14.9 1.7 collective-permute-done.3.refs_3_
  16.6 5.3 %collective-permute-done.2.refs_2_ = bf16[288,384]{1,0:T(8,128)(2,1)S(1)} collective-permute-done((bf16[288,384]{1,0:T(8,128)(2,1)S(1)}, bf16[288,384]{1,0:T(8,128)(2,1)S(1)}, u32[]{:S(2)}, u32[]{:S(2)}) %collective-permute-start.2) | collective-permute-done | bytes 221216 | tf_op jit(solution)/shard_map/ppermute | solution.py:52
  26.2 11.3 %all-to-all-start = ((bf16[32,8,1280]{2,1,0:T(8,128)(2,1)}), bf16[32,8,1280]{2,1,0:T(8,128)(2,1)S(1)}, u32[]{:S(2)}, u32[]{:S(2)}) async-start(bf16[32,8,1280]{2,1,0:T(8,128)(2,1)} %bitcast.45), calls=%async_computation | async-start | bytes 1310720 | tf_op jit(solution)/shard_map/all_to_all | solution.py:47
  38.4 2.4 collective-permute-start.6
  40.8 2.0 collective-permute-start.5
  43.6 3.5 %collective-permute-done.6 = bf16[256,384]{1,0:T(8,128)(2,1)S(1)} collective-permute-done((bf16[256,384]{1,0:T(8,128)(2,1)S(1)}, bf16[256,384]{1,0:T(8,128)(2,1)S(1)}, u32[]{:S(2)}, u32[]{:S(2)}) %collective-permute-start.6) | collective-permute-done | bytes 196640 | tf_op jit(solution)/shard_map/ppermute | solution.py:52
  47.1 3.7 %collective-permute-done.5 = bf16[256,384]{1,0:T(8,128)(2,1)S(1)} collective-permute-done((bf16[256,384]{1,0:T(8,128)(2,1)S(1)}, bf16[256,384]{1,0:T(8,128)(2,1)S(1)}, u32[]{:S(2)}, u32[]{:S(2)}) %collective-permute-start.5) | collective-permute-done | bytes 196640 | tf_op jit(solution)/shard_map/ppermute | solution.py:52
  51.6 5.4 %all-to-all-done.y_ref = bf16[32,8,1280]{2,1,0:T(8,128)(2,1)S(1)} async-done(((bf16[32,8,1280]{2,1,0:T(8,128)(2,1)}), bf16[32,8,1280]{2,1,0:T(8,128)(2,1)S(1)}, u32[]{:S(2)}, u32[]{:S(2)}) %all-to-all-start) | async-done | bytes 655392 | tf_op jit(solution)/shard_map/all_to_all | solution.py:47
  58.0 4.9 %all-to-all-start.1 = ((bf16[32,8,1280]{2,1,0:T(8,128)(2,1)}), bf16[32,8,1280]{2,1,0:T(8,128)(2,1)S(1)}, u32[]{:S(2)}, u32[]{:S(2)}) async-start(bf16[32,8,1280]{2,1,0:T(8,128)(2,1)} %copy-done.6), calls=%async_computation.1 | async-start | bytes 1310720 | tf_op jit(solution)/shard_map/all_to_all | solution.py:412
  63.0 19.3 %all-to-all-done.1 = bf16[32,8,1280]{2,1,0:T(8,128)(2,1)S(1)} async-done(((bf16[32,8,1280]{2,1,0:T(8,128)(2,1)}), bf16[32,8,1280]{2,1,0:T(8,128)(2,1)S(1)}, u32[]{:S(2)}, u32[]{:S(2)}) %all-to-all-start.1) | async-done | bytes 655392 | tf_op jit(solution)/shard_map/all_to_all | solution.py:412
  82.3 2.6 %broadcast_select_fusion = (bf16[1280,384]{1,0:T(8,128)(2,1)}, bf16[1280,384]{1,0:T(8,128)(2,1)S(1)}) fusion(bf16[1280,384]{1,0:T(8,128)(2,1)} %get-tuple-element.28, bf16[1280,384]{1,0:T(8,128)(2,1)} %collective-permute-done.8, pred[]{:T(512)S(6)} %eq.8), kind=kLoop, calls=%fused_computation.9 | loop fusion | flops 983040 | bytes 3932161 | tf_op jit(solution)/shard_map/jit(_where)/select_n | solution.py:359
  85.6 4.1 %collective-permute-start.11 = (bf16[288,384]{1,0:T(8,128)(2,1)S(1)}, bf16[288,384]{1,0:T(8,128)(2,1)S(1)}, u32[]{:S(2)}, u32[]{:S(2)}) collective-permute-start(bf16[288,384]{1,0:T(8,128)(2,1)S(1)} %shard_map.134.refs_0_), channel_id=1, source_target_pairs={{0,96},{32,0},{64,32},{96,64},{1,97},{33,1},{65,33},{97,65},{2,98}... | collective-permute-start | bytes 663560 | tf_op jit(solution)/shard_map/ppermute | solution.py:52
  89.7 1.5 collective-permute-start.9
  92.1 3.4 %collective-permute-done.11.refs_3_ = bf16[288,384]{1,0:T(8,128)(2,1)S(1)} collective-permute-done((bf16[288,384]{1,0:T(8,128)(2,1)S(1)}, bf16[288,384]{1,0:T(8,128)(2,1)S(1)}, u32[]{:S(2)}, u32[]{:S(2)}) %collective-permute-start.11) | collective-permute-done | bytes 221216 | tf_op jit(solution)/shard_map/ppermute | solution.py:52
  95.4 4.8 %collective-permute-done.10.refs_2_ = bf16[288,384]{1,0:T(8,128)(2,1)S(1)} collective-permute-done((bf16[288,384]{1,0:T(8,128)(2,1)S(1)}, bf16[288,384]{1,0:T(8,128)(2,1)S(1)}, u32[]{:S(2)}, u32[]{:S(2)}) %collective-permute-start.10) | collective-permute-done | bytes 221216 | tf_op jit(solution)/shard_map/ppermute | solution.py:52
  103.0 5.0 %all-to-all-start.2 = ((bf16[32,8,1408]{2,1,0:T(8,128)(2,1)}), bf16[32,8,1408]{2,1,0:T(8,128)(2,1)}, u32[]{:S(2)}, u32[]{:S(2)}) async-start(bf16[32,8,1408]{2,1,0:T(8,128)(2,1)} %bitcast.44), calls=%async_computation.2 | async-start | bytes 1441792 | tf_op jit(solution)/shard_map/all_to_all | solution.py:47
  108.7 1.8 maximum_select_fusion.resid_ref
  110.5 2.5 fusion.2
  114.1 15.3 %all-to-all-done.2.y_ref = bf16[32,8,1408]{2,1,0:T(8,128)(2,1)} async-done(((bf16[32,8,1408]{2,1,0:T(8,128)(2,1)}), bf16[32,8,1408]{2,1,0:T(8,128)(2,1)}, u32[]{:S(2)}, u32[]{:S(2)}) %all-to-all-start.2) | async-done | bytes 720928 | tf_op jit(solution)/shard_map/all_to_all | solution.py:47
  129.4 2.2 shard_map.136
  131.7 5.1 %all-to-all-start.3 = ((bf16[32,8,1280]{2,1,0:T(8,128)(2,1)}), bf16[32,8,1280]{2,1,0:T(8,128)(2,1)}, u32[]{:S(2)}, u32[]{:S(2)}) async-start(bf16[32,8,1280]{2,1,0:T(8,128)(2,1)} %shard_map.136), calls=%async_computation.3 | async-start | bytes 1310720 | tf_op jit(solution)/shard_map/all_to_all | solution.py:434
  138.0 1.8 collective-permute-start.13
  139.8 1.5 collective-permute-start.15
  141.3 2.0 collective-permute-start.14
  143.3 5.3 %collective-permute-done.13 = bf16[128,1024]{1,0:T(8,128)(2,1)} collective-permute-done((bf16[128,1024]{1,0:T(8,128)(2,1)S(1)}, bf16[128,1024]{1,0:T(8,128)(2,1)}, u32[]{:S(2)}, u32[]{:S(2)}) %collective-permute-start.13) | collective-permute-done | bytes 262176 | tf_op jit(solution)/shard_map/ppermute | solution.py:52
  148.6 5.3 %collective-permute-done.14 = bf16[128,1024]{1,0:T(8,128)(2,1)} collective-permute-done((bf16[128,1024]{1,0:T(8,128)(2,1)S(1)}, bf16[128,1024]{1,0:T(8,128)(2,1)}, u32[]{:S(2)}, u32[]{:S(2)}) %collective-permute-start.14) | collective-permute-done | bytes 262176 | tf_op jit(solution)/shard_map/ppermute | solution.py:52
  153.9 2.1 add_add_fusion.1
  156.1 2.0 convolution_convert_fusion.refs_0_
  158.1 3.3 %collective-permute-start.18 = (bf16[256,384]{1,0:T(8,128)(2,1)S(1)}, bf16[256,384]{1,0:T(8,128)(2,1)S(1)}, u32[]{:S(2)}, u32[]{:S(2)}) collective-permute-start(bf16[256,384]{1,0:T(8,128)(2,1)S(1)} %convolution_convert_fusion.refs_0_), channel_id=1, source_target_pairs={{0,96},{32,0},{64,32},{96,64},{1,97},{33,1},{65,33},{97,65},{2,98}... | collective-permute-start | bytes 589832 | tf_op jit(solution)/shard_map/ppermute | solution.py:52
  161.4 2.3 collective-permute-start.16
  163.7 2.3 collective-permute-done.18.refs_3_
  166.0 2.6 collective-permute-done.17.refs_2_
  170.3 9.2 %all-to-all-start.4 = ((bf16[32,8,1408]{2,1,0:T(8,128)(2,1)}), bf16[32,8,1408]{2,1,0:T(8,128)(2,1)S(1)}, u32[]{:S(2)}, u32[]{:S(2)}) async-start(bf16[32,8,1408]{2,1,0:T(8,128)(2,1)} %bitcast.42), calls=%async_computation.4 | async-start | bytes 1441792 | tf_op jit(solution)/shard_map/all_to_all | solution.py:47
  181.1 16.5 %all-to-all-done.4.y_ref = bf16[32,8,1408]{2,1,0:T(8,128)(2,1)S(1)} async-done(((bf16[32,8,1408]{2,1,0:T(8,128)(2,1)}), bf16[32,8,1408]{2,1,0:T(8,128)(2,1)S(1)}, u32[]{:S(2)}, u32[]{:S(2)}) %all-to-all-start.4) | async-done | bytes 720928 | tf_op jit(solution)/shard_map/all_to_all | solution.py:47
  197.9 21.4 %all_to_all.35 = bf16[32,8,1280]{2,1,0:T(8,128)(2,1)S(1)} all-to-all(bf16[32,8,1280]{2,1,0:T(8,128)(2,1)S(1)} %shard_map.138), channel_id=1, replica_groups=mesh['section'=2,'dp'=4,'latent'=32] {'latent'}, dimensions={0} | all-to-all | bytes 1310720 | tf_op jit(solution)/shard_map/all_to_all | solution.py:434
  219.3 1.3 bitcast_select_fusion
  220.9 2.1 collective-permute-done.19.rest_ref
  223.0 3.8 %shard_map.139 = (bf16[128,1152]{1,0:T(8,128)(2,1)S(1)}, bf16[128,1152]{1,0:T(8,128)(2,1)S(1)}, bf16[128,1152]{1,0:T(8,128)(2,1)S(1)}, bf16[128,1152]{1,0:T(8,128)(2,1)S(1)}) custom-call(bf16[256,1280]{1,0:T(8,128)(2,1)S(1)} %get-tuple-element.49.own_ref, bf16[256,1280]{1,0:T(8,128)(2,1)S(1)} %collective-permute-done.19.rest_ref, ...), custom_call_target="tpu_custom_call" | custom-call | flops 1342177280 | bytes 4000000 | tf_op jit(solution)/shard_map/pallas_call | solution.py:158
  226.8 1.3 collective-permute-start.20
  230.3 6.4 %collective-permute-done.20 = bf16[128,1152]{1,0:T(8,128)(2,1)S(1)} collective-permute-done((bf16[128,1152]{1,0:T(8,128)(2,1)S(1)}, bf16[128,1152]{1,0:T(8,128)(2,1)S(1)}, u32[]{:S(2)}, u32[]{:S(2)}) %collective-permute-start.20) | collective-permute-done | bytes 294944 | tf_op jit(solution)/shard_map/ppermute | solution.py:52
  236.7 2.8 %collective-permute-done.21 = bf16[128,1152]{1,0:T(8,128)(2,1)S(1)} collective-permute-done((bf16[128,1152]{1,0:T(8,128)(2,1)S(1)}, bf16[128,1152]{1,0:T(8,128)(2,1)S(1)}, u32[]{:S(2)}, u32[]{:S(2)}) %collective-permute-start.21) | collective-permute-done | bytes 294944 | tf_op jit(solution)/shard_map/ppermute | solution.py:52
  239.5 4.4 %collective-permute-done.22 = bf16[128,1152]{1,0:T(8,128)(2,1)S(1)} collective-permute-done((bf16[128,1152]{1,0:T(8,128)(2,1)S(1)}, bf16[128,1152]{1,0:T(8,128)(2,1)S(1)}, u32[]{:S(2)}, u32[]{:S(2)}) %collective-permute-start.22) | collective-permute-done | bytes 294944 | tf_op jit(solution)/shard_map/ppermute | solution.py:52
  245.0 14.2 %all_to_all.36 = f32[32,1,128]{2,1,0:T(1,128)S(1)} all-to-all(f32[32,1,128]{2,1,0:T(1,128)S(1)} %broadcast_in_dim.13), channel_id=1, replica_groups=mesh['section'=2,'dp'=4,'latent'=32] {'latent'}, dimensions={0} | all-to-all | bytes 32768 | tf_op jit(solution)/shard_map/all_to_all | solution.py:41
  (93 shorter events, 25.5 us)
Async XLA Ops:
  0.6 109.9 %copy-start = (bf16[1,1280,1024]{2,1,0:T(8,128)(2,1)S(1)}, bf16[1,1280,1024]{2,1,0:T(8,128)(2,1)}, u32[]{:S(2)}) copy-start(bf16[1,1280,1024]{2,1,0:T(8,128)(2,1)} %param.14) | copy-start | bytes 7864324
  0.6 13.0 %collective-permute-start.4 = (bf16[384,1280]{1,0:T(8,128)(2,1)}, bf16[384,1280]{1,0:T(8,128)(2,1)}, u32[]{:S(2)}, u32[]{:S(2)}) collective-permute-start(bf16[384,1280]{1,0:T(8,128)(2,1)} %bitcast.46), channel_id=1, source_target_pairs={{0,128},{128,0},{1,129},{129,1},{2,130},{130,2},{3,131},{131,3},{4... | collective-permute-start | bytes 2949128 | tf_op jit(solution)/shard_map/ppermute | solution.py:356
  5.3 3.2 %copy-start.17 = (bf16[288,384]{1,0:T(8,128)(2,1)S(1)}, bf16[288,384]{1,0:T(8,128)(2,1)}, u32[]{:S(2)}) copy-start(bf16[288,384]{1,0:T(8,128)(2,1)} %get-tuple-element.24) | copy-start | bytes 663556
  5.3 3.2 %collective-permute-start = (bf16[288,384]{1,0:T(8,128)(2,1)}, bf16[288,384]{1,0:T(8,128)(2,1)S(1)}, u32[]{:S(2)}, u32[]{:S(2)}) collective-permute-start(bf16[288,384]{1,0:T(8,128)(2,1)} %get-tuple-element.25), channel_id=1, source_target_pairs={{0,128},{128,0},{1,129},{129,1},{2,130},{130,2},{3,131},{131,3},{4... | collective-permute-start | bytes 663560 | tf_op jit(solution)/shard_map/ppermute | solution.py:356
  8.6 14.1 %copy-start.9 = (bf16[288,384]{1,0:T(8,128)(2,1)}, bf16[288,384]{1,0:T(8,128)(2,1)S(1)}, u32[]{:S(2)}) copy-start(bf16[288,384]{1,0:T(8,128)(2,1)S(1)} %get-tuple-element.56.refs_0_) | copy-start | bytes 663556
  8.6 8.0 %collective-permute-start.3 = (bf16[288,384]{1,0:T(8,128)(2,1)S(1)}, bf16[288,384]{1,0:T(8,128)(2,1)S(1)}, u32[]{:S(2)}, u32[]{:S(2)}) collective-permute-start(bf16[288,384]{1,0:T(8,128)(2,1)S(1)} %get-tuple-element.56.refs_0_), channel_id=1, source_target_pairs={{0,96},{32,0},{64,32},{96,64},{1,97},{33,1},{65,33},{97,65},{2,98}... | collective-permute-start | bytes 663560 | tf_op jit(solution)/shard_map/ppermute | solution.py:52
  10.8 11.1 %collective-permute-start.2 = (bf16[288,384]{1,0:T(8,128)(2,1)S(1)}, bf16[288,384]{1,0:T(8,128)(2,1)S(1)}, u32[]{:S(2)}, u32[]{:S(2)}) collective-permute-start(bf16[288,384]{1,0:T(8,128)(2,1)S(1)} %get-tuple-element.56.refs_0_), channel_id=1, source_target_pairs={{0,64},{32,96},{64,0},{96,32},{1,65},{33,97},{65,1},{97,33},{2,66}... | collective-permute-start | bytes 663560 | tf_op jit(solution)/shard_map/ppermute | solution.py:52
  11.7 11.0 %collective-permute-start.1 = (bf16[288,384]{1,0:T(8,128)(2,1)S(1)}, bf16[288,384]{1,0:T(8,128)(2,1)S(1)}, u32[]{:S(2)}, u32[]{:S(2)}) collective-permute-start(bf16[288,384]{1,0:T(8,128)(2,1)S(1)} %get-tuple-element.56.refs_0_), channel_id=1, source_target_pairs={{0,32},{32,64},{64,96},{96,0},{1,33},{33,65},{65,97},{97,1},{2,34}... | collective-permute-start | bytes 663560 | tf_op jit(solution)/shard_map/ppermute | solution.py:52
  23.6 1.0 copy-start.1
  24.6 0.8 copy-start.10
  25.4 0.8 copy-start.13
  26.2 30.8 %all-to-all-start = ((bf16[32,8,1280]{2,1,0:T(8,128)(2,1)}), bf16[32,8,1280]{2,1,0:T(8,128)(2,1)S(1)}, u32[]{:S(2)}, u32[]{:S(2)}) async-start(bf16[32,8,1280]{2,1,0:T(8,128)(2,1)} %bitcast.45), calls=%async_computation | async-start | bytes 1310720 | tf_op jit(solution)/shard_map/all_to_all | solution.py:47
  38.4 8.7 %collective-permute-start.6 = (bf16[256,384]{1,0:T(8,128)(2,1)S(1)}, bf16[256,384]{1,0:T(8,128)(2,1)S(1)}, u32[]{:S(2)}, u32[]{:S(2)}) collective-permute-start(bf16[256,384]{1,0:T(8,128)(2,1)S(1)} %slice.56), channel_id=1, source_target_pairs={{0,64},{32,96},{64,0},{96,32},{1,65},{33,97},{65,1},{97,33},{2,66}... | collective-permute-start | bytes 589832 | tf_op jit(solution)/shard_map/ppermute | solution.py:52
  40.8 10.0 %collective-permute-start.5 = (bf16[256,384]{1,0:T(8,128)(2,1)S(1)}, bf16[256,384]{1,0:T(8,128)(2,1)S(1)}, u32[]{:S(2)}, u32[]{:S(2)}) collective-permute-start(bf16[256,384]{1,0:T(8,128)(2,1)S(1)} %slice.56), channel_id=1, source_target_pairs={{0,32},{32,64},{64,96},{96,0},{1,33},{33,65},{65,97},{97,1},{2,34}... | collective-permute-start | bytes 589832 | tf_op jit(solution)/shard_map/ppermute | solution.py:52
  42.8 7.9 %collective-permute-start.7 = (bf16[256,384]{1,0:T(8,128)(2,1)S(1)}, bf16[256,384]{1,0:T(8,128)(2,1)S(1)}, u32[]{:S(2)}, u32[]{:S(2)}) collective-permute-start(bf16[256,384]{1,0:T(8,128)(2,1)S(1)} %slice.56), channel_id=1, source_target_pairs={{0,96},{32,0},{64,32},{96,64},{1,97},{33,1},{65,33},{97,65},{2,98}... | collective-permute-start | bytes 589832 | tf_op jit(solution)/shard_map/ppermute | solution.py:52
  57.1 0.8 copy-start.6
  58.0 24.3 %all-to-all-start.1 = ((bf16[32,8,1280]{2,1,0:T(8,128)(2,1)}), bf16[32,8,1280]{2,1,0:T(8,128)(2,1)S(1)}, u32[]{:S(2)}, u32[]{:S(2)}) async-start(bf16[32,8,1280]{2,1,0:T(8,128)(2,1)} %copy-done.6), calls=%async_computation.1 | async-start | bytes 1310720 | tf_op jit(solution)/shard_map/all_to_all | solution.py:412
  62.9 19.4 %collective-permute-start.8 = (bf16[1280,384]{1,0:T(8,128)(2,1)}, bf16[1280,384]{1,0:T(8,128)(2,1)}, u32[]{:S(2)}, u32[]{:S(2)}) collective-permute-start(bf16[1280,384]{1,0:T(8,128)(2,1)} %get-tuple-element.28), channel_id=1, source_target_pairs={{0,128},{128,0},{1,129},{129,1},{2,130},{130,2},{3,131},{131,3},{4... | collective-permute-start | bytes 2949128 | tf_op jit(solution)/shard_map/ppermute | solution.py:356
  82.2 18.8 %collective-permute-start.12 = (bf16[256,1280]{1,0:T(8,128)(2,1)S(1)}, bf16[256,1280]{1,0:T(8,128)(2,1)S(1)}, u32[]{:S(2)}, u32[]{:S(2)}) collective-permute-start(bf16[256,1280]{1,0:T(8,128)(2,1)S(1)} %bitcast.39), channel_id=1, source_target_pairs={{0,128},{128,0},{1,129},{129,1},{2,130},{130,2},{3,131},{131,3},{4... | collective-permute-start | bytes 1966088 | tf_op jit(solution)/shard_map/ppermute | solution.py:356
  84.9 16.2 %copy-start.8 = (f32[256,384]{1,0:T(8,128)S(1)}, f32[256,384]{1,0:T(8,128)}, u32[]{:S(2)}) copy-start(f32[256,384]{1,0:T(8,128)} %convert_add_fusion.refs_4_) | copy-start | bytes 1179652
  85.6 9.9 %collective-permute-start.11 = (bf16[288,384]{1,0:T(8,128)(2,1)S(1)}, bf16[288,384]{1,0:T(8,128)(2,1)S(1)}, u32[]{:S(2)}, u32[]{:S(2)}) collective-permute-start(bf16[288,384]{1,0:T(8,128)(2,1)S(1)} %shard_map.134.refs_0_), channel_id=1, source_target_pairs={{0,96},{32,0},{64,32},{96,64},{1,97},{33,1},{65,33},{97,65},{2,98}... | collective-permute-start | bytes 663560 | tf_op jit(solution)/shard_map/ppermute | solution.py:52
  89.7 10.6 %collective-permute-start.10 = (bf16[288,384]{1,0:T(8,128)(2,1)S(1)}, bf16[288,384]{1,0:T(8,128)(2,1)S(1)}, u32[]{:S(2)}, u32[]{:S(2)}) collective-permute-start(bf16[288,384]{1,0:T(8,128)(2,1)S(1)} %shard_map.134.refs_0_), channel_id=1, source_target_pairs={{0,64},{32,96},{64,0},{96,32},{1,65},{33,97},{65,1},{97,33},{2,66}... | collective-permute-start | bytes 663560 | tf_op jit(solution)/shard_map/ppermute | solution.py:52
  89.7 11.3 %collective-permute-start.9 = (bf16[288,384]{1,0:T(8,128)(2,1)S(1)}, bf16[288,384]{1,0:T(8,128)(2,1)S(1)}, u32[]{:S(2)}, u32[]{:S(2)}) collective-permute-start(bf16[288,384]{1,0:T(8,128)(2,1)S(1)} %shard_map.134.refs_0_), channel_id=1, source_target_pairs={{0,32},{32,64},{64,96},{96,0},{1,33},{33,65},{65,97},{97,1},{2,34}... | collective-permute-start | bytes 663560 | tf_op jit(solution)/shard_map/ppermute | solution.py:52
  101.0 1.0 copy-start.16
  102.1 0.9 copy-start.12
  103.0 26.5 %all-to-all-start.2 = ((bf16[32,8,1408]{2,1,0:T(8,128)(2,1)}), bf16[32,8,1408]{2,1,0:T(8,128)(2,1)}, u32[]{:S(2)}, u32[]{:S(2)}) async-start(bf16[32,8,1408]{2,1,0:T(8,128)(2,1)} %bitcast.44), calls=%async_computation.2 | async-start | bytes 1441792 | tf_op jit(solution)/shard_map/all_to_all | solution.py:47
  113.1 1.1 copy-start.2
  131.7 24.5 %all-to-all-start.3 = ((bf16[32,8,1280]{2,1,0:T(8,128)(2,1)}), bf16[32,8,1280]{2,1,0:T(8,128)(2,1)}, u32[]{:S(2)}, u32[]{:S(2)}) async-start(bf16[32,8,1280]{2,1,0:T(8,128)(2,1)} %shard_map.136), calls=%async_computation.3 | async-start | bytes 1310720 | tf_op jit(solution)/shard_map/all_to_all | solution.py:434
  138.0 10.6 %collective-permute-start.13 = (bf16[128,1024]{1,0:T(8,128)(2,1)S(1)}, bf16[128,1024]{1,0:T(8,128)(2,1)}, u32[]{:S(2)}, u32[]{:S(2)}) collective-permute-start(bf16[128,1024]{1,0:T(8,128)(2,1)S(1)} %get-tuple-element.52), channel_id=1, source_target_pairs={{0,32},{32,64},{64,96},{96,0},{1,33},{33,65},{65,97},{97,1},{2,34}... | collective-permute-start | bytes 786440 | tf_op jit(solution)/shard_map/ppermute | solution.py:52
  139.8 8.8 %collective-permute-start.15 = (bf16[128,1024]{1,0:T(8,128)(2,1)S(1)}, bf16[128,1024]{1,0:T(8,128)(2,1)}, u32[]{:S(2)}, u32[]{:S(2)}) collective-permute-start(bf16[128,1024]{1,0:T(8,128)(2,1)S(1)} %get-tuple-element.53), channel_id=1, source_target_pairs={{0,96},{32,0},{64,32},{96,64},{1,97},{33,1},{65,33},{97,65},{2,98}... | collective-permute-start | bytes 786440 | tf_op jit(solution)/shard_map/ppermute | solution.py:52
  141.3 12.5 %collective-permute-start.14 = (bf16[128,1024]{1,0:T(8,128)(2,1)S(1)}, bf16[128,1024]{1,0:T(8,128)(2,1)}, u32[]{:S(2)}, u32[]{:S(2)}) collective-permute-start(bf16[128,1024]{1,0:T(8,128)(2,1)S(1)} %get-tuple-element.54), channel_id=1, source_target_pairs={{0,64},{32,96},{64,0},{96,32},{1,65},{33,97},{65,1},{97,33},{2,66}... | collective-permute-start | bytes 786440 | tf_op jit(solution)/shard_map/ppermute | solution.py:52
  156.0 12.7 %copy-start.11 = (f32[264,512]{1,0:T(8,128)S(1)}, f32[264,512]{1,0:T(8,128)}, u32[]{:S(2)}) copy-start(f32[264,512]{1,0:T(8,128)} %copy-done.10) | copy-start | bytes 1622020
  156.1 12.5 %copy-start.4 = (bf16[1280,384]{1,0:T(8,128)(2,1)S(1)}, bf16[1280,384]{1,0:T(8,128)(2,1)}, u32[]{:S(2)}) copy-start(bf16[1280,384]{1,0:T(8,128)(2,1)} %get-tuple-element.46.refs_5_) | copy-start | bytes 2949124
  158.1 7.9 %collective-permute-start.18 = (bf16[256,384]{1,0:T(8,128)(2,1)S(1)}, bf16[256,384]{1,0:T(8,128)(2,1)S(1)}, u32[]{:S(2)}, u32[]{:S(2)}) collective-permute-start(bf16[256,384]{1,0:T(8,128)(2,1)S(1)} %convolution_convert_fusion.refs_0_), channel_id=1, source_target_pairs={{0,96},{32,0},{64,32},{96,64},{1,97},{33,1},{65,33},{97,65},{2,98}... | collective-permute-start | bytes 589832 | tf_op jit(solution)/shard_map/ppermute | solution.py:52
  161.4 7.2 %collective-permute-start.17 = (bf16[256,384]{1,0:T(8,128)(2,1)S(1)}, bf16[256,384]{1,0:T(8,128)(2,1)S(1)}, u32[]{:S(2)}, u32[]{:S(2)}) collective-permute-start(bf16[256,384]{1,0:T(8,128)(2,1)S(1)} %convolution_convert_fusion.refs_0_), channel_id=1, source_target_pairs={{0,64},{32,96},{64,0},{96,32},{1,65},{33,97},{65,1},{97,33},{2,66}... | collective-permute-start | bytes 589832 | tf_op jit(solution)/shard_map/ppermute | solution.py:52
  161.4 7.2 %collective-permute-start.16 = (bf16[256,384]{1,0:T(8,128)(2,1)S(1)}, bf16[256,384]{1,0:T(8,128)(2,1)S(1)}, u32[]{:S(2)}, u32[]{:S(2)}) collective-permute-start(bf16[256,384]{1,0:T(8,128)(2,1)S(1)} %convolution_convert_fusion.refs_0_), channel_id=1, source_target_pairs={{0,32},{32,64},{64,96},{96,0},{1,33},{33,65},{65,97},{97,1},{2,34}... | collective-permute-start | bytes 589832 | tf_op jit(solution)/shard_map/ppermute | solution.py:52
  169.4 0.9 copy-start.5
  170.3 27.4 %all-to-all-start.4 = ((bf16[32,8,1408]{2,1,0:T(8,128)(2,1)}), bf16[32,8,1408]{2,1,0:T(8,128)(2,1)S(1)}, u32[]{:S(2)}, u32[]{:S(2)}) async-start(bf16[32,8,1408]{2,1,0:T(8,128)(2,1)} %bitcast.42), calls=%async_computation.4 | async-start | bytes 1441792 | tf_op jit(solution)/shard_map/all_to_all | solution.py:47
  197.9 25.1 %copy-start.7 = (bf16[1,1024,1280]{2,1,0:T(8,128)(2,1)S(1)}, bf16[1,1024,1280]{2,1,0:T(8,128)(2,1)}, u32[]{:S(2)}) copy-start(bf16[1,1024,1280]{2,1,0:T(8,128)(2,1)} %param.16) | copy-start | bytes 7864324
  219.3 3.7 %copy-start.3 = (bf16[512,1280]{1,0:T(8,128)(2,1)S(1)}, bf16[512,1280]{1,0:T(8,128)(2,1)}, u32[]{:S(2)}) copy-start(bf16[512,1280]{1,0:T(8,128)(2,1)} %copy-done.2) | copy-start | bytes 3932164
  219.3 3.7 %copy-start.14 = (f32[1,1280]{1,0:T(1,128)S(1)}, f32[1,1280]{1,0:T(1,128)}, u32[]{:S(2)}) copy-start(f32[1,1280]{1,0:T(1,128)} %bias_ref.1) | copy-start | bytes 15364
  220.6 2.4 collective-permute-start.19
  226.8 17.4 %copy-start.15 = (f32[128,1024]{1,0:T(8,128)S(1)}, f32[128,1024]{1,0:T(8,128)}, u32[]{:S(2)}) copy-start(f32[128,1024]{1,0:T(8,128)} %add_add_fusion.1) | copy-start | bytes 1572868
  226.8 17.4 %copy-start.18 = (f32[1,1024]{1,0:T(1,128)S(1)}, f32[1,1024]{1,0:T(1,128)}, u32[]{:S(2)}) copy-start(f32[1,1024]{1,0:T(1,128)} %param.15) | copy-start | bytes 12292
  226.8 9.9 %collective-permute-start.20 = (bf16[128,1152]{1,0:T(8,128)(2,1)S(1)}, bf16[128,1152]{1,0:T(8,128)(2,1)S(1)}, u32[]{:S(2)}, u32[]{:S(2)}) collective-permute-start(bf16[128,1152]{1,0:T(8,128)(2,1)S(1)} %get-tuple-element.43), channel_id=1, source_target_pairs={{0,32},{32,64},{64,96},{96,0},{1,33},{33,65},{65,97},{97,1},{2,34}... | collective-permute-start | bytes 884744 | tf_op jit(solution)/shard_map/ppermute | solution.py:52
  228.1 11.4 %collective-permute-start.21 = (bf16[128,1152]{1,0:T(8,128)(2,1)S(1)}, bf16[128,1152]{1,0:T(8,128)(2,1)S(1)}, u32[]{:S(2)}, u32[]{:S(2)}) collective-permute-start(bf16[128,1152]{1,0:T(8,128)(2,1)S(1)} %get-tuple-element.44), channel_id=1, source_target_pairs={{0,64},{32,96},{64,0},{96,32},{1,65},{33,97},{65,1},{97,33},{2,66}... | collective-permute-start | bytes 884744 | tf_op jit(solution)/shard_map/ppermute | solution.py:52
  229.1 14.8 %collective-permute-start.22 = (bf16[128,1152]{1,0:T(8,128)(2,1)S(1)}, bf16[128,1152]{1,0:T(8,128)(2,1)S(1)}, u32[]{:S(2)}, u32[]{:S(2)}) collective-permute-start(bf16[128,1152]{1,0:T(8,128)(2,1)S(1)} %get-tuple-element.45), channel_id=1, source_target_pairs={{0,96},{32,0},{64,32},{96,64},{1,97},{33,1},{65,33},{97,65},{2,98}... | collective-permute-start | bytes 884744 | tf_op jit(solution)/shard_map/ppermute | solution.py:52
